TPU v7x, 32 devices: a whole 2x2x4 slice. The times are simulated.
32 devices in a mesh: dp: 16 (over z, x, core), tp: 2 (over y).
Axes of the slice: x: 2, y: 2, z: 4, core: 2. Of those that a mesh axis runs over, the one named last changes fastest.
Arguments:
- tokens: bfloat16 [65536, 768], P('dp'), may hold values from -6 to 6
- long_lengths: int32 [32], P('dp'), may hold values from 256 to 1024, as said below
- short_lengths: int32 [128], P('dp'), may hold values from 64 to 256, as said below
- ln1_gain: bfloat16 [768], replicated, may hold values from 0.25 to 1.75
- ln1_bias: bfloat16 [768], replicated, may hold values from -2 to 2
- w_query: bfloat16 [768, 768], P(None, 'tp'), may hold values from -0.21875 to 0.21875
- b_query: bfloat16 [768], P('tp'), may hold values from -2 to 2
- w_key: bfloat16 [768, 768], P(None, 'tp'), may hold values from -0.21875 to 0.21875
- w_value: bfloat16 [768, 768], P(None, 'tp'), may hold values from -0.21875 to 0.21875
- b_value: bfloat16 [768], P('tp'), may hold values from -2 to 2
- w_out: bfloat16 [768, 768], P('tp'), may hold values from -3 to 3
- b_out: bfloat16 [768], replicated, may hold values from -2 to 2
- ln2_gain: bfloat16 [768], replicated, may hold values from 0.25 to 1.75
- ln2_bias: bfloat16 [768], replicated, may hold values from -2 to 2
- w_up: bfloat16 [768, 3072], P(None, 'tp'), may hold values from -0.21875 to 0.21875
- b_up: bfloat16 [3072], P('tp'), may hold values from -2 to 2
- w_down: bfloat16 [3072, 768], P('tp'), may hold values from -0.109375 to 0.109375
- b_down: bfloat16 [768], replicated, may hold values from -2 to 2
- cotangent: bfloat16 [65536, 768], P(('dp', 'tp')), may hold values from -6 to 6
Outputs:
- output: bfloat16 [65536, 768], P(('dp', 'tp'))
- grad_tokens: float32 [65536, 768], P(('dp', 'tp'))
- grad_ln1_gain: float32 [768], replicated
- grad_ln1_bias: float32 [768], replicated
- grad_w_query: float32 [768, 768], P(None, 'tp')
- grad_b_query: float32 [768], P('tp')
- grad_w_key: float32 [768, 768], P(None, 'tp')
- grad_w_value: float32 [768, 768], P(None, 'tp')
- grad_b_value: float32 [768], P('tp')
- grad_w_out: float32 [768, 768], P('tp')
- grad_b_out: float32 [768], replicated
- grad_ln2_gain: float32 [768], replicated
- grad_ln2_bias: float32 [768], replicated
- grad_w_up: float32 [768, 3072], P(None, 'tp')
- grad_b_up: float32 [3072], P('tp')
- grad_w_down: float32 [3072, 768], P('tp')
- grad_b_down: float32 [768], replicated
Inputs may be any that keep to these rules, and one draw needn't show every extreme that they name: `long_lengths`: valid tokens of each high-resolution image; keys at or after it are masked. `short_lengths`: valid tokens of each low-resolution image; keys at or after it are masked.
All inputs are finite; a program needn't handle non-finite values.
Results may differ from a plain program's by a relative error of at most 0.012.
The roundings to bfloat16 on the way count: a program that leaves them out, or rounds other values in their place, can miss the bound.
Values may be sent and summed in bfloat16 or wider, within the bound.
A program may use at most 320 MiB of HBM per device.

v0:
```python
import functools
import math

import jax
import jax.numpy as jnp
from jax import lax
from jax.experimental import pallas as pl
from jax.experimental.pallas import tpu as pltpu
from jax.sharding import PartitionSpec as P

HEAD_DIM = 48
LEN_L = 1024
LEN_S = 256
F32 = jnp.float32
BF16 = jnp.bfloat16
LOG2E = math.log2(math.e)
SCALE = HEAD_DIM ** (-0.5)
VMEM_LIMIT = 58 << 20
HEAD_GROUP = 2


def contract(left, right, left_dim, right_dim):
    return lax.dot_general(
        left, right, (((left_dim,), (right_dim,)), ((), ())), preferred_element_type=F32
    )


def params():
    return pltpu.CompilerParams(vmem_limit_bytes=VMEM_LIMIT)


def cost(flops, bytes_accessed, transcendentals=0):
    return pl.CostEstimate(
        flops=int(flops), bytes_accessed=int(bytes_accessed), transcendentals=int(transcendentals)
    )


def whole(shape):
    zeros = (0,) * len(shape)
    return pl.BlockSpec(shape, lambda *_: zeros)


def norm_parts(values):
    center = values - jnp.mean(values, axis=-1, keepdims=True)
    inv = lax.rsqrt(jnp.mean(center * center, axis=-1, keepdims=True) + 1e-06)
    return center * inv, inv


def norm_back(hat, inv, grad_hat):
    mean_grad = jnp.mean(grad_hat, axis=-1, keepdims=True)
    mean_both = jnp.mean(grad_hat * hat, axis=-1, keepdims=True)
    return inv * (grad_hat - mean_grad - hat * mean_both)


def project_norm_kernel(rank_ref, tok_ref, gain_ref, shift_ref, w_ref, b_ref, x_ref, own_ref, qkv_ref):
    hat, _ = norm_parts(tok_ref[...].astype(F32))
    normed = (hat * gain_ref[...] + shift_ref[...]).astype(BF16)
    x_ref[...] = normed
    own_ref[...] = tok_ref[...]
    qkv_ref[0] = (contract(w_ref[...], normed, 0, 1) + b_ref[...]).astype(BF16)


def project_kernel(_, x_ref, w_ref, b_ref, qkv_ref):
    qkv_ref[0] = (contract(w_ref[...], x_ref[...], 0, 1) + b_ref[...]).astype(BF16)


def own_row_block(per_part):
    def index(i, rank_ref):
        part = i // per_part
        return (part * 2 * per_part + rank_ref[0] * per_part + i % per_part, 0)

    return index


def project_norm(rank, tokens, gain, shift, w_cat, b_col, rows, block):
    width, out = w_cat.shape
    per_part = LEN_L // block
    by_row = pl.BlockSpec((block, width), lambda i, _: (i, 0))
    return pl.pallas_call(
        project_norm_kernel,
        grid_spec=pltpu.PrefetchScalarGridSpec(
            num_scalar_prefetch=1,
            grid=(rows // block,),
            in_specs=[
                pl.BlockSpec((block, width), own_row_block(per_part)),
                whole((1, width)),
                whole((1, width)),
                whole((width, out)),
                whole((out, 1)),
            ],
            out_specs=[by_row, by_row, pl.BlockSpec((1, out, block), lambda i, _: (0, 0, i))],
        ),
        out_shape=[
            jax.ShapeDtypeStruct((rows, width), BF16),
            jax.ShapeDtypeStruct((rows, width), BF16),
            jax.ShapeDtypeStruct((2, out, rows), BF16),
        ],
        compiler_params=params(),
        cost_estimate=cost(2 * rows * width * out, 4 * rows * width + 2 * out * rows),
        name="project_norm",
    )(rank, tokens, gain, shift, w_cat, b_col)


def project(both, normed, w_cat, b_col, block):
    rows, width = normed.shape
    out = w_cat.shape[1]
    return pl.pallas_call(
        project_kernel,
        grid=(rows // block,),
        in_specs=[
            pl.BlockSpec(memory_space=pl.ANY),
            pl.BlockSpec((block, width), lambda i: (i, 0)),
            whole((width, out)),
            whole((out, 1)),
        ],
        out_specs=pl.BlockSpec((1, out, block), lambda i: (1, 0, i)),
        out_shape=jax.ShapeDtypeStruct(both.shape, BF16),
        input_output_aliases={0: 0},
        compiler_params=params(),
        cost_estimate=cost(2 * rows * width * out, 2 * rows * width + 2 * out * rows),
        name="project",
    )(both, normed, w_cat, b_col)


def three_terms(value):
    high = value.astype(BF16).astype(F32)
    rest = value - high
    mid = rest.astype(BF16).astype(F32)
    return [high, mid, rest - mid]


def extra_rows(rows, count):
    at = lax.broadcasted_iota(jnp.int32, (16, count), 0)
    out = jnp.zeros((16, count), F32)
    for place, row in enumerate(rows):
        out = jnp.where(at == place, row, out)
    return out.astype(BF16)


def scaled_query(query):
    wide = query.astype(F32) * (SCALE * LOG2E)
    high = wide.astype(BF16)
    return [high, (wide - high.astype(F32)).astype(BF16)]


def attend_forward_kernel(mask_ref, qkv_ref, *refs, block):
    out_ref, log_ref = refs[-2:]
    heads, rows = qkv_ref.shape[2], qkv_ref.shape[4]
    work = []
    for head in range(heads):
        work += [(head, 0, LEN_L, at, block) for at in range(0, LEN_L, block)]
        work += [(head, start, LEN_S, 0, LEN_S) for start in range(LEN_L, rows, LEN_S)]

    def scores(item):
        head, start, count, at, size = item
        every = slice(start, start + count)
        keys = qkv_ref[0, 1, head, :, every]
        key_rows = jnp.concatenate([keys, keys, extra_rows([mask_ref[:, every]], count)], 0)
        query = scaled_query(qkv_ref[0, 0, head, :, start + at : start + at + size])
        query_rows = jnp.concatenate([*query, jnp.ones((16, size), BF16)], 0)
        return contract(key_rows, query_rows, 0, 0)

    def finish(item, score):
        head, start, count, at, size = item
        here = slice(start + at, start + at + size)
        values = qkv_ref[0, 2, head, :, start : start + count]
        value_rows = jnp.concatenate([values, jnp.ones((16, count), BF16)], 0)
        top = jnp.max(score, axis=0, keepdims=True)
        weights = jnp.exp2(score - top).astype(BF16)
        mixed = contract(value_rows, weights, 1, 0)
        total = mixed[HEAD_DIM : HEAD_DIM + 1]
        out_ref[0, head, :, here] = (mixed[:HEAD_DIM] * (1.0 / total)).astype(BF16)
        log_ref[0, head, :, here] = top + jnp.log2(total)

    score = scores(work[0])
    for place, item in enumerate(work):
        later = scores(work[place + 1]) if place + 1 < len(work) else None
        finish(item, score)
        score = later


def pair_count(heads, rows):
    return heads * (LEN_L**2 + (rows - LEN_L) * LEN_S)


def attend_forward(mask, qkv, part, earlier=(), block=1024):
    _, _, heads, _, rows = qkv.shape
    group = HEAD_GROUP
    pairs = pair_count(heads, rows)
    return pl.pallas_call(
        functools.partial(attend_forward_kernel, block=block),
        grid=(heads // group,),
        in_specs=[
            whole((1, rows)),
            pl.BlockSpec((1, 3, group, HEAD_DIM, rows), lambda h: (part, 0, h, 0, 0)),
            *(pl.BlockSpec(memory_space=pl.ANY) for _ in earlier),
        ],
        out_specs=[
            pl.BlockSpec((1, group, HEAD_DIM, rows), lambda h: (part, h, 0, 0)),
            pl.BlockSpec((1, group, 1, rows), lambda h: (part, h, 0, 0)),
        ],
        out_shape=[
            jax.ShapeDtypeStruct((2, heads, HEAD_DIM, rows), BF16),
            jax.ShapeDtypeStruct((2, heads, 1, rows), F32),
        ],
        input_output_aliases={2: 0, 3: 1} if earlier else {},
        compiler_params=params(),
        cost_estimate=cost(pairs * 2 * 512, 8 * heads * HEAD_DIM * rows, pairs),
        name="attend_forward",
    )(mask, qkv, *earlier)


class PlaneSum:
    COPIES = 10

    def __init__(self, refs):
        (self.own, self.seen, self.out, self.acc, self.from_core, self.seen_here, self.from_x,
         self.from_z, self.send, self.recv, self.local) = refs
        me = lax.axis_index("dp")
        self.core, self.x, self.z = me % 2, (me // 2) % 2, me // 4
        self.rows = self.own.shape[0]

    @staticmethod
    def buffers(shape):
        rows, width = shape
        return [
            pltpu.VMEM((rows // 2, width), BF16),
            pltpu.VMEM((rows // 2, width), BF16),
            pltpu.VMEM((rows // 2, width), BF16),
            pltpu.VMEM((rows // 4, width), BF16),
            pltpu.VMEM((3, rows // 16, width), BF16),
            pltpu.SemaphoreType.DMA((PlaneSum.COPIES,)),
            pltpu.SemaphoreType.DMA((PlaneSum.COPIES,)),
            pltpu.SemaphoreType.DMA((3,)),
        ]

    def device(self, z, x, core):
        return {"dp": (z * 2 + x) * 2 + core}

    def copy(self, source, target, place, device):
        return pltpu.make_async_remote_copy(
            src_ref=source,
            dst_ref=target,
            send_sem=self.send.at[place],
            recv_sem=self.recv.at[place],
            device_id=device,
            device_id_type=pl.DeviceIdType.MESH,
        )

    def part(self, ref, start, count):
        return ref.at[pl.ds(pl.multiple_of(start, 16), count)]

    def core_copy(self):
        half = self.rows // 2
        return self.copy(
            self.part(self.own, (1 - self.core) * half, half),
            self.from_core,
            0,
            self.device(self.z, self.x, 1 - self.core),
        )

    def local_copies(self):
        half = self.rows // 2
        return [
            pltpu.make_async_copy(
                self.part(self.own, self.core * half, half), self.acc, self.local.at[0]
            ),
            pltpu.make_async_copy(self.seen, self.seen_here, self.local.at[1]),
        ]

    def x_copy(self):
        count = self.rows // 4
        return self.copy(
            self.part(self.acc, (1 - self.x) * count, count),
            self.from_x,
            1,
            self.device(self.z, 1 - self.x, self.core),
        )

    def z_copies(self):
        count = self.rows // 16
        copies = []
        for step in (1, 2, 3):
            there = (self.z + step) % 4
            copies.append(
                self.copy(
                    self.part(self.acc, self.x * 4 * count + there * count, count),
                    self.from_z.at[step - 1],
                    1 + step,
                    self.device(there, self.x, self.core),
                )
            )
        return copies

    def piece(self):
        count = self.rows // 16
        inside = self.x * 4 * count + self.z * count
        place = self.core * 8 * count + inside
        return self.part(self.acc, inside, count), self.part(self.out, place, count)

    def keep_copy(self):
        mine, place = self.piece()
        return pltpu.make_async_copy(mine, place, self.local.at[2])

    def back_z_copies(self):
        mine, place = self.piece()
        return [
            self.copy(mine, place, 4 + step, self.device((self.z + step) % 4, self.x, self.core))
            for step in (1, 2, 3)
        ]

    def back_x_copy(self):
        count = self.rows // 4
        place = self.part(self.out, self.core * 2 * count + self.x * count, count)
        return self.copy(place, place, 8, self.device(self.z, 1 - self.x, self.core))

    def back_core_copy(self):
        count = self.rows // 2
        place = self.part(self.out, self.core * count, count)
        return self.copy(place, place, 9, self.device(self.z, self.x, 1 - self.core))

    def add(self, start, count, terms):
        tile = 48
        width = self.acc.shape[1]

        def body(i, _):
            at = pl.multiple_of(i * tile, 16)
            here = pl.ds(pl.multiple_of(start + at, 16), tile)
            total = self.acc[here, :].astype(F32)
            for term in terms:
                total = total + term[pl.ds(at, tile), :].astype(F32)
            self.acc[here, :] = total.astype(BF16)
            return 0

        lax.fori_loop(0, count // tile, body, 0)

    def begin(self):
        self.core_copy().start()
        for copy in self.local_copies():
            copy.start()

    def along_x(self):
        self.core_copy().wait()
        for copy in self.local_copies():
            copy.wait()
        self.add(0, self.rows // 2, [self.from_core, self.seen_here])
        self.x_copy().start()

    def along_z(self):
        self.x_copy().wait()
        count = self.rows // 4
        self.add(self.x * count, count, [self.from_x])
        for copy in self.z_copies():
            copy.start()

    def back_along_z(self):
        for copy in self.z_copies():
            copy.wait()
        count = self.rows // 16
        inside = self.x * 4 * count + self.z * count
        self.add(inside, count, [self.from_z.at[i] for i in range(3)])
        self.keep_copy().start()
        for copy in self.back_z_copies():
            copy.start()

    def back_along_x(self):
        self.keep_copy().wait()
        for copy in self.back_z_copies():
            copy.wait()
        self.back_x_copy().start()

    def back_to_core(self):
        self.back_x_copy().wait()
        self.back_core_copy().start()

    def end(self):
        self.back_core_copy().wait()


def greet_plane():
    me = lax.axis_index("dp")
    core, x, z = me % 2, (me // 2) % 2, me // 4
    barrier = pltpu.get_barrier_semaphore()
    others = [(z, x, 1 - core), (z, 1 - x, core)] + [((z + i) % 4, x, core) for i in (1, 2, 3)]
    for other_z, other_x, other_core in others:
        pl.semaphore_signal(
            barrier,
            inc=1,
            device_id={"dp": (other_z * 2 + other_x) * 2 + other_core},
            device_id_type=pl.DeviceIdType.MESH,
        )
    pl.semaphore_wait(barrier, len(others))


SUM_STEPS = (
    (0, 1, 5, 8, 12, 15, 15),
    (0, 4, 8, 12, 15, 15, 15),
    (0, 2, 5, 9, 12, 15, 15),
)


def attend_backward_kernel(*refs, block, sums):
    mask_ref, qkv_ref, out_ref, log_ref, grad_ref = refs[:5]
    sum_in = refs[5 : 5 + 2 * sums]
    dqkv_ref = refs[5 + 2 * sums]
    sum_out = refs[6 + 2 * sums : 6 + 3 * sums]
    scratch = refs[6 + 3 * sums :]
    each = len(scratch) // sums
    plane = [
        PlaneSum((*sum_in[2 * i : 2 * i + 2], sum_out[i], *scratch[each * i : each * (i + 1)]))
        for i in range(sums)
    ]
    step = pl.program_id(0)

    for at in sorted({at for times in SUM_STEPS for at in times[:-2]}):

        @pl.when(step == at)
        def _(at=at):
            if at == 0:
                greet_plane()
            for one, times in zip(plane, SUM_STEPS):
                for when, action in zip(
                    times[:-2],
                    (one.begin, one.along_x, one.along_z, one.back_along_z, one.back_along_x),
                ):
                    if when == at:
                        action()

    rows = qkv_ref.shape[4]
    images = [(0, LEN_L, block)] + [(at, LEN_S, LEN_S) for at in range(LEN_L, rows, LEN_S)]
    for start, count, size in images:
        every = slice(start, start + count)
        keys = qkv_ref[0, 1, 0, :, every]
        values = qkv_ref[0, 2, 0, :, every]
        ones = jnp.ones((1, count), F32)
        key_rows = jnp.concatenate(
            [keys, keys, extra_rows([ones, ones, ones, mask_ref[:, every]], count)], 0
        )
        value_rows = jnp.concatenate([values, extra_rows([ones, ones, ones], count)], 0)
        grad_values = grad_keys = None
        for at in range(start, start + count, size):
            here = slice(at, at + size)
            query = qkv_ref[0, 0, 0, :, here]
            grads = grad_ref[0, 0, :, here]
            inner = jnp.sum(
                grads.astype(F32) * out_ref[0, 0, :, here].astype(F32), axis=0, keepdims=True
            )
            terms = three_terms(-log_ref[0, 0, :, here]) + [jnp.ones((1, size), F32)]
            query_rows = jnp.concatenate([*scaled_query(query), extra_rows(terms, size)], 0)
            grad_rows = jnp.concatenate([grads, extra_rows(three_terms(-inner), size)], 0)
            score = contract(query_rows, key_rows, 0, 0)
            grad_probs = contract(grad_rows, value_rows, 0, 0)
            probs = jnp.exp2(score)
            grad_score = (probs * grad_probs).astype(BF16)
            part_values = contract(grads, probs.astype(BF16), 1, 0)
            part_keys = contract(query, grad_score, 1, 0)
            grad_values = part_values if grad_values is None else grad_values + part_values
            grad_keys = part_keys if grad_keys is None else grad_keys + part_keys
            dqkv_ref[0, 0, 0, :, here] = (contract(keys, grad_score, 1, 1) * SCALE).astype(BF16)
        dqkv_ref[0, 1, 0, :, every] = (grad_keys * SCALE).astype(BF16)
        dqkv_ref[0, 2, 0, :, every] = grad_values.astype(BF16)

    @pl.when(step == pl.num_programs(0) - 1)
    def _():
        for one in plane:
            one.back_to_core()
        for one in plane:
            one.end()


def attend_backward(mask, qkv, out, log_total, grads, terms, block=256):
    _, _, heads, _, rows = qkv.shape
    pairs = pair_count(2 * heads, rows)
    anywhere = pl.BlockSpec(memory_space=pl.ANY)
    all_three = pl.BlockSpec((1, 3, 1, HEAD_DIM, rows), lambda h: (h // heads, 0, h % heads, 0, 0))
    one = pl.BlockSpec((1, 1, HEAD_DIM, rows), lambda h: (h // heads, h % heads, 0, 0))
    row = pl.BlockSpec((1, 1, 1, rows), lambda h: (h // heads, h % heads, 0, 0))
    shapes = [own.shape for own, _ in terms]
    return pl.pallas_call(
        functools.partial(attend_backward_kernel, block=block, sums=len(terms)),
        grid=(2 * heads,),
        in_specs=[whole((1, rows)), all_three, one, row, one] + [anywhere] * (2 * len(terms)),
        out_specs=[all_three] + [anywhere] * len(terms),
        out_shape=[jax.ShapeDtypeStruct(qkv.shape, BF16)]
        + [jax.ShapeDtypeStruct(shape, BF16) for shape in shapes],
        scratch_shapes=[ref for shape in shapes for ref in PlaneSum.buffers(shape)],
        compiler_params=pltpu.CompilerParams(
            vmem_limit_bytes=VMEM_LIMIT, collective_id=0, has_side_effects=True
        ),
        cost_estimate=cost(pairs * 5 * 512, 32 * heads * HEAD_DIM * rows, pairs),
        name="attend_backward",
    )(mask, qkv, out, log_total, grads, *(array for pair in terms for array in pair))


def middle_kernel(
    tok_ref, att_ref, w_ref, b_ref, gain_ref, shift_ref, resid_ref, mid_ref
):
    resid = tok_ref[...].astype(F32) + contract(att_ref[...], w_ref[...], 0, 0) + b_ref[...]
    resid_ref[...] = resid
    hat, _ = norm_parts(resid)
    mid_ref[...] = (hat * gain_ref[...] + shift_ref[...]).astype(BF16)


def middle(tokens, attended, w_out, b_out, gain, shift, block):
    heads_width, rows = attended.shape
    width = w_out.shape[1]
    by_row = pl.BlockSpec((block, width), lambda i: (i, 0))
    return pl.pallas_call(
        middle_kernel,
        grid=(rows // block,),
        in_specs=[
            by_row,
            pl.BlockSpec((heads_width, block), lambda i: (0, i)),
            whole((heads_width, width)),
            whole((1, width)),
            whole((1, width)),
            whole((1, width)),
        ],
        out_specs=[by_row, by_row],
        out_shape=[
            jax.ShapeDtypeStruct((rows, width), F32),
            jax.ShapeDtypeStruct((rows, width), BF16),
        ],
        compiler_params=params(),
        cost_estimate=cost(2 * rows * width * heads_width, 12 * rows * width),
        name="middle",
    )(tokens, attended, w_out, b_out, gain, shift)


ERFC_TERMS = (0.254829592, -0.284496736, 1.421413741, -1.453152027, 1.061405429)
ERFC_SLOPE = 0.3275911


def gelu_and_slope(value):
    bell = jnp.exp2(value * value * (-0.5 * LOG2E))
    base = 1.0 + jnp.abs(value) * (ERFC_SLOPE * math.sqrt(0.5))
    ratio = 1.0 / base
    poly = ERFC_TERMS[4] * 0.5
    for term in ERFC_TERMS[3::-1]:
        poly = poly * ratio + term * 0.5
    tail = poly * ratio * bell
    below = jnp.where(value < 0.0, tail, 1.0 - tail)
    return value * below, below + value * bell * (1.0 / math.sqrt(2.0 * math.pi))


def feed_kernel(
    mid_ref, grad_ref, up_ref, b_ref, down_ref, sum_ref, gmid_ref, dup_ref, ddown_ref, db_ref,
    act_ref, gpre_ref, *, chunk,
):
    @pl.when(pl.program_id(0) == 0)
    def _():
        sum_ref[...] = jnp.zeros_like(sum_ref)
        gmid_ref[...] = jnp.zeros_like(gmid_ref)

    rows = mid_ref.shape[0]
    up, down, bias = up_ref[...], down_ref[...], b_ref[...]

    def products(at):
        here = slice(at, at + chunk)
        return (
            contract(mid_ref[here], up, 1, 0) + bias,
            contract(grad_ref[here], down, 1, 1),
        )

    now = products(0)
    db = None
    for at in range(0, rows, chunk):
        here = slice(at, at + chunk)
        later = products(at + chunk) if at + chunk < rows else None
        value, slope = gelu_and_slope(now[0])
        act = value.astype(BF16)
        gpre = (slope * now[1]).astype(BF16)
        act_ref[here] = act
        gpre_ref[here] = gpre
        part = jnp.sum(gpre.astype(F32), axis=0, keepdims=True)
        db = part if db is None else db + part
        sum_ref[here] += contract(act, down, 1, 0)
        gmid_ref[here] += contract(gpre, up, 1, 1)
        now = later
    db_ref[...] = db
    ddown_ref[...] = contract(act_ref[...], grad_ref[...], 0, 0).astype(BF16)
    dup_ref[...] = contract(mid_ref[...], gpre_ref[...], 0, 0).astype(BF16)


def feed(mid, grads, w_up, b_up, w_down, block=512, chunk=512):
    rows, width = mid.shape
    hidden = w_up.shape[1]
    return pl.pallas_call(
        functools.partial(feed_kernel, chunk=chunk),
        grid=(hidden // block,),
        in_specs=[
            whole((rows, width)),
            whole((rows, width)),
            pl.BlockSpec((width, block), lambda j: (0, j)),
            pl.BlockSpec((1, block), lambda j: (0, j)),
            pl.BlockSpec((block, width), lambda j: (j, 0)),
        ],
        out_specs=[
            whole((rows, width)),
            whole((rows, width)),
            pl.BlockSpec((width, block), lambda j: (0, j)),
            pl.BlockSpec((block, width), lambda j: (j, 0)),
            pl.BlockSpec((1, block), lambda j: (0, j)),
        ],
        out_shape=[
            jax.ShapeDtypeStruct((rows, width), F32),
            jax.ShapeDtypeStruct((rows, width), F32),
            jax.ShapeDtypeStruct((width, hidden), BF16),
            jax.ShapeDtypeStruct((hidden, width), BF16),
            jax.ShapeDtypeStruct((1, hidden), F32),
        ],
        scratch_shapes=[pltpu.VMEM((rows, block), BF16), pltpu.VMEM((rows, block), BF16)],
        compiler_params=params(),
        cost_estimate=cost(12 * rows * width * hidden, 20 * rows * width, 2 * rows * hidden),
        name="feed",
    )(mid, grads, w_up, b_up, w_down)


def branch_kernel(
    resid_ref, sum1_ref, sum2_ref, gmid1_ref, gmid2_ref, grad_ref, gain_ref, bdown_ref, w_ref,
    att_ref, out_ref, gresid_ref, gatt_ref, dw_own_ref, dw_other_ref, small_ref, acc_ref,
):
    @pl.when(pl.program_id(0) == 0)
    def _():
        acc_ref[...] = jnp.zeros_like(acc_ref)
        small_ref[...] = jnp.zeros_like(small_ref)

    resid = resid_ref[...]
    grads = grad_ref[...].astype(F32)
    out_ref[...] = (resid + sum1_ref[...] + sum2_ref[...] + bdown_ref[...]).astype(BF16)
    gmid = gmid1_ref[...] + gmid2_ref[...]
    hat, inv = norm_parts(resid)
    gresid = grads + norm_back(hat, inv, gmid * gain_ref[...])
    gresid_ref[...] = gresid
    branch = gresid.astype(BF16)
    gatt_ref[...] = contract(w_ref[...], branch, 1, 1).astype(BF16)
    acc_ref[...] += contract(branch, att_ref[...], 0, 1)
    small_ref[0:1] += jnp.sum(gmid * hat, axis=0, keepdims=True)
    small_ref[1:2] += jnp.sum(gmid, axis=0, keepdims=True)
    small_ref[2:3] += jnp.sum(gresid, axis=0, keepdims=True)
    small_ref[3:4] += jnp.sum(grads, axis=0, keepdims=True)

    @pl.when(pl.program_id(0) == pl.num_programs(0) - 1)
    def _():
        half = dw_own_ref.shape[1]
        dw_own_ref[...] = acc_ref[:, :half].astype(BF16)
        dw_other_ref[...] = acc_ref[:, half:].astype(BF16)


def branch(resid, sums, gmids, grads, gain, b_down, w_out, attended, block):
    rows, width = resid.shape
    heads_width = attended.shape[0]
    by_row = pl.BlockSpec((block, width), lambda i: (i, 0))
    columns = pl.BlockSpec((heads_width, block), lambda i: (0, i))
    half = (width, heads_width // 2)
    return pl.pallas_call(
        branch_kernel,
        grid=(rows // block,),
        in_specs=[by_row] * 6
        + [whole((1, width)), whole((1, width)), whole((heads_width, width)), columns],
        out_specs=[by_row, by_row, columns, whole(half), whole(half), whole((8, width))],
        out_shape=[
            jax.ShapeDtypeStruct((rows, width), BF16),
            jax.ShapeDtypeStruct((rows, width), F32),
            jax.ShapeDtypeStruct((heads_width, rows), BF16),
            jax.ShapeDtypeStruct(half, BF16),
            jax.ShapeDtypeStruct(half, BF16),
            jax.ShapeDtypeStruct((8, width), F32),
        ],
        scratch_shapes=[pltpu.VMEM((width, heads_width), F32)],
        compiler_params=params(),
        cost_estimate=cost(4 * rows * width * heads_width, 32 * rows * width),
        name="branch",
    )(resid, *sums, *gmids, grads, gain, b_down, w_out, attended)


def back_kernel(
    tok_ref, x_ref, d_ref, w_ref, w2_ref, gresid_ref, gain_ref,
    gtok_ref, dw_ref, dw2_ref, db_ref, small_ref, acc_ref,
):
    @pl.when(pl.program_id(0) == 0)
    def _():
        acc_ref[...] = jnp.zeros_like(acc_ref)
        db_ref[...] = jnp.zeros_like(db_ref)
        small_ref[...] = jnp.zeros_like(small_ref)

    gin = contract(d_ref[0], w_ref[...], 0, 1) + contract(d_ref[1], w2_ref[...], 0, 1)
    for half in (0, 1):
        acc_ref[half] += contract(x_ref[...], d_ref[half], 0, 1)
        db_ref[half] += jnp.sum(d_ref[half].astype(F32), axis=1, keepdims=True)
    hat, inv = norm_parts(tok_ref[...].astype(F32))
    gtok_ref[...] = gresid_ref[...] + norm_back(hat, inv, gin * gain_ref[...])
    small_ref[0:1] += jnp.sum(gin * hat, axis=0, keepdims=True)
    small_ref[1:2] += jnp.sum(gin, axis=0, keepdims=True)

    @pl.when(pl.program_id(0) == pl.num_programs(0) - 1)
    def _():
        dw_ref[...] = acc_ref[0].astype(BF16)
        dw2_ref[...] = acc_ref[1].astype(BF16)


def back(tokens, normed, dqkv, w_cat, w_cat2, gresid, gain, block):
    rows, width = normed.shape
    out = w_cat.shape[1]
    by_row = pl.BlockSpec((block, width), lambda i: (i, 0))
    return pl.pallas_call(
        back_kernel,
        grid=(rows // block,),
        in_specs=[
            by_row,
            by_row,
            pl.BlockSpec((2, out, block), lambda i: (0, 0, i)),
            whole((width, out)),
            whole((width, out)),
            by_row,
            whole((1, width)),
        ],
        out_specs=[
            by_row,
            whole((width, out)),
            whole((width, out)),
            whole((2, out, 1)),
            whole((8, width)),
        ],
        out_shape=[
            jax.ShapeDtypeStruct((rows, width), F32),
            jax.ShapeDtypeStruct((width, out), BF16),
            jax.ShapeDtypeStruct((width, out), BF16),
            jax.ShapeDtypeStruct((2, out, 1), F32),
            jax.ShapeDtypeStruct((8, width), F32),
        ],
        scratch_shapes=[pltpu.VMEM((2, width, out), F32)],
        compiler_params=params(),
        cost_estimate=cost(8 * rows * width * out, 16 * rows * width),
        name="back",
    )(tokens, normed, dqkv, w_cat, w_cat2, gresid, gain)


def sum_kernel(*refs):
    greet_plane()
    one = PlaneSum(refs)
    for action in (one.begin, one.along_x, one.along_z, one.back_along_z, one.back_along_x):
        action()
    one.back_to_core()
    one.end()


def plane_sum(own, seen):
    anywhere = pl.BlockSpec(memory_space=pl.ANY)
    return pl.pallas_call(
        sum_kernel,
        in_specs=[anywhere, anywhere],
        out_specs=anywhere,
        out_shape=jax.ShapeDtypeStruct(own.shape, BF16),
        scratch_shapes=PlaneSum.buffers(own.shape),
        compiler_params=pltpu.CompilerParams(
            vmem_limit_bytes=VMEM_LIMIT, collective_id=1, has_side_effects=True
        ),
        name="plane_sum",
    )(own, seen)


def swap_tp(array):
    return lax.ppermute(array, "tp", [(0, 1), (1, 0)])


def swap_dp(array, bit):
    count = lax.axis_size("dp")
    return lax.ppermute(array, "dp", [(i, i ^ bit) for i in range(count)])


def dp_bit(bit):
    return (lax.axis_index("dp") & bit) != 0


def joined(mine, theirs, second):
    return jnp.where(second, jnp.concatenate([theirs, mine], 0), jnp.concatenate([mine, theirs], 0))


def half_of(array, second):
    size = array.shape[0] // 2
    return lax.dynamic_slice_in_dim(array, jnp.where(second, size, 0), size, 0)


def fetch_other(array, bits):
    piece = array
    for bit in reversed(bits):
        piece = half_of(piece, dp_bit(bit))
    piece = swap_tp(piece)
    for bit in bits:
        piece = joined(piece, swap_dp(piece, bit), dp_bit(bit))
    return piece


def add_low(left, right):
    return (left.astype(F32) + right.astype(F32)).astype(BF16)


def partner_term(other):
    second = dp_bit(1)
    both = add_low(half_of(other, second), swap_dp(half_of(other, ~second), 1))
    return swap_tp(both)


def by_images(
    tokens, long_lengths, short_lengths, ln1_gain, ln1_bias, w_query, b_query, w_key, w_value,
    b_value, w_out, b_out, ln2_gain, ln2_bias, w_up, b_up, w_down, b_down, cotangent,
):
    rank = lax.axis_index("tp")
    rank_arr = jnp.reshape(rank, (1,)).astype(jnp.int32)
    second = rank == 1
    rows = tokens.shape[0] // 2
    width = tokens.shape[1]
    half = w_query.shape[1]
    heads = half // HEAD_DIM
    long_len = lax.dynamic_slice_in_dim(long_lengths, rank, 1, 0)
    shorts = short_lengths.shape[0] // 2
    short_len = lax.dynamic_slice_in_dim(short_lengths, rank * shorts, shorts, 0)
    valid = jnp.concatenate(
        [
            jnp.arange(LEN_L) < long_len[0],
            (jnp.arange(LEN_S)[None, :] < short_len[:, None]).reshape(-1),
        ]
    )
    mask = jnp.where(valid, 0.0, -1e30).astype(F32).reshape(1, -1)
    row = lambda vector: vector.astype(F32).reshape(1, -1)
    core, xbit = 1, 2

    w_cat = jnp.concatenate([w_query, w_key, w_value], axis=1)
    w_cat2 = fetch_other(w_cat, [core, xbit])
    bias = jnp.concatenate([b_query, b_value, b_up]).astype(F32)
    bias2 = swap_tp(bias)

    def column(packed):
        return jnp.concatenate(
            [packed[:half], jnp.zeros((half,), F32), packed[half : 2 * half]]
        ).reshape(-1, 1)

    w_out2 = fetch_other(w_out, [core, xbit])
    w_up2 = fetch_other(w_up, [core, xbit])
    w_down2 = fetch_other(w_down, [core, xbit])
    kept = half_of(cotangent, second)
    got = swap_tp(half_of(cotangent, ~second))
    grads = joined(kept, got, second)

    normed, own_tokens, qkv = project_norm(
        rank_arr, tokens, row(ln1_gain), row(ln1_bias), w_cat, column(bias), rows, 512
    )
    parts = (2, 3, heads, HEAD_DIM, rows)
    att = attend_forward(mask, qkv.reshape(parts), 0)
    qkv = project(qkv, normed, w_cat2, column(bias2), 512).reshape(parts)
    att, log_total = attend_forward(mask, qkv, 1, att)
    attended = att.reshape(2 * half, rows)
    w_out_all = jnp.concatenate([w_out, w_out2], axis=0)
    resid, mid = middle(
        own_tokens, attended, w_out_all, row(b_out), row(ln2_gain), row(ln2_bias), 512
    )
    sum2, gmid2, dup2, ddown2, dbup2 = feed(mid, grads, w_up2, row(bias2[2 * half :]), w_down2)
    seen_up, seen_down = partner_term(dup2), partner_term(ddown2)
    sum1, gmid1, dup1, ddown1, dbup1 = feed(mid, grads, w_up, row(bias[2 * half :]), w_down)
    out, gresid, gatt, dwout1, dwout2, small2 = branch(
        resid, (sum1, sum2), (gmid1, gmid2), grads, row(ln2_gain), row(b_down), w_out_all,
        attended, 512,
    )
    dqkv, grad_up, grad_down, grad_out_t = attend_backward(
        mask, qkv, att, log_total, gatt.reshape(2, heads, HEAD_DIM, rows),
        ((dup1, seen_up), (ddown1, seen_down), (dwout1, partner_term(dwout2))),
    )
    result = joined(half_of(out, second), swap_tp(half_of(out, ~second)), second)
    gtok, dw_cat, dw_cat2, db, small1 = back(
        own_tokens, normed, dqkv.reshape(2, 3 * half, rows), w_cat, w_cat2, gresid,
        row(ln1_gain), 512,
    )
    grad_cat = plane_sum(dw_cat, partner_term(dw_cat2)).astype(F32)
    sent = swap_tp(half_of(gtok, ~second).astype(BF16)).astype(F32)
    grad_tokens = joined(half_of(gtok, second), sent, second)

    one = jnp.concatenate([db[0, :half, 0], db[0, 2 * half :, 0], dbup1[0]])
    two = jnp.concatenate([db[1, :half, 0], db[1, 2 * half :, 0], dbup2[0]])
    ordered = joined(one, two, second)
    packed = jnp.concatenate([small1[0], small1[1], *(small2[i] for i in range(4)), ordered])
    packed = lax.psum(packed, ("dp", "tp"))
    small = packed[: 6 * width].reshape(6, width)
    mine = half_of(packed[6 * width :], second)
    return (
        result,
        grad_tokens,
        small[0],
        small[1],
        grad_cat[:, :half],
        mine[:half],
        grad_cat[:, half : 2 * half],
        grad_cat[:, 2 * half :],
        mine[half : 2 * half],
        grad_out_t.T.astype(F32),
        small[4],
        small[2],
        small[3],
        grad_up.astype(F32),
        mine[2 * half :],
        grad_down.astype(F32),
        small[5],
    )


def layer_norm(values, gain, shift):
    center = values - jnp.mean(values, axis=-1, keepdims=True)
    spread = jnp.mean(center * center, axis=-1, keepdims=True)
    return center * lax.rsqrt(spread + 1e-06) * gain + shift


def dot_plain(left, right):
    return jnp.dot(left, right, preferred_element_type=jnp.float32)


def dot_rows(left, right):
    return lax.dot_general(
        left, right, (((0,), (0,)), ((), ())), preferred_element_type=jnp.float32
    )


def dot_back(left, right):
    return lax.dot_general(
        left, right, (((1,), (1,)), ((), ())), preferred_element_type=jnp.float32
    )


def group_shape(image_count, seq_len, head_count):
    per_step = math.gcd(image_count, max(1, 512 // seq_len))
    return (image_count // per_step, per_step, seq_len, head_count, HEAD_DIM)


def masked_scores(query_blk, key_blk, length_blk):
    seq_len = query_blk.shape[1]
    raw = jnp.einsum(
        "bqhd,bkhd->bhqk", query_blk, key_blk, preferred_element_type=jnp.float32
    ) * HEAD_DIM ** (-0.5)
    keep = jnp.arange(seq_len, dtype=jnp.int32)[None, :] < length_blk[:, None]
    return jnp.where(keep[:, None, None, :], raw, -1e30)


def attention_forward(queries, key_rows, value_rows, lengths, seq_len):
    image_count = lengths.shape[0]
    head_count = queries.shape[1] // HEAD_DIM
    block_shape = group_shape(image_count, seq_len, head_count)

    def one_step(block):
        query_blk, key_blk, value_blk, length_blk = block
        scores = masked_scores(query_blk, key_blk, length_blk)
        row_top = jnp.max(scores, axis=-1, keepdims=True)
        exp_terms = jnp.exp(scores - row_top)
        row_total = jnp.sum(exp_terms, axis=-1, keepdims=True)
        weights = (exp_terms / row_total).astype(jnp.bfloat16)
        mixed = jnp.einsum(
            "bhqk,bkhd->bqhd", weights, value_blk, preferred_element_type=jnp.float32
        )
        return (mixed, (row_top + jnp.log(row_total))[..., 0])

    mixed, log_total = lax.map(
        one_step,
        (
            queries.reshape(block_shape),
            key_rows.reshape(block_shape),
            value_rows.reshape(block_shape),
            lengths.reshape(block_shape[:2]),
        ),
    )
    return (mixed.reshape(image_count * seq_len, head_count * HEAD_DIM), log_total)


def attention_backward(queries, key_rows, value_rows, grads, lengths, log_total, seq_len):
    image_count = lengths.shape[0]
    head_count = queries.shape[1] // HEAD_DIM
    block_shape = group_shape(image_count, seq_len, head_count)
    scale = HEAD_DIM ** (-0.5)

    def one_step(block):
        query_blk, key_blk, value_blk, grad_blk, length_blk, total_blk = block
        scores = masked_scores(query_blk, key_blk, length_blk)
        probs = jnp.exp(scores - total_blk[..., None])
        grad_values = jnp.einsum(
            "bhqk,bqhd->bkhd",
            probs.astype(jnp.bfloat16),
            grad_blk,
            preferred_element_type=jnp.float32,
        )
        grad_probs = jnp.einsum(
            "bqhd,bkhd->bhqk", grad_blk, value_blk, preferred_element_type=jnp.float32
        )
        inner = jnp.sum(probs * grad_probs, axis=-1, keepdims=True)
        grad_scores = (probs * (grad_probs - inner)).astype(jnp.bfloat16)
        grad_queries = (
            jnp.einsum("bhqk,bkhd->bqhd", grad_scores, key_blk, preferred_element_type=jnp.float32)
            * scale
        )
        grad_keys = (
            jnp.einsum(
                "bhqk,bqhd->bkhd", grad_scores, query_blk, preferred_element_type=jnp.float32
            )
            * scale
        )
        return (grad_queries, grad_keys, grad_values)

    results = lax.map(
        one_step,
        (
            queries.reshape(block_shape),
            key_rows.reshape(block_shape),
            value_rows.reshape(block_shape),
            grads.reshape(block_shape),
            lengths.reshape(block_shape[:2]),
            log_total,
        ),
    )
    flat = (image_count * seq_len, head_count * HEAD_DIM)
    return tuple((item.reshape(flat) for item in results))


def local(
    tokens,
    long_lengths,
    short_lengths,
    ln1_gain,
    ln1_bias,
    w_query,
    b_query,
    w_key,
    w_value,
    b_value,
    w_out,
    b_out,
    ln2_gain,
    ln2_bias,
    w_up,
    b_up,
    w_down,
    b_down,
    cotangent,
):
    tp_count = lax.axis_size("tp")
    tp_rank = lax.axis_index("tp")
    row_count = tokens.shape[0]
    share = row_count // tp_count
    split = long_lengths.shape[0] * LEN_L
    gain_one = ln1_gain.astype(jnp.float32)
    shift_one = ln1_bias.astype(jnp.float32)
    gain_two = ln2_gain.astype(jnp.float32)
    shift_two = ln2_bias.astype(jnp.float32)
    normed_in = layer_norm(tokens.astype(jnp.float32), gain_one, shift_one).astype(jnp.bfloat16)
    queries = (dot_plain(normed_in, w_query) + b_query.astype(jnp.float32)).astype(jnp.bfloat16)
    key_rows = dot_plain(normed_in, w_key).astype(jnp.bfloat16)
    value_rows = (dot_plain(normed_in, w_value) + b_value.astype(jnp.float32)).astype(jnp.bfloat16)
    long_mixed, long_total = attention_forward(
        queries[:split], key_rows[:split], value_rows[:split], long_lengths, LEN_L
    )
    short_mixed, short_total = attention_forward(
        queries[split:], key_rows[split:], value_rows[split:], short_lengths, LEN_S
    )
    attended = jnp.concatenate([long_mixed, short_mixed], axis=0).astype(jnp.bfloat16)
    attn_sum = lax.psum_scatter(dot_plain(attended, w_out), "tp", scatter_dimension=0, tiled=True)
    own_tokens = lax.dynamic_slice_in_dim(tokens, tp_rank * share, share, 0).astype(jnp.float32)
    resid = own_tokens + attn_sum + b_out.astype(jnp.float32)
    normed_mid = layer_norm(resid, gain_two, shift_two).astype(jnp.bfloat16)
    grad_out = cotangent.astype(jnp.float32)
    mid_rows = lax.all_gather(normed_mid, "tp", axis=0, tiled=True)
    pre_up = dot_plain(mid_rows, w_up) + b_up.astype(jnp.float32)
    activ = jax.nn.gelu(pre_up, approximate=False).astype(jnp.bfloat16)
    ffn_sum = lax.psum_scatter(
        dot_plain(activ, w_down).astype(jnp.bfloat16), "tp", scatter_dimension=0, tiled=True
    ).astype(jnp.float32)
    result = resid + ffn_sum + b_down.astype(jnp.float32)
    grad_rows = lax.all_gather(cotangent, "tp", axis=0, tiled=True)
    grad_w_down = dot_rows(activ, grad_rows)
    grad_activ = dot_back(grad_rows, w_down)
    _, gelu_back = jax.vjp(lambda inner: jax.nn.gelu(inner, approximate=False), pre_up)
    grad_pre = gelu_back(grad_activ)[0].astype(jnp.bfloat16)
    grad_w_up = dot_rows(mid_rows, grad_pre)
    grad_b_up = jnp.sum(grad_pre.astype(jnp.float32), axis=0)
    grad_mid = lax.psum_scatter(dot_back(grad_pre, w_up), "tp", scatter_dimension=0, tiled=True)
    _, norm_two_back = jax.vjp(layer_norm, resid, gain_two, shift_two)
    grad_resid_norm, grad_gain_two, grad_shift_two = norm_two_back(grad_mid)
    grad_resid = grad_out + grad_resid_norm
    grad_b_down = jnp.sum(grad_out, axis=0)
    grad_b_out = jnp.sum(grad_resid, axis=0)
    grad_branch = lax.all_gather(grad_resid.astype(jnp.bfloat16), "tp", axis=0, tiled=True)
    grad_w_out = dot_rows(attended, grad_branch)
    grad_attended = dot_back(grad_branch, w_out).astype(jnp.bfloat16)
    long_grads = attention_backward(
        queries[:split],
        key_rows[:split],
        value_rows[:split],
        grad_attended[:split],
        long_lengths,
        long_total,
        LEN_L,
    )
    short_grads = attention_backward(
        queries[split:],
        key_rows[split:],
        value_rows[split:],
        grad_attended[split:],
        short_lengths,
        short_total,
        LEN_S,
    )
    grad_queries = jnp.concatenate([long_grads[0], short_grads[0]], axis=0).astype(jnp.bfloat16)
    grad_keys = jnp.concatenate([long_grads[1], short_grads[1]], axis=0).astype(jnp.bfloat16)
    grad_values = jnp.concatenate([long_grads[2], short_grads[2]], axis=0).astype(jnp.bfloat16)
    grad_w_query = dot_rows(normed_in, grad_queries)
    grad_b_query = jnp.sum(grad_queries.astype(jnp.float32), axis=0)
    grad_w_key = dot_rows(normed_in, grad_keys)
    grad_w_value = dot_rows(normed_in, grad_values)
    grad_b_value = jnp.sum(grad_values.astype(jnp.float32), axis=0)
    grad_in = lax.psum_scatter(
        dot_back(grad_queries, w_query)
        + dot_back(grad_keys, w_key)
        + dot_back(grad_values, w_value),
        "tp",
        scatter_dimension=0,
        tiled=True,
    )
    _, norm_one_back = jax.vjp(layer_norm, own_tokens, gain_one, shift_one)
    grad_tokens_norm, grad_gain_one, grad_shift_one = norm_one_back(grad_in)
    grad_tokens = grad_resid + grad_tokens_norm
    summed = lax.psum(
        (
            grad_w_query,
            grad_b_query,
            grad_w_key,
            grad_w_value,
            grad_b_value,
            grad_w_out,
            grad_w_up,
            grad_b_up,
            grad_w_down,
        ),
        "dp",
    )
    shared = lax.psum(
        (grad_gain_one, grad_shift_one, grad_b_out, grad_gain_two, grad_shift_two, grad_b_down),
        ("dp", "tp"),
    )
    return (
        result.astype(jnp.bfloat16),
        grad_tokens,
        shared[0],
        shared[1],
        summed[0],
        summed[1],
        summed[2],
        summed[3],
        summed[4],
        summed[5],
        shared[2],
        shared[3],
        shared[4],
        summed[6],
        summed[7],
        summed[8],
        shared[5],
    )


def pick(*arrays):
    tokens, long_lengths, short_lengths, w_query, w_up = (arrays[i] for i in (0, 1, 2, 5, 14))
    fits = (
        lax.axis_size("tp") == 2
        and lax.axis_size("dp") == 16
        and long_lengths.shape[0] == 2
        and short_lengths.shape[0] == 8
        and tokens.shape == (2 * LEN_L + 8 * LEN_S, 768)
        and w_query.shape[1] == 8 * HEAD_DIM
        and w_up.shape[1] == 1536
    )
    return by_images(*arrays) if fits else local(*arrays)


def solution(mesh):
    placed = (
        P("dp", None),
        P("dp"),
        P("dp"),
        P(),
        P(),
        P(None, "tp"),
        P("tp"),
        P(None, "tp"),
        P(None, "tp"),
        P("tp"),
        P("tp", None),
        P(),
        P(),
        P(),
        P(None, "tp"),
        P("tp"),
        P("tp", None),
        P(),
        P(("dp", "tp"), None),
    )
    return jax.shard_map(
        pick,
        mesh=mesh,
        in_specs=placed,
        out_specs=(
            P(("dp", "tp"), None),
            P(("dp", "tp"), None),
            P(),
            P(),
            P(None, "tp"),
            P("tp"),
            P(None, "tp"),
            P(None, "tp"),
            P("tp"),
            P("tp", None),
            P(),
            P(),
            P(),
            P(None, "tp"),
            P("tp"),
            P("tp", None),
            P(),
        ),
        check_vma=False,
    )
```

profile of v0, /device:TPU:0, one launch (start us, length us, event | category | flops | bytes accessed | tf_op | source)
XLA Modules:
  0.0 646.2 jit_solution(5335266576906533658)
XLA Ops:
  18.2 3.3 constant_dynamic-slice_fusion.10
  26.7 9.6 %project_norm.1 = (bf16[2048,768]{1,0:T(8,128)(2,1)}, bf16[2048,768]{1,0:T(8,128)(2,1)}, bf16[2,1152,2048]{2,1,0:T(8,128)(2,1)}) custom-call(s32[1]{0:T(128)} %bitcast.rank_ref, bf16[4096,768]{1,0:T(8,128)(2,1)} %tok_ref.1, f32[1,768]{1,0:T(1,128)} %reshape.171.gain_ref, f32[1,768]{1,0:T(1,128)} %reshape.173.shift_ref, bf16[768,1152]{1,0:T(8,128)(2,1)} %copy-done.7, ...), custom_call_target="tpu_custom_call" | custom-call | flops 3623878656 | bytes 11010048 | tf_op jit(solution)/shard_map/project_norm/pallas_call | solution.py:79
  38.4 8.2 %collective-permute-done = bf16[192,1152]{1,0:T(8,128)(2,1)} collective-permute-done((bf16[192,1152]{1,0:T(8,128)(2,1)}, bf16[192,1152]{1,0:T(8,128)(2,1)}, u32[]{:S(2)}, u32[]{:S(2)}) %collective-permute-start) | collective-permute-done | bytes 442400 | tf_op jit(solution)/shard_map/ppermute | solution.py:764
  47.0 16.7 %attend_forward.2 = (bf16[2,8,48,2048]{3,2,1,0:T(8,128)(2,1)}, f32[2,8,1,2048]{3,2,1,0:T(1,128)}) custom-call(f32[1,2048]{1,0:T(1,128)} %add_select_fusion.mask_ref.refs_0_, bf16[2,3,8,48,2048]{4,3,2,1,0:T(8,128)(2,1)} %bitcast.13), custom_call_target="tpu_custom_call" | custom-call | flops 10737418240 | bytes 6291456 | tf_op jit(solution)/shard_map/attend_forward/pallas_call | solution.py:190
  75.6 3.7 collective-permute-done.7
  81.4 7.9 %collective-permute-done.2 = bf16[384,1152]{1,0:T(8,128)(2,1)S(1)} collective-permute-done((bf16[384,1152]{1,0:T(8,128)(2,1)S(1)}, bf16[384,1152]{1,0:T(8,128)(2,1)S(1)}, u32[]{:S(2)}, u32[]{:S(2)}) %collective-permute-start.2) | collective-permute-done | bytes 884768 | tf_op jit(solution)/shard_map/ppermute | solution.py:769
  91.2 8.0 %project.1 = bf16[2,1152,2048]{2,1,0:T(8,128)(2,1)} custom-call(bf16[2,1152,2048]{2,1,0:T(8,128)(2,1)} %get-tuple-element.52._, bf16[2048,768]{1,0:T(8,128)(2,1)} %get-tuple-element.53.x_ref, bf16[768,1152]{1,0:T(8,128)(2,1)} %maximum_select_fusion.5.w_ref.w2_ref, f32[1152,1]{1,0:T(8,128)} %reshape.183.b_ref), custom_call_target="tpu_custom_call", output_to_operand_aliasing={{}: (0, {})} | custom-call | flops 3623878656 | bytes 7864320 | tf_op jit(solution)/shard_map/project/pallas_call | solution.py:107
  99.2 16.9 %attend_forward.3 = (bf16[2,8,48,2048]{3,2,1,0:T(8,128)(2,1)}, f32[2,8,1,2048]{3,2,1,0:T(1,128)}) custom-call(f32[1,2048]{1,0:T(1,128)} %add_select_fusion.mask_ref.refs_0_, bf16[2,3,8,48,2048]{4,3,2,1,0:T(8,128)(2,1)} %bitcast.14, bf16[2,8,48,2048]{3,2,1,0:T(8,128)(2,1)} %get-tuple-element.54.refs_0_, ...), custom_call_target="tpu_custom_call", output_to_operand_aliasing={{0}: (2, {}), {1}: (3, {})} | custom-call | flops 10737418240 | bytes 6291456 | tf_op jit(solution)/shard_map/attend_forward/pallas_call | solution.py:190
  116.1 8.6 %middle.1 = (f32[2048,768]{1,0:T(8,128)}, bf16[2048,768]{1,0:T(8,128)(2,1)}) custom-call(bf16[2048,768]{1,0:T(8,128)(2,1)} %get-tuple-element.51.tok_ref, bf16[768,2048]{1,0:T(8,128)(2,1)} %bitcast.18, bf16[768,768]{1,0:T(8,128)(2,1)} %pad_maximum_fusion.w_ref, f32[1,768]{1,0:T(1,128)} %reshape.175.b_ref, f32[1,768]{1,0:T(1,128)} %reshape.177.gain_ref, ...), custom_call_target="tpu_custom_call" | custom-call | flops 2415919104 | bytes 18874368 | tf_op jit(solution)/shard_map/middle/pallas_call | solution.py:508
  124.7 3.1 maximum_select_fusion.4.down_ref
  127.9 11.8 %collective-permute-done.10 = bf16[384,1536]{1,0:T(8,128)(2,1)} collective-permute-done((bf16[384,1536]{1,0:T(8,128)(2,1)S(1)}, bf16[384,1536]{1,0:T(8,128)(2,1)}, u32[]{:S(2)}, u32[]{:S(2)}) %collective-permute-start.10) | collective-permute-done | bytes 1179680 | tf_op jit(solution)/shard_map/ppermute | solution.py:769
  142.7 40.4 %feed.3 = (f32[2048,768]{1,0:T(8,128)}, f32[2048,768]{1,0:T(8,128)}, bf16[768,1536]{1,0:T(8,128)(2,1)}, bf16[1536,768]{1,0:T(8,128)(2,1)}, f32[1,1536]{1,0:T(1,128)}) custom-call(bf16[2048,768]{1,0:T(8,128)(2,1)} %get-tuple-element.58.mid_ref, bf16[2048,768]{1,0:T(8,128)(2,1)} %maximum_select_fusion.1.grad_ref, ...), custom_call_target="tpu_custom_call" | custom-call | flops 28991029248 | bytes 31457280 | tf_op jit(solution)/shard_map/feed/pallas_call | solution.py:588
  187.2 48.3 %feed.2 = (f32[2048,768]{1,0:T(8,128)}, f32[2048,768]{1,0:T(8,128)}, bf16[768,1536]{1,0:T(8,128)(2,1)}, bf16[1536,768]{1,0:T(8,128)(2,1)}, f32[1,1536]{1,0:T(1,128)}) custom-call(bf16[2048,768]{1,0:T(8,128)(2,1)} %get-tuple-element.58.mid_ref, bf16[2048,768]{1,0:T(8,128)(2,1)} %maximum_select_fusion.1.grad_ref, bf16[768,1536]{1,0:T(8,128)(2,1)} %up_ref.1, ...), custom_call_target="tpu_custom_call" | custom-call | flops 28991029248 | bytes 31457280 | tf_op jit(solution)/shard_map/feed/pallas_call | solution.py:588
  235.6 21.8 %branch.1 = (bf16[2048,768]{1,0:T(8,128)(2,1)}, f32[2048,768]{1,0:T(8,128)}, bf16[768,2048]{1,0:T(8,128)(2,1)}, bf16[768,384]{1,0:T(8,128)(2,1)}, bf16[768,384]{1,0:T(8,128)(2,1)}, /*index=5*/f32[8,768]{1,0:T(8,128)}) custom-call(f32[2048,768]{1,0:T(8,128)} %get-tuple-element.57.resid_ref, f32[2048,768]{1,0:T(8,128)} %get-tuple-element.59.sum1_ref, ...), custom_call_target="tpu_custom_call" | custom-call | flops 4831838208 | bytes 50331648 | tf_op jit(solution)/shard_map/branch/pallas_call | solution.py:656
  257.4 3.4 constant_dynamic-slice_fusion.6
  273.7 24.5 %collective-permute-done.14 = bf16[1024,768]{1,0:T(8,128)(2,1)S(1)} collective-permute-done((bf16[1024,768]{1,0:T(8,128)(2,1)}, bf16[1024,768]{1,0:T(8,128)(2,1)S(1)}, u32[]{:S(2)}, u32[]{:S(2)}) %collective-permute-start.14) | collective-permute-done | bytes 1572896 | tf_op jit(solution)/shard_map/ppermute | solution.py:764
  300.2 54.2 %collective-permute-done.20.refs_10_ = bf16[384,384]{1,0:T(8,128)(2,1)S(1)} collective-permute-done((bf16[384,384]{1,0:T(8,128)(2,1)S(1)}, bf16[384,384]{1,0:T(8,128)(2,1)S(1)}, u32[]{:S(2)}, u32[]{:S(2)}) %collective-permute-start.20) | collective-permute-done | bytes 294944 | tf_op jit(solution)/shard_map/ppermute | solution.py:764
  355.1 98.9 %attend_backward.1 = (bf16[2,3,8,48,2048]{4,3,2,1,0:T(8,128)(2,1)}, bf16[768,1536]{1,0:T(8,128)(2,1)}, bf16[1536,768]{1,0:T(8,128)(2,1)}, bf16[768,384]{1,0:T(8,128)(2,1)}) custom-call(f32[1,2048]{1,0:T(1,128)} %add_select_fusion.mask_ref.refs_0_, bf16[2,3,8,48,2048]{4,3,2,1,0:T(8,128)(2,1)} %bitcast.15, bf16[2,8,48,2048]{3,2,1,0:T(8,128)(2,1)} %get-tuple-element.56.refs_2_, ...), custom_call_target="tpu_custom_call" | custom-call | flops 53687091200 | bytes 25165824 | tf_op jit(solution)/shard_map/attend_backward/pallas_call | solution.py:479
  454.0 26.6 %back.1 = (f32[2048,768]{1,0:T(8,128)}, bf16[768,1152]{1,0:T(8,128)(2,1)}, bf16[768,1152]{1,0:T(8,128)(2,1)}, f32[2,1152,1]{2,1,0:T(8,128)}, f32[8,768]{1,0:T(8,128)}) custom-call(bf16[2048,768]{1,0:T(8,128)(2,1)} %get-tuple-element.51.tok_ref, bf16[2048,768]{1,0:T(8,128)(2,1)} %get-tuple-element.53.x_ref, bf16[2,1152,2048]{2,1,0:T(8,128)(2,1)} %bitcast.22, ...), custom_call_target="tpu_custom_call" | custom-call | flops 14495514624 | bytes 25165824 | tf_op jit(solution)/shard_map/back/pallas_call | solution.py:706
  485.7 3.2 dynamic-slice_convert_fusion
  491.8 69.9 %psum.7 = f32[9216]{0:T(1024)S(1)} all-reduce(f32[9216]{0:T(1024)S(1)} %select_dynamic-update-slice_fusion), channel_id=1, replica_groups=mesh['dp'=16,'tp'=2] {'dp','tp'}, use_global_device_ids=true, to_apply=%region_0.1 | all-reduce | flops 9216 | bytes 73728 | tf_op jit(solution)/shard_map/psum | solution.py:882
  582.2 11.5 %collective-permute-done.23.refs_1_ = bf16[384,1152]{1,0:T(8,128)(2,1)S(1)} collective-permute-done((bf16[384,1152]{1,0:T(8,128)(2,1)S(1)}, bf16[384,1152]{1,0:T(8,128)(2,1)S(1)}, u32[]{:S(2)}, u32[]{:S(2)}) %collective-permute-start.23) | collective-permute-done | bytes 884768 | tf_op jit(solution)/shard_map/ppermute | solution.py:764
  594.7 47.7 %plane_sum.1 = bf16[768,1152]{1,0:T(8,128)(2,1)} custom-call(bf16[768,1152]{1,0:T(8,128)(2,1)} %get-tuple-element.80.refs_0_, bf16[384,1152]{1,0:T(8,128)(2,1)} %copy-done.6), custom_call_target="tpu_custom_call" | custom-call | tf_op jit(solution)/shard_map/plane_sum/pallas_call | solution.py:750
  642.4 3.3 fusion.3
  (190 shorter events, 93.0 us)
Async XLA Ops:
  1.5 24.1 %collective-permute-start.3 = (f32[2304]{0:T(1024)S(1)}, f32[2304]{0:T(1024)S(1)}, u32[]{:S(2)}, u32[]{:S(2)}) collective-permute-start(f32[2304]{0:T(1024)S(1)} %maximum_convert_fusion), channel_id=1, source_target_pairs={{0,1},{1,0},{2,3},{3,2},{4,5},{5,4},{6,7},{7,6},{8,9},{9,8},{10,11... | collective-permute-start | bytes 27656 | tf_op jit(solution)/shard_map/ppermute | solution.py:764
  5.5 21.2 %collective-permute-start.4 = (bf16[96,768]{1,0:T(8,128)(2,1)S(1)}, bf16[96,768]{1,0:T(8,128)(2,1)S(1)}, u32[]{:S(2)}, u32[]{:S(2)}) collective-permute-start(bf16[96,768]{1,0:T(8,128)(2,1)S(1)} %constant_dynamic-slice_fusion.11), channel_id=1, source_target_pairs={{0,1},{1,0},{2,3},{3,2},{4,5},{5,4},{6,7},{7,6},{8,9},{9,8},{10,11... | collective-permute-start | bytes 442376 | tf_op jit(solution)/shard_map/ppermute | solution.py:764
  7.7 57.7 %collective-permute-start.8 = (bf16[192,1536]{1,0:T(8,128)(2,1)}, bf16[192,1536]{1,0:T(8,128)(2,1)}, u32[]{:S(2)}, u32[]{:S(2)}) collective-permute-start(bf16[192,1536]{1,0:T(8,128)(2,1)} %constant_dynamic-slice_fusion.8), channel_id=1, source_target_pairs={{0,1},{1,0},{2,3},{3,2},{4,5},{5,4},{6,7},{7,6},{8,9},{9,8},{10,11... | collective-permute-start | bytes 1769480 | tf_op jit(solution)/shard_map/ppermute | solution.py:764
  11.7 34.9 %collective-permute-start.11 = (bf16[384,768]{1,0:T(8,128)(2,1)}, bf16[384,768]{1,0:T(8,128)(2,1)}, u32[]{:S(2)}, u32[]{:S(2)}) collective-permute-start(bf16[384,768]{1,0:T(8,128)(2,1)} %constant_dynamic-slice_fusion.7), channel_id=1, source_target_pairs={{0,1},{1,0},{2,3},{3,2},{4,5},{5,4},{6,7},{7,6},{8,9},{9,8},{10,11... | collective-permute-start | bytes 1769480 | tf_op jit(solution)/shard_map/ppermute | solution.py:764
  14.1 32.4 %collective-permute-start = (bf16[192,1152]{1,0:T(8,128)(2,1)}, bf16[192,1152]{1,0:T(8,128)(2,1)}, u32[]{:S(2)}, u32[]{:S(2)}) collective-permute-start(bf16[192,1152]{1,0:T(8,128)(2,1)} %constant_dynamic-slice_fusion.12), channel_id=1, source_target_pairs={{0,1},{1,0},{2,3},{3,2},{4,5},{5,4},{6,7},{7,6},{8,9},{9,8},{10,11... | collective-permute-start | bytes 1327112 | tf_op jit(solution)/shard_map/ppermute | solution.py:764
  25.6 53.7 %collective-permute-start.7 = (bf16[1024,768]{1,0:T(8,128)(2,1)}, bf16[1024,768]{1,0:T(8,128)(2,1)S(1)}, u32[]{:S(2)}, u32[]{:S(2)}) collective-permute-start(bf16[1024,768]{1,0:T(8,128)(2,1)} %get-tuple-element.131), channel_id=1, source_target_pairs={{0,1},{1,0},{2,3},{3,2},{4,5},{5,4},{6,7},{7,6},{8,9},{9,8},{10,11... | collective-permute-start | bytes 4718600 | tf_op jit(solution)/shard_map/ppermute | solution.py:764
  26.7 9.6 %collective-permute-start.5 = (bf16[96,768]{1,0:T(8,128)(2,1)S(1)}, bf16[96,768]{1,0:T(8,128)(2,1)S(1)}, u32[]{:S(2)}, u32[]{:S(2)}) collective-permute-start(bf16[96,768]{1,0:T(8,128)(2,1)S(1)} %collective-permute-done.4), channel_id=1, source_target_pairs={{0,2},{2,0},{4,6},{6,4},{8,10},{10,8},{12,14},{14,12},{16,18},{18,... | collective-permute-start | bytes 442376 | tf_op jit(solution)/shard_map/ppermute | solution.py:769
  36.3 32.3 %collective-permute-start.6 = (bf16[192,768]{1,0:T(8,128)(2,1)S(1)}, bf16[192,768]{1,0:T(8,128)(2,1)S(1)}, u32[]{:S(2)}, u32[]{:S(2)}) collective-permute-start(bf16[192,768]{1,0:T(8,128)(2,1)S(1)} %maximum_select_fusion.10), channel_id=1, source_target_pairs={{0,4},{2,6},{4,0},{6,2},{8,12},{10,14},{12,8},{14,10},{16,20},{18,... | collective-permute-start | bytes 884744 | tf_op jit(solution)/shard_map/ppermute | solution.py:769
  46.5 18.8 %collective-permute-start.1 = (bf16[192,1152]{1,0:T(8,128)(2,1)}, bf16[192,1152]{1,0:T(8,128)(2,1)S(1)}, u32[]{:S(2)}, u32[]{:S(2)}) collective-permute-start(bf16[192,1152]{1,0:T(8,128)(2,1)} %collective-permute-done), channel_id=1, source_target_pairs={{0,2},{2,0},{4,6},{6,4},{8,10},{10,8},{12,14},{14,12},{16,18},{18,... | collective-permute-start | bytes 1327112 | tf_op jit(solution)/shard_map/ppermute | solution.py:769
  46.5 23.4 %collective-permute-start.12 = (bf16[384,768]{1,0:T(8,128)(2,1)}, bf16[384,768]{1,0:T(8,128)(2,1)S(1)}, u32[]{:S(2)}, u32[]{:S(2)}) collective-permute-start(bf16[384,768]{1,0:T(8,128)(2,1)} %collective-permute-done.11), channel_id=1, source_target_pairs={{0,2},{2,0},{4,6},{6,4},{8,10},{10,8},{12,14},{14,12},{16,18},{18,... | collective-permute-start | bytes 1769480 | tf_op jit(solution)/shard_map/ppermute | solution.py:769
  65.3 6.5 %collective-permute-start.9 = (bf16[192,1536]{1,0:T(8,128)(2,1)}, bf16[192,1536]{1,0:T(8,128)(2,1)S(1)}, u32[]{:S(2)}, u32[]{:S(2)}) collective-permute-start(bf16[192,1536]{1,0:T(8,128)(2,1)} %collective-permute-done.8), channel_id=1, source_target_pairs={{0,2},{2,0},{4,6},{6,4},{8,10},{10,8},{12,14},{14,12},{16,18},{18,... | collective-permute-start | bytes 1769480 | tf_op jit(solution)/shard_map/ppermute | solution.py:769
  66.8 22.5 %collective-permute-start.2 = (bf16[384,1152]{1,0:T(8,128)(2,1)S(1)}, bf16[384,1152]{1,0:T(8,128)(2,1)S(1)}, u32[]{:S(2)}, u32[]{:S(2)}) collective-permute-start(bf16[384,1152]{1,0:T(8,128)(2,1)S(1)} %maximum_select_fusion.8), channel_id=1, source_target_pairs={{0,4},{2,6},{4,0},{6,2},{8,12},{10,14},{12,8},{14,10},{16,20},{18,... | collective-permute-start | bytes 2654216 | tf_op jit(solution)/shard_map/ppermute | solution.py:769
  71.6 53.1 %collective-permute-start.13 = (bf16[768,768]{1,0:T(8,128)(2,1)S(1)}, bf16[768,768]{1,0:T(8,128)(2,1)}, u32[]{:S(2)}, u32[]{:S(2)}) collective-permute-start(bf16[768,768]{1,0:T(8,128)(2,1)S(1)} %maximum_select_fusion.7), channel_id=1, source_target_pairs={{0,4},{2,6},{4,0},{6,2},{8,12},{10,14},{12,8},{14,10},{16,20},{18,... | collective-permute-start | bytes 3538952 | tf_op jit(solution)/shard_map/ppermute | solution.py:769
  73.7 65.9 %collective-permute-start.10 = (bf16[384,1536]{1,0:T(8,128)(2,1)S(1)}, bf16[384,1536]{1,0:T(8,128)(2,1)}, u32[]{:S(2)}, u32[]{:S(2)}) collective-permute-start(bf16[384,1536]{1,0:T(8,128)(2,1)S(1)} %maximum_select_fusion.6), channel_id=1, source_target_pairs={{0,4},{2,6},{4,0},{6,2},{8,12},{10,14},{12,8},{14,10},{16,20},{18,... | collective-permute-start | bytes 3538952 | tf_op jit(solution)/shard_map/ppermute | solution.py:769
  185.6 76.9 %collective-permute-start.15 = (bf16[384,1536]{1,0:T(8,128)(2,1)}, bf16[384,1536]{1,0:T(8,128)(2,1)}, u32[]{:S(2)}, u32[]{:S(2)}) collective-permute-start(bf16[384,1536]{1,0:T(8,128)(2,1)} %constant_dynamic-slice_fusion.4), channel_id=1, source_target_pairs={{0,2},{2,0},{4,6},{6,4},{8,10},{10,8},{12,14},{14,12},{16,18},{18,... | collective-permute-start | bytes 3538952 | tf_op jit(solution)/shard_map/ppermute | solution.py:769
  186.7 78.7 %collective-permute-start.17 = (bf16[768,768]{1,0:T(8,128)(2,1)}, bf16[768,768]{1,0:T(8,128)(2,1)}, u32[]{:S(2)}, u32[]{:S(2)}) collective-permute-start(bf16[768,768]{1,0:T(8,128)(2,1)} %constant_dynamic-slice_fusion.3), channel_id=1, source_target_pairs={{0,2},{2,0},{4,6},{6,4},{8,10},{10,8},{12,14},{14,12},{16,18},{18,... | collective-permute-start | bytes 3538952 | tf_op jit(solution)/shard_map/ppermute | solution.py:769
  260.7 37.4 %collective-permute-start.14 = (bf16[1024,768]{1,0:T(8,128)(2,1)}, bf16[1024,768]{1,0:T(8,128)(2,1)S(1)}, u32[]{:S(2)}, u32[]{:S(2)}) collective-permute-start(bf16[1024,768]{1,0:T(8,128)(2,1)} %get-tuple-element.129), channel_id=1, source_target_pairs={{0,1},{1,0},{2,3},{3,2},{4,5},{5,4},{6,7},{7,6},{8,9},{9,8},{10,11... | collective-permute-start | bytes 4718600 | tf_op jit(solution)/shard_map/ppermute | solution.py:764
  265.1 89.3 %collective-permute-start.16 = (bf16[384,1536]{1,0:T(8,128)(2,1)}, bf16[384,1536]{1,0:T(8,128)(2,1)}, u32[]{:S(2)}, u32[]{:S(2)}) collective-permute-start(bf16[384,1536]{1,0:T(8,128)(2,1)} %add_convert_fusion.1), channel_id=1, source_target_pairs={{0,1},{1,0},{2,3},{3,2},{4,5},{5,4},{6,7},{7,6},{8,9},{9,8},{10,11... | collective-permute-start | bytes 3538952 | tf_op jit(solution)/shard_map/ppermute | solution.py:764
  268.0 86.4 %collective-permute-start.18 = (bf16[768,768]{1,0:T(8,128)(2,1)}, bf16[768,768]{1,0:T(8,128)(2,1)}, u32[]{:S(2)}, u32[]{:S(2)}) collective-permute-start(bf16[768,768]{1,0:T(8,128)(2,1)} %add_convert_fusion), channel_id=1, source_target_pairs={{0,1},{1,0},{2,3},{3,2},{4,5},{5,4},{6,7},{7,6},{8,9},{9,8},{10,11... | collective-permute-start | bytes 3538952 | tf_op jit(solution)/shard_map/ppermute | solution.py:764
  270.5 1.8 collective-permute-start.19
  273.3 81.1 %collective-permute-start.20 = (bf16[384,384]{1,0:T(8,128)(2,1)S(1)}, bf16[384,384]{1,0:T(8,128)(2,1)S(1)}, u32[]{:S(2)}, u32[]{:S(2)}) collective-permute-start(bf16[384,384]{1,0:T(8,128)(2,1)S(1)} %add_convert_fusion.3), channel_id=1, source_target_pairs={{0,1},{1,0},{2,3},{3,2},{4,5},{5,4},{6,7},{7,6},{8,9},{9,8},{10,11... | collective-permute-start | bytes 884744 | tf_op jit(solution)/shard_map/ppermute | solution.py:764
  485.3 86.1 %collective-permute-start.22 = (bf16[384,1152]{1,0:T(8,128)(2,1)}, bf16[384,1152]{1,0:T(8,128)(2,1)}, u32[]{:S(2)}, u32[]{:S(2)}) collective-permute-start(bf16[384,1152]{1,0:T(8,128)(2,1)} %constant_dynamic-slice_fusion), channel_id=1, source_target_pairs={{0,2},{2,0},{4,6},{6,4},{8,10},{10,8},{12,14},{14,12},{16,18},{18,... | collective-permute-start | bytes 2654216 | tf_op jit(solution)/shard_map/ppermute | solution.py:769
  488.9 88.6 %collective-permute-start.21 = (bf16[1024,768]{1,0:T(8,128)(2,1)}, bf16[1024,768]{1,0:T(8,128)(2,1)}, u32[]{:S(2)}, u32[]{:S(2)}) collective-permute-start(bf16[1024,768]{1,0:T(8,128)(2,1)} %dynamic-slice_convert_fusion), channel_id=1, source_target_pairs={{0,1},{1,0},{2,3},{3,2},{4,5},{5,4},{6,7},{7,6},{8,9},{9,8},{10,11... | collective-permute-start | bytes 4718600 | tf_op jit(solution)/shard_map/ppermute | solution.py:764
  573.1 20.7 %collective-permute-start.23 = (bf16[384,1152]{1,0:T(8,128)(2,1)S(1)}, bf16[384,1152]{1,0:T(8,128)(2,1)S(1)}, u32[]{:S(2)}, u32[]{:S(2)}) collective-permute-start(bf16[384,1152]{1,0:T(8,128)(2,1)S(1)} %add_convert_fusion.2), channel_id=1, source_target_pairs={{0,1},{1,0},{2,3},{3,2},{4,5},{5,4},{6,7},{7,6},{8,9},{9,8},{10,11... | collective-permute-start | bytes 2654216 | tf_op jit(solution)/shard_map/ppermute | solution.py:764
  (32 other events, 222.8 us)
where the time goes:
time: 656 us; the launch traced here: 646 us
  Pallas kernels  344 us (52%)
  waiting for transfers between devices  123 us (19%)
  blocking collectives  69.9 us (11%)
  local copies, waits for them, and re-layouts  44.4 us (7%)
  other arithmetic  40.7 us (6%)
  starting transfers between devices  22.6 us (3%)
    ppermute x12, waiting for transfers between devices, swap_tp(): return lax.ppermute(array, 'tp', [(0, 1), (1, 0)])  102 us
    pallas_call x1, Pallas kernels, attend_backward(): pl.pallas_call(functools.partial(attend_backward_kernel, block=block, sum...  98.9 us
    pallas_call x2, Pallas kernels, feed(): pl.pallas_call(functools.partial(feed_kernel, chunk=chunk), grid=(hidden...  88.7 us
    psum x1, blocking collectives, by_images(): packed = lax.psum(packed, ('dp', 'tp'))  69.9 us
    pallas_call x1, Pallas kernels, plane_sum(): pl.pallas_call(sum_kernel, in_specs=[anywhere, anywhere], out_specs=anywh...  47.7 us
    pallas_call x2, Pallas kernels, attend_forward(): pl.pallas_call(functools.partial(attend_forward_kernel, block=block), gri...  33.6 us
    pallas_call x1, Pallas kernels, back(): pl.pallas_call(back_kernel, grid=(rows // block,), in_specs=[by_row, by_r...  26.6 us
    pallas_call x1, Pallas kernels, branch(): pl.pallas_call(branch_kernel, grid=(rows // block,), in_specs=[by_row] *...  21.8 us
  transfers between devices with their start and end apart: 24, of which 8 were waited for; matrix products, arithmetic and copies ran while one was open for 10% of the time, Pallas kernels for 20%

commit v1 on v0

--- a/solution.py
+++ b/solution.py
@@ -210,129 +210,149 @@
     )(mask, qkv, *earlier)
 
 
-class PlaneSum:
-    COPIES = 10
-
-    def __init__(self, refs):
-        (self.own, self.seen, self.out, self.acc, self.from_core, self.seen_here, self.from_x,
-         self.from_z, self.send, self.recv, self.local) = refs
+class Place:
+    def __init__(self):
         me = lax.axis_index("dp")
         self.core, self.x, self.z = me % 2, (me // 2) % 2, me // 4
-        self.rows = self.own.shape[0]
+        self.rank = lax.axis_index("tp")
+
+    def at(self, z=None, x=None, core=None):
+        z = self.z if z is None else z
+        x = self.x if x is None else x
+        core = self.core if core is None else core
+        return {"dp": (z * 2 + x) * 2 + core}
+
+    def across_core(self):
+        return self.at(core=1 - self.core)
+
+    def across_x(self):
+        return self.at(x=1 - self.x)
+
+    def along_z(self, step):
+        return self.at(z=(self.z + step) % 4)
+
+    def partner(self):
+        return {"tp": 1 - self.rank}
+
+    def greet(self):
+        barrier = pltpu.get_barrier_semaphore()
+        others = [self.across_core(), self.across_x(), self.partner()]
+        others += [self.along_z(step) for step in (1, 2, 3)]
+        for other in others:
+            pl.semaphore_signal(
+                barrier, inc=1, device_id=other, device_id_type=pl.DeviceIdType.MESH
+            )
+        pl.semaphore_wait(barrier, len(others))
+
+
+def send_to(source, target, send, recv, device):
+    return pltpu.make_async_remote_copy(
+        src_ref=source,
+        dst_ref=target,
+        send_sem=send,
+        recv_sem=recv,
+        device_id=device,
+        device_id_type=pl.DeviceIdType.MESH,
+    )
+
+
+def part(ref, start, count):
+    return ref.at[pl.ds(pl.multiple_of(start, 16), count)]
+
+
+def add_rows(target, start, count, terms):
+    tile = 48
+
+    def body(i, _):
+        at = pl.multiple_of(i * tile, 16)
+        here = pl.ds(pl.multiple_of(start + at, 16), tile)
+        total = target[here, :].astype(F32)
+        for term in terms:
+            total = total + term[pl.ds(at, tile), :].astype(F32)
+        target[here, :] = total.astype(BF16)
+        return 0
+
+    lax.fori_loop(0, count // tile, body, 0)
+
+
+class PlaneSum:
+    def __init__(self, place, own, seen, out, refs):
+        self.place, self.own, self.seen, self.out = place, own, seen, out
+        (self.acc, self.seen_here, self.from_core, self.from_x, self.from_z,
+         self.send, self.recv, self.local) = refs
+        self.rows = own.shape[0]
 
     @staticmethod
-    def buffers(shape):
-        rows, width = shape
+    def buffers(rows, width):
         return [
             pltpu.VMEM((rows // 2, width), BF16),
             pltpu.VMEM((rows // 2, width), BF16),
             pltpu.VMEM((rows // 2, width), BF16),
             pltpu.VMEM((rows // 4, width), BF16),
             pltpu.VMEM((3, rows // 16, width), BF16),
-            pltpu.SemaphoreType.DMA((PlaneSum.COPIES,)),
-            pltpu.SemaphoreType.DMA((PlaneSum.COPIES,)),
+            pltpu.SemaphoreType.DMA((10,)),
+            pltpu.SemaphoreType.DMA((10,)),
             pltpu.SemaphoreType.DMA((3,)),
         ]
 
-    def device(self, z, x, core):
-        return {"dp": (z * 2 + x) * 2 + core}
-
     def copy(self, source, target, place, device):
-        return pltpu.make_async_remote_copy(
-            src_ref=source,
-            dst_ref=target,
-            send_sem=self.send.at[place],
-            recv_sem=self.recv.at[place],
-            device_id=device,
-            device_id_type=pl.DeviceIdType.MESH,
-        )
-
-    def part(self, ref, start, count):
-        return ref.at[pl.ds(pl.multiple_of(start, 16), count)]
+        return send_to(source, target, self.send.at[place], self.recv.at[place], device)
 
     def core_copy(self):
         half = self.rows // 2
-        return self.copy(
-            self.part(self.own, (1 - self.core) * half, half),
-            self.from_core,
-            0,
-            self.device(self.z, self.x, 1 - self.core),
-        )
+        source = part(self.own, (1 - self.place.core) * half, half)
+        return self.copy(source, self.from_core, 0, self.place.across_core())
 
     def local_copies(self):
         half = self.rows // 2
-        return [
-            pltpu.make_async_copy(
-                self.part(self.own, self.core * half, half), self.acc, self.local.at[0]
-            ),
-            pltpu.make_async_copy(self.seen, self.seen_here, self.local.at[1]),
-        ]
+        source = part(self.own, self.place.core * half, half)
+        copies = [pltpu.make_async_copy(source, self.acc, self.local.at[0])]
+        if self.seen is not None:
+            copies.append(pltpu.make_async_copy(self.seen, self.seen_here, self.local.at[1]))
+        return copies
 
     def x_copy(self):
         count = self.rows // 4
-        return self.copy(
-            self.part(self.acc, (1 - self.x) * count, count),
-            self.from_x,
-            1,
-            self.device(self.z, 1 - self.x, self.core),
-        )
+        source = part(self.acc, (1 - self.place.x) * count, count)
+        return self.copy(source, self.from_x, 1, self.place.across_x())
 
     def z_copies(self):
         count = self.rows // 16
         copies = []
         for step in (1, 2, 3):
-            there = (self.z + step) % 4
-            copies.append(
-                self.copy(
-                    self.part(self.acc, self.x * 4 * count + there * count, count),
-                    self.from_z.at[step - 1],
-                    1 + step,
-                    self.device(there, self.x, self.core),
-                )
-            )
+            there = (self.place.z + step) % 4
+            source = part(self.acc, self.place.x * 4 * count + there * count, count)
+            target = self.from_z.at[step - 1]
+            copies.append(self.copy(source, target, 1 + step, self.place.along_z(step)))
         return copies
 
     def piece(self):
         count = self.rows // 16
-        inside = self.x * 4 * count + self.z * count
-        place = self.core * 8 * count + inside
-        return self.part(self.acc, inside, count), self.part(self.out, place, count)
+        inside = self.place.x * 4 * count + self.place.z * count
+        return (
+            part(self.acc, inside, count),
+            part(self.out, self.place.core * 8 * count + inside, count),
+        )
 
     def keep_copy(self):
-        mine, place = self.piece()
-        return pltpu.make_async_copy(mine, place, self.local.at[2])
+        mine, there = self.piece()
+        return pltpu.make_async_copy(mine, there, self.local.at[2])
 
     def back_z_copies(self):
-        mine, place = self.piece()
+        mine, there = self.piece()
         return [
-            self.copy(mine, place, 4 + step, self.device((self.z + step) % 4, self.x, self.core))
-            for step in (1, 2, 3)
+            self.copy(mine, there, 4 + step, self.place.along_z(step)) for step in (1, 2, 3)
         ]
 
     def back_x_copy(self):
         count = self.rows // 4
-        place = self.part(self.out, self.core * 2 * count + self.x * count, count)
-        return self.copy(place, place, 8, self.device(self.z, 1 - self.x, self.core))
+        there = part(self.out, self.place.core * 2 * count + self.place.x * count, count)
+        return self.copy(there, there, 8, self.place.across_x())
 
     def back_core_copy(self):
         count = self.rows // 2
-        place = self.part(self.out, self.core * count, count)
-        return self.copy(place, place, 9, self.device(self.z, self.x, 1 - self.core))
-
-    def add(self, start, count, terms):
-        tile = 48
-        width = self.acc.shape[1]
-
-        def body(i, _):
-            at = pl.multiple_of(i * tile, 16)
-            here = pl.ds(pl.multiple_of(start + at, 16), tile)
-            total = self.acc[here, :].astype(F32)
-            for term in terms:
-                total = total + term[pl.ds(at, tile), :].astype(F32)
-            self.acc[here, :] = total.astype(BF16)
-            return 0
-
-        lax.fori_loop(0, count // tile, body, 0)
+        there = part(self.out, self.place.core * count, count)
+        return self.copy(there, there, 9, self.place.across_core())
 
     def begin(self):
         self.core_copy().start()
@@ -343,13 +363,13 @@
         self.core_copy().wait()
         for copy in self.local_copies():
             copy.wait()
-        self.add(0, self.rows // 2, [self.from_core, self.seen_here])
+        add_rows(self.acc, 0, self.rows // 2, [self.from_core, self.seen_here])
         self.x_copy().start()
 
     def along_z(self):
         self.x_copy().wait()
         count = self.rows // 4
-        self.add(self.x * count, count, [self.from_x])
+        add_rows(self.acc, self.place.x * count, count, [self.from_x])
         for copy in self.z_copies():
             copy.start()
 
@@ -357,8 +377,8 @@
         for copy in self.z_copies():
             copy.wait()
         count = self.rows // 16
-        inside = self.x * 4 * count + self.z * count
-        self.add(inside, count, [self.from_z.at[i] for i in range(3)])
+        inside = self.place.x * 4 * count + self.place.z * count
+        add_rows(self.acc, inside, count, [self.from_z.at[i] for i in range(3)])
         self.keep_copy().start()
         for copy in self.back_z_copies():
             copy.start()
@@ -377,119 +397,101 @@
         self.back_core_copy().wait()
 
 
-def greet_plane():
-    me = lax.axis_index("dp")
-    core, x, z = me % 2, (me // 2) % 2, me // 4
-    barrier = pltpu.get_barrier_semaphore()
-    others = [(z, x, 1 - core), (z, 1 - x, core)] + [((z + i) % 4, x, core) for i in (1, 2, 3)]
-    for other_z, other_x, other_core in others:
-        pl.semaphore_signal(
-            barrier,
-            inc=1,
-            device_id={"dp": (other_z * 2 + other_x) * 2 + other_core},
-            device_id_type=pl.DeviceIdType.MESH,
+class PartnerTerm:
+    def __init__(self, place, other, seen, refs):
+        self.place, self.other, self.seen = place, other, seen
+        self.from_core, self.send, self.recv = refs
+        self.half = other.shape[0] // 2
+
+    @staticmethod
+    def buffers(rows, width):
+        return [
+            pltpu.VMEM((rows // 2, width), BF16),
+            pltpu.SemaphoreType.DMA((2,)),
+            pltpu.SemaphoreType.DMA((2,)),
+        ]
+
+    def core_copy(self):
+        source = part(self.other, (1 - self.place.core) * self.half, self.half)
+        return send_to(
+            source, self.from_core, self.send.at[0], self.recv.at[0], self.place.across_core()
         )
-    pl.semaphore_wait(barrier, len(others))
-
-
-SUM_STEPS = (
-    (0, 1, 5, 8, 12, 15, 15),
-    (0, 4, 8, 12, 15, 15, 15),
-    (0, 2, 5, 9, 12, 15, 15),
-)
-
-
-def attend_backward_kernel(*refs, block, sums):
-    mask_ref, qkv_ref, out_ref, log_ref, grad_ref = refs[:5]
-    sum_in = refs[5 : 5 + 2 * sums]
-    dqkv_ref = refs[5 + 2 * sums]
-    sum_out = refs[6 + 2 * sums : 6 + 3 * sums]
-    scratch = refs[6 + 3 * sums :]
-    each = len(scratch) // sums
-    plane = [
-        PlaneSum((*sum_in[2 * i : 2 * i + 2], sum_out[i], *scratch[each * i : each * (i + 1)]))
-        for i in range(sums)
-    ]
-    step = pl.program_id(0)
-
-    for at in sorted({at for times in SUM_STEPS for at in times[:-2]}):
-
-        @pl.when(step == at)
-        def _(at=at):
-            if at == 0:
-                greet_plane()
-            for one, times in zip(plane, SUM_STEPS):
-                for when, action in zip(
-                    times[:-2],
-                    (one.begin, one.along_x, one.along_z, one.back_along_z, one.back_along_x),
-                ):
-                    if when == at:
-                        action()
-
-    rows = qkv_ref.shape[4]
-    images = [(0, LEN_L, block)] + [(at, LEN_S, LEN_S) for at in range(LEN_L, rows, LEN_S)]
-    for start, count, size in images:
-        every = slice(start, start + count)
-        keys = qkv_ref[0, 1, 0, :, every]
-        values = qkv_ref[0, 2, 0, :, every]
-        ones = jnp.ones((1, count), F32)
-        key_rows = jnp.concatenate(
-            [keys, keys, extra_rows([ones, ones, ones, mask_ref[:, every]], count)], 0
+
+    def partner_copy(self):
+        return send_to(
+            self.from_core, self.seen, self.send.at[1], self.recv.at[1], self.place.partner()
         )
-        value_rows = jnp.concatenate([values, extra_rows([ones, ones, ones], count)], 0)
-        grad_values = grad_keys = None
-        for at in range(start, start + count, size):
-            here = slice(at, at + size)
-            query = qkv_ref[0, 0, 0, :, here]
-            grads = grad_ref[0, 0, :, here]
-            inner = jnp.sum(
-                grads.astype(F32) * out_ref[0, 0, :, here].astype(F32), axis=0, keepdims=True
-            )
-            terms = three_terms(-log_ref[0, 0, :, here]) + [jnp.ones((1, size), F32)]
-            query_rows = jnp.concatenate([*scaled_query(query), extra_rows(terms, size)], 0)
-            grad_rows = jnp.concatenate([grads, extra_rows(three_terms(-inner), size)], 0)
-            score = contract(query_rows, key_rows, 0, 0)
-            grad_probs = contract(grad_rows, value_rows, 0, 0)
-            probs = jnp.exp2(score)
-            grad_score = (probs * grad_probs).astype(BF16)
-            part_values = contract(grads, probs.astype(BF16), 1, 0)
-            part_keys = contract(query, grad_score, 1, 0)
-            grad_values = part_values if grad_values is None else grad_values + part_values
-            grad_keys = part_keys if grad_keys is None else grad_keys + part_keys
-            dqkv_ref[0, 0, 0, :, here] = (contract(keys, grad_score, 1, 1) * SCALE).astype(BF16)
-        dqkv_ref[0, 1, 0, :, every] = (grad_keys * SCALE).astype(BF16)
-        dqkv_ref[0, 2, 0, :, every] = grad_values.astype(BF16)
-
-    @pl.when(step == pl.num_programs(0) - 1)
-    def _():
-        for one in plane:
-            one.back_to_core()
-        for one in plane:
-            one.end()
-
-
-def attend_backward(mask, qkv, out, log_total, grads, terms, block=256):
-    _, _, heads, _, rows = qkv.shape
-    pairs = pair_count(2 * heads, rows)
-    anywhere = pl.BlockSpec(memory_space=pl.ANY)
-    all_three = pl.BlockSpec((1, 3, 1, HEAD_DIM, rows), lambda h: (h // heads, 0, h % heads, 0, 0))
-    one = pl.BlockSpec((1, 1, HEAD_DIM, rows), lambda h: (h // heads, h % heads, 0, 0))
-    row = pl.BlockSpec((1, 1, 1, rows), lambda h: (h // heads, h % heads, 0, 0))
-    shapes = [own.shape for own, _ in terms]
-    return pl.pallas_call(
-        functools.partial(attend_backward_kernel, block=block, sums=len(terms)),
-        grid=(2 * heads,),
-        in_specs=[whole((1, rows)), all_three, one, row, one] + [anywhere] * (2 * len(terms)),
-        out_specs=[all_three] + [anywhere] * len(terms),
-        out_shape=[jax.ShapeDtypeStruct(qkv.shape, BF16)]
-        + [jax.ShapeDtypeStruct(shape, BF16) for shape in shapes],
-        scratch_shapes=[ref for shape in shapes for ref in PlaneSum.buffers(shape)],
-        compiler_params=pltpu.CompilerParams(
-            vmem_limit_bytes=VMEM_LIMIT, collective_id=0, has_side_effects=True
-        ),
-        cost_estimate=cost(pairs * 5 * 512, 32 * heads * HEAD_DIM * rows, pairs),
-        name="attend_backward",
-    )(mask, qkv, out, log_total, grads, *(array for pair in terms for array in pair))
+
+    def begin(self):
+        self.core_copy().start()
+
+    def to_partner(self):
+        self.core_copy().wait()
+        mine = part(self.other, self.place.core * self.half, self.half)
+        add_rows(self.from_core, 0, self.half, [mine])
+        self.partner_copy().start()
+
+    def end(self):
+        self.partner_copy().wait()
+
+
+class SmallSum:
+    ROWS = 16
+
+    def __init__(self, place, own, other, refs):
+        self.place, self.own, self.other = place, own, other
+        self.sums, self.got, self.send, self.recv = refs
+
+    @staticmethod
+    def buffers(width):
+        rows = SmallSum.ROWS
+        return [
+            pltpu.VMEM((3, rows, width), F32),
+            pltpu.VMEM((6, rows, width), F32),
+            pltpu.SemaphoreType.DMA((6,)),
+            pltpu.SemaphoreType.DMA((6,)),
+        ]
+
+    def copy(self, source, place, device):
+        return send_to(source, self.got.at[place], self.send.at[place], self.recv.at[place], device)
+
+    def partner_copy(self):
+        return self.copy(self.other, 0, self.place.partner())
+
+    def core_copy(self):
+        return self.copy(self.sums.at[0], 1, self.place.across_core())
+
+    def x_copy(self):
+        return self.copy(self.sums.at[1], 2, self.place.across_x())
+
+    def z_copies(self):
+        return [
+            self.copy(self.sums.at[2], 2 + step, self.place.along_z(step)) for step in (1, 2, 3)
+        ]
+
+    def begin(self):
+        self.partner_copy().start()
+
+    def over_cores(self):
+        self.partner_copy().wait()
+        self.sums[0] = self.own[...] + self.got[0]
+        self.core_copy().start()
+
+    def over_x(self):
+        self.core_copy().wait()
+        self.sums[1] = self.sums[0] + self.got[1]
+        self.x_copy().start()
+
+    def over_z(self):
+        self.x_copy().wait()
+        self.sums[2] = self.sums[1] + self.got[2]
+        for copy in self.z_copies():
+            copy.start()
+
+    def end(self):
+        for copy in self.z_copies():
+            copy.wait()
+        return self.sums[2] + self.got[3] + self.got[4] + self.got[5]
 
 
 def middle_kernel(
@@ -674,90 +676,319 @@
     )(resid, *sums, *gmids, grads, gain, b_down, w_out, attended)
 
 
-def back_kernel(
-    tok_ref, x_ref, d_ref, w_ref, w2_ref, gresid_ref, gain_ref,
-    gtok_ref, dw_ref, dw2_ref, db_ref, small_ref, acc_ref,
+TAIL_BLOCK = 512
+SUM_ACTIONS = ("begin", "along_x", "along_z", "back_along_z", "back_along_x", "back_to_core")
+SUM_STEPS = (
+    (0, 1, 3, 7, 9, 11),
+    (0, 3, 5, 11, 13, 15),
+    (0, 5, 9, 15, 17, 19),
+    (0, 7, 13, 17, 20, 99),
+    (0, 4, 6, 8, 10, 13),
+    (17, 18, 20, 99, 99, 99),
+)
+LAST = 99
+
+
+def tail_kernel(
+    mask_ref, qkv_ref, att_ref, log_ref, gatt_ref, gain_ref, small2_ref, dbup1_ref, dbup2_ref,
+    wout2_ref, x_hbm, w_hbm, w2_hbm, tok_hbm, gresid_hbm, up_hbm, down_hbm, wout_hbm, seen_up,
+    seen_down, out_hbm,
+    gtok_ref, small_ref, got_hbm, gup_hbm, gdown_hbm, gout_hbm, gcat_hbm, got_out,
+    d_ref, x_ref, w_ref, tok_ref, gresid_ref, dw_ref, dw2_ref, sent_ref, own_small, other_small,
+    load_sem, row_sem, tok_send, tok_recv, *scratch, heads, block,
 ):
-    @pl.when(pl.program_id(0) == 0)
+    step = pl.program_id(0)
+    place = Place()
+    first_rows = 2 * heads + 1
+    width = x_ref.shape[1]
+    half = heads * HEAD_DIM
+    halves = width
+
+    groups = []
+    at = 0
+    for count in [8] * 6 + [3, 3, 4]:
+        groups.append(scratch[at : at + count])
+        at += count
+    columns = lambda ref, i: ref.at[:, pl.ds(i * halves, halves)]
+    rows_of = lambda ref, i, count: ref.at[pl.ds(i * count, count)]
+    sums = [
+        PlaneSum(place, columns(up_hbm, i), columns(seen_up, i), columns(gup_hbm, i), groups[i])
+        for i in (0, 1)
+    ]
+    down_rows = down_hbm.shape[0] // 2
+    sums += [
+        PlaneSum(
+            place,
+            rows_of(down_hbm, i, down_rows),
+            rows_of(seen_down, i, down_rows // 2),
+            rows_of(gdown_hbm, i, down_rows),
+            groups[2 + i],
+        )
+        for i in (0, 1)
+    ]
+    sums.append(PlaneSum(place, wout_hbm, None, gout_hbm, groups[4]))
+    sums.append(PlaneSum(place, dw_ref, None, gcat_hbm, groups[5]))
+    cat_term = PartnerTerm(place, dw2_ref, groups[5][1], groups[6])
+    out_term = PartnerTerm(place, wout2_ref, groups[4][1], groups[7])
+    small = SmallSum(place, own_small, other_small, groups[8])
+    theirs = pl.ds(pl.multiple_of((1 - place.rank) * LEN_L, LEN_L), LEN_L)
+    out_copy = send_to(
+        out_hbm.at[theirs], got_out, tok_send.at[2], tok_recv.at[2], place.partner()
+    )
+
+    loads = [
+        pltpu.make_async_copy(x_hbm, x_ref, load_sem.at[0]),
+        pltpu.make_async_copy(w_hbm, w_ref.at[0], load_sem.at[1]),
+        pltpu.make_async_copy(w2_hbm, w_ref.at[1], load_sem.at[2]),
+    ]
+
+    def row_start(i):
+        mine = i // 2
+        return ((1 - mine) * (1 - place.rank) + mine * place.rank) * LEN_L + (i % 2) * TAIL_BLOCK
+
+    def row_loads(i):
+        start = pl.ds(pl.multiple_of(row_start(i), TAIL_BLOCK), TAIL_BLOCK)
+        slot = i % 2
+        return [
+            pltpu.make_async_copy(tok_hbm.at[start], tok_ref.at[slot], row_sem.at[slot, 0]),
+            pltpu.make_async_copy(gresid_hbm.at[start], gresid_ref.at[slot], row_sem.at[slot, 1]),
+        ]
+
+    def token_copy(i):
+        there = pl.ds(i * TAIL_BLOCK, TAIL_BLOCK)
+        return send_to(
+            sent_ref.at[there], got_hbm.at[there], tok_send.at[i], tok_recv.at[i], place.partner()
+        )
+
+    def weight_gradient(source, target):
+        for i in range(3):
+            here = pl.ds(i * half, half)
+            product = contract(x_ref[...], d_ref[source, here, :], 0, 1)
+            target[:, here] = product.astype(BF16)
+
+    def bias_rows(source, target):
+        ones = jnp.ones((16, d_ref.shape[2]), BF16)
+        for i, which in ((0, 0), (1, 2)):
+            row = contract(ones, d_ref[source, pl.ds(which * half, half), :], 1, 1)
+            target[8:9, pl.ds(i * half, half)] = row[:1]
+
+    last_step = first_rows + 3
+    events = {}
+    for one, times in zip(sums, SUM_STEPS):
+        for when, action in zip(times, SUM_ACTIONS):
+            events.setdefault(when, []).append(getattr(one, action))
+    late = events.pop(LAST, [])
+
+    for when in sorted(events):
+
+        @pl.when(step == when)
+        def _(when=when):
+            if when == 0:
+                place.greet()
+                out_term.begin()
+            if when == 1:
+                out_term.to_partner()
+                out_copy.start()
+            if when == 4:
+                out_term.end()
+            for action in events[when]:
+                action()
+
+    @pl.when(step == 2)
     def _():
-        acc_ref[...] = jnp.zeros_like(acc_ref)
-        db_ref[...] = jnp.zeros_like(db_ref)
-        small_ref[...] = jnp.zeros_like(small_ref)
-
-    gin = contract(d_ref[0], w_ref[...], 0, 1) + contract(d_ref[1], w2_ref[...], 0, 1)
-    for half in (0, 1):
-        acc_ref[half] += contract(x_ref[...], d_ref[half], 0, 1)
-        db_ref[half] += jnp.sum(d_ref[half].astype(F32), axis=1, keepdims=True)
-    hat, inv = norm_parts(tok_ref[...].astype(F32))
-    gtok_ref[...] = gresid_ref[...] + norm_back(hat, inv, gin * gain_ref[...])
-    small_ref[0:1] += jnp.sum(gin * hat, axis=0, keepdims=True)
-    small_ref[1:2] += jnp.sum(gin, axis=0, keepdims=True)
-
-    @pl.when(pl.program_id(0) == pl.num_programs(0) - 1)
+        for copy in loads:
+            copy.start()
+
+    @pl.when(step == heads)
     def _():
-        dw_ref[...] = acc_ref[0].astype(BF16)
-        dw2_ref[...] = acc_ref[1].astype(BF16)
-
-
-def back(tokens, normed, dqkv, w_cat, w_cat2, gresid, gain, block):
-    rows, width = normed.shape
-    out = w_cat.shape[1]
-    by_row = pl.BlockSpec((block, width), lambda i: (i, 0))
+        for copy in loads:
+            copy.wait()
+        weight_gradient(1, dw2_ref)
+        cat_term.begin()
+
+    @pl.when(step == heads + 1)
+    def _():
+        cat_term.to_partner()
+        own_small[...] = jnp.zeros_like(own_small)
+        other_small[...] = jnp.zeros_like(other_small)
+        bias_rows(1, other_small)
+
+    @pl.when(step < 2 * heads)
+    def _():
+        back_one_head(mask_ref, qkv_ref, att_ref, log_ref, gatt_ref, d_ref, step, heads, block)
+
+    @pl.when(step == 2 * heads)
+    def _():
+        for copy in row_loads(0):
+            copy.start()
+        cat_term.end()
+        weight_gradient(0, dw_ref)
+        bias_rows(0, own_small)
+
+    for i in range(4):
+
+        @pl.when(step == first_rows + i)
+        def _(i=i):
+            for copy in row_loads(i):
+                copy.wait()
+            if i < 3:
+                for copy in row_loads(i + 1):
+                    copy.start()
+            here = pl.ds(pl.multiple_of(row_start(i), TAIL_BLOCK), TAIL_BLOCK)
+            gin = contract(d_ref[0, :, here], w_ref[0], 0, 1)
+            gin += contract(d_ref[1, :, here], w_ref[1], 0, 1)
+            hat, inv = norm_parts(tok_ref[i % 2].astype(F32))
+            gtok = gresid_ref[i % 2] + norm_back(hat, inv, gin * gain_ref[...])
+            own_small[0:1] += jnp.sum(gin * hat, axis=0, keepdims=True)
+            own_small[1:2] += jnp.sum(gin, axis=0, keepdims=True)
+            if i < 2:
+                sent_ref[pl.ds(i * TAIL_BLOCK, TAIL_BLOCK), :] = gtok.astype(BF16)
+                token_copy(i).start()
+            else:
+                gtok_ref[...] = gtok
+
+    @pl.when(step == last_step)
+    def _():
+        own_small[2:6] = small2_ref[0:4]
+        other_small[0:2] = own_small[0:2]
+        other_small[2:6] = small2_ref[0:4]
+        for i in (0, 1):
+            own_small[6 + i : 7 + i] = dbup1_ref[:, pl.ds(i * width, width)]
+            other_small[6 + i : 7 + i] = dbup2_ref[:, pl.ds(i * width, width)]
+        small.begin()
+        late_steps = iter(late)
+        small.over_cores()
+        small.over_x()
+        small.over_z()
+        for action in late_steps:
+            action()
+        small_ref[...] = small.end()
+        out_copy.wait()
+        for i in (0, 1):
+            token_copy(i).wait()
+        for one in sums:
+            one.end()
+
+
+def back_one_head(mask_ref, qkv_ref, att_ref, log_ref, gatt_ref, d_ref, step, heads, block):
+    rows = qkv_ref.shape[4]
+    half = heads * HEAD_DIM
+    source = 1 - step // heads
+    head_at = pl.multiple_of((step % heads) * HEAD_DIM, HEAD_DIM)
+
+    def store(which, columns, value):
+        d_ref[source, pl.ds(which * half + head_at, HEAD_DIM), columns] = value.astype(BF16)
+
+    images = [(0, LEN_L, block)] + [(at, LEN_S, LEN_S) for at in range(LEN_L, rows, LEN_S)]
+    for start, count, size in images:
+        every = slice(start, start + count)
+        keys = qkv_ref[0, 1, 0, :, every]
+        values = qkv_ref[0, 2, 0, :, every]
+        ones = jnp.ones((1, count), F32)
+        key_rows = jnp.concatenate(
+            [keys, keys, extra_rows([ones, ones, ones, mask_ref[:, every]], count)], 0
+        )
+        value_rows = jnp.concatenate([values, extra_rows([ones, ones, ones], count)], 0)
+        grad_values = grad_keys = None
+        for at in range(start, start + count, size):
+            here = slice(at, at + size)
+            query = qkv_ref[0, 0, 0, :, here]
+            grads = gatt_ref[0, 0, :, here]
+            inner = jnp.sum(
+                grads.astype(F32) * att_ref[0, 0, :, here].astype(F32), axis=0, keepdims=True
+            )
+            terms = three_terms(-log_ref[0, 0, :, here]) + [jnp.ones((1, size), F32)]
+            query_rows = jnp.concatenate([*scaled_query(query), extra_rows(terms, size)], 0)
+            grad_rows = jnp.concatenate([grads, extra_rows(three_terms(-inner), size)], 0)
+            score = contract(query_rows, key_rows, 0, 0)
+            grad_probs = contract(grad_rows, value_rows, 0, 0)
+            probs = jnp.exp2(score)
+            grad_score = (probs * grad_probs).astype(BF16)
+            part_values = contract(grads, probs.astype(BF16), 1, 0)
+            part_keys = contract(query, grad_score, 1, 0)
+            grad_values = part_values if grad_values is None else grad_values + part_values
+            grad_keys = part_keys if grad_keys is None else grad_keys + part_keys
+            store(0, here, contract(keys, grad_score, 1, 1) * SCALE)
+        store(1, every, grad_keys * SCALE)
+        store(2, every, grad_values)
+
+
+def tail(
+    mask, qkv, att, log_total, gatt, gain, small2, dbup1, dbup2, dwout2, normed, w_cat, w_cat2,
+    tokens, gresid, dup, ddown, dwout, seen_up, seen_down, out_rows, block=256,
+):
+    _, _, heads, _, rows = qkv.shape
+    width, out = w_cat.shape
+    anywhere = pl.BlockSpec(memory_space=pl.ANY)
+    last = 2 * heads - 1
+
+    def head(h):
+        h = jnp.minimum(h, last)
+        return 1 - h // heads, h % heads
+
+    all_three = pl.BlockSpec(
+        (1, 3, 1, HEAD_DIM, rows), lambda h: (head(h)[0], 0, head(h)[1], 0, 0)
+    )
+    one = pl.BlockSpec((1, 1, HEAD_DIM, rows), lambda h: (*head(h), 0, 0))
+    row = pl.BlockSpec((1, 1, 1, rows), lambda h: (*head(h), 0, 0))
+    sum_shapes = [(width, width)] * 4 + [dwout.shape, (width, out)]
+    scratch = [
+        pltpu.VMEM((2, out, rows), BF16),
+        pltpu.VMEM((rows, width), BF16),
+        pltpu.VMEM((2, width, out), BF16),
+        pltpu.VMEM((2, TAIL_BLOCK, width), BF16),
+        pltpu.VMEM((2, TAIL_BLOCK, width), F32),
+        pltpu.VMEM((width, out), BF16),
+        pltpu.VMEM((width, out), BF16),
+        pltpu.VMEM((rows // 2, width), BF16),
+        pltpu.VMEM((SmallSum.ROWS, width), F32),
+        pltpu.VMEM((SmallSum.ROWS, width), F32),
+        pltpu.SemaphoreType.DMA((3,)),
+        pltpu.SemaphoreType.DMA((2, 2)),
+        pltpu.SemaphoreType.DMA((3,)),
+        pltpu.SemaphoreType.DMA((3,)),
+    ]
+    for shape in sum_shapes:
+        scratch += PlaneSum.buffers(*shape)
+    scratch += PartnerTerm.buffers(width, out) + PartnerTerm.buffers(*dwout.shape)
+    scratch += SmallSum.buffers(width)
+    pairs = pair_count(2 * heads, rows)
+    first_rows = 2 * heads + 1
     return pl.pallas_call(
-        back_kernel,
-        grid=(rows // block,),
+        functools.partial(tail_kernel, heads=heads, block=block),
+        grid=(first_rows + 4,),
         in_specs=[
-            by_row,
-            by_row,
-            pl.BlockSpec((2, out, block), lambda i: (0, 0, i)),
-            whole((width, out)),
-            whole((width, out)),
-            by_row,
-            whole((1, width)),
+            whole((1, rows)), all_three, one, row, one, whole((1, width)), whole((8, width)),
+            whole((1, 2 * width)), whole((1, 2 * width)), whole(dwout.shape),
+        ]
+        + [anywhere] * 11,
+        out_specs=[
+            pl.BlockSpec(
+                (TAIL_BLOCK, width), lambda h: (jnp.maximum(h - first_rows - 2, 0), 0)
+            ),
+            whole((SmallSum.ROWS, width)),
+        ]
+        + [anywhere] * 6,
+        out_shape=[
+            jax.ShapeDtypeStruct((rows // 2, width), F32),
+            jax.ShapeDtypeStruct((SmallSum.ROWS, width), F32),
+            jax.ShapeDtypeStruct((rows // 2, width), BF16),
+            jax.ShapeDtypeStruct(dup.shape, BF16),
+            jax.ShapeDtypeStruct(ddown.shape, BF16),
+            jax.ShapeDtypeStruct(dwout.shape, BF16),
+            jax.ShapeDtypeStruct((width, out), BF16),
+            jax.ShapeDtypeStruct((rows // 2, width), BF16),
         ],
-        out_specs=[
-            by_row,
-            whole((width, out)),
-            whole((width, out)),
-            whole((2, out, 1)),
-            whole((8, width)),
-        ],
-        out_shape=[
-            jax.ShapeDtypeStruct((rows, width), F32),
-            jax.ShapeDtypeStruct((width, out), BF16),
-            jax.ShapeDtypeStruct((width, out), BF16),
-            jax.ShapeDtypeStruct((2, out, 1), F32),
-            jax.ShapeDtypeStruct((8, width), F32),
-        ],
-        scratch_shapes=[pltpu.VMEM((2, width, out), F32)],
-        compiler_params=params(),
-        cost_estimate=cost(8 * rows * width * out, 16 * rows * width),
-        name="back",
-    )(tokens, normed, dqkv, w_cat, w_cat2, gresid, gain)
-
-
-def sum_kernel(*refs):
-    greet_plane()
-    one = PlaneSum(refs)
-    for action in (one.begin, one.along_x, one.along_z, one.back_along_z, one.back_along_x):
-        action()
-    one.back_to_core()
-    one.end()
-
-
-def plane_sum(own, seen):
-    anywhere = pl.BlockSpec(memory_space=pl.ANY)
-    return pl.pallas_call(
-        sum_kernel,
-        in_specs=[anywhere, anywhere],
-        out_specs=anywhere,
-        out_shape=jax.ShapeDtypeStruct(own.shape, BF16),
-        scratch_shapes=PlaneSum.buffers(own.shape),
+        scratch_shapes=scratch,
         compiler_params=pltpu.CompilerParams(
-            vmem_limit_bytes=VMEM_LIMIT, collective_id=1, has_side_effects=True
+            vmem_limit_bytes=VMEM_LIMIT, collective_id=0, has_side_effects=True
         ),
-        name="plane_sum",
-    )(own, seen)
+        cost_estimate=cost(pairs * 5 * 512, 32 * heads * HEAD_DIM * rows, pairs),
+        name="tail",
+    )(
+        mask, qkv, att, log_total, gatt, gain, small2, dbup1, dbup2, dwout2, normed, w_cat, w_cat2,
+        tokens, gresid, dup, ddown, dwout, seen_up, seen_down, out_rows,
+    )
 
 
 def swap_tp(array):
@@ -796,10 +1027,13 @@
     return (left.astype(F32) + right.astype(F32)).astype(BF16)
 
 
-def partner_term(other):
+def over_cores(other, chunks=1):
     second = dp_bit(1)
-    both = add_low(half_of(other, second), swap_dp(half_of(other, ~second), 1))
-    return swap_tp(both)
+    split = other.reshape(chunks, other.shape[0] // chunks, other.shape[1])
+    half = split.shape[1] // 2
+    take = lambda which: lax.dynamic_slice_in_dim(split, jnp.where(which, half, 0), half, 1)
+    both = add_low(take(second), swap_dp(take(~second), 1))
+    return both.reshape(-1, other.shape[1])
 
 
 def by_images(
@@ -856,48 +1090,37 @@
         own_tokens, attended, w_out_all, row(b_out), row(ln2_gain), row(ln2_bias), 512
     )
     sum2, gmid2, dup2, ddown2, dbup2 = feed(mid, grads, w_up2, row(bias2[2 * half :]), w_down2)
-    seen_up, seen_down = partner_term(dup2), partner_term(ddown2)
+    mid, both_up, both_down = lax.optimization_barrier((mid, over_cores(dup2), over_cores(ddown2, 2)))
+    seen_up, seen_down = swap_tp(both_up), swap_tp(both_down)
     sum1, gmid1, dup1, ddown1, dbup1 = feed(mid, grads, w_up, row(bias[2 * half :]), w_down)
     out, gresid, gatt, dwout1, dwout2, small2 = branch(
         resid, (sum1, sum2), (gmid1, gmid2), grads, row(ln2_gain), row(b_down), w_out_all,
         attended, 512,
     )
-    dqkv, grad_up, grad_down, grad_out_t = attend_backward(
-        mask, qkv, att, log_total, gatt.reshape(2, heads, HEAD_DIM, rows),
-        ((dup1, seen_up), (ddown1, seen_down), (dwout1, partner_term(dwout2))),
-    )
-    result = joined(half_of(out, second), swap_tp(half_of(out, ~second)), second)
-    gtok, dw_cat, dw_cat2, db, small1 = back(
-        own_tokens, normed, dqkv.reshape(2, 3 * half, rows), w_cat, w_cat2, gresid,
-        row(ln1_gain), 512,
-    )
-    grad_cat = plane_sum(dw_cat, partner_term(dw_cat2)).astype(F32)
-    sent = swap_tp(half_of(gtok, ~second).astype(BF16)).astype(F32)
-    grad_tokens = joined(half_of(gtok, second), sent, second)
-
-    one = jnp.concatenate([db[0, :half, 0], db[0, 2 * half :, 0], dbup1[0]])
-    two = jnp.concatenate([db[1, :half, 0], db[1, 2 * half :, 0], dbup2[0]])
-    ordered = joined(one, two, second)
-    packed = jnp.concatenate([small1[0], small1[1], *(small2[i] for i in range(4)), ordered])
-    packed = lax.psum(packed, ("dp", "tp"))
-    small = packed[: 6 * width].reshape(6, width)
-    mine = half_of(packed[6 * width :], second)
+    gtok, small, got_tok, grad_up, grad_down, grad_out_t, grad_cat, got_out = tail(
+        mask, qkv, att, log_total, gatt.reshape(2, heads, HEAD_DIM, rows), row(ln1_gain), small2,
+        dbup1, dbup2, dwout2, normed, w_cat, w_cat2, own_tokens, gresid, dup1, ddown1, dwout1,
+        seen_up, seen_down, out,
+    )
+    result = joined(half_of(out, second), got_out, second)
+    grad_tokens = joined(gtok, got_tok.astype(F32), second)
+    grad_cat = grad_cat.astype(F32)
     return (
         result,
         grad_tokens,
         small[0],
         small[1],
         grad_cat[:, :half],
-        mine[:half],
+        small[8, :half],
         grad_cat[:, half : 2 * half],
         grad_cat[:, 2 * half :],
-        mine[half : 2 * half],
+        small[8, half:],
         grad_out_t.T.astype(F32),
         small[4],
         small[2],
         small[3],
         grad_up.astype(F32),
-        mine[2 * half :],
+        small[6:8].reshape(-1),
         grad_down.astype(F32),
         small[5],
     )

time: 656 us -> 451 us (0.69)
  the two profiles are of different devices: /device:TPU:0 before, /device:TPU:27 now
where the time goes in v1:
time: 451 us; the launch traced here: 442 us
  Pallas kernels  326 us (72%)
  waiting for transfers between devices  35.2 us (8%)
  other arithmetic  32.4 us (7%)
  local copies, waits for them, and re-layouts  32.1 us (7%)
  starting transfers between devices  15.2 us (3%)
    pallas_call x1, Pallas kernels, tail(): pl.pallas_call(functools.partial(tail_kernel, heads=heads, block=block),...  155 us
    pallas_call x2, Pallas kernels, feed(): pl.pallas_call(functools.partial(feed_kernel, chunk=chunk), grid=(hidden...  88.6 us
    pallas_call x2, Pallas kernels, attend_forward(): pl.pallas_call(functools.partial(attend_forward_kernel, block=block), gri...  33.6 us
    ppermute x10, waiting for transfers between devices, swap_dp(): return lax.ppermute(array, 'dp', [(i, i ^ bit) for i in range(count)])  22.8 us
    pallas_call x1, Pallas kernels, branch(): pl.pallas_call(branch_kernel, grid=(rows // block,), in_specs=[by_row] *...  22 us
    select_n x11, other arithmetic, joined(): jnp.where(second, jnp.concatenate([theirs, mine], 0), jnp.concatenate([mi...  20.3 us
    ppermute x8, waiting for transfers between devices, swap_tp(): return lax.ppermute(array, 'tp', [(0, 1), (1, 0)])  12.4 us
    dynamic_slice x6, local copies, waits for them, and re-layouts, half_of(): return lax.dynamic_slice_in_dim(array, jnp.where(second, size, 0), size, 0)  10.7 us
  transfers between devices with their start and end apart: 18, of which 6 were waited for; matrix products, arithmetic and copies ran while one was open for 8% of the time, Pallas kernels for 29%

profile of v1, /device:TPU:27, one launch (start us, length us, event | category | flops | bytes accessed | tf_op | source)
XLA Modules:
  0.0 442.0 jit_solution(13435272458481727122)
XLA Ops:
  4.0 2.1 constant_dynamic-slice_fusion.3
  15.3 3.3 constant_dynamic-slice_fusion.5
  22.8 2.4 collective-permute-start.5
  25.1 9.6 %project_norm.1 = (bf16[2048,768]{1,0:T(8,128)(2,1)}, bf16[2048,768]{1,0:T(8,128)(2,1)}, bf16[2,1152,2048]{2,1,0:T(8,128)(2,1)}) custom-call(s32[1]{0:T(128)} %bitcast.1.rank_ref, bf16[4096,768]{1,0:T(8,128)(2,1)} %tok_ref.1, f32[1,768]{1,0:T(1,128)} %reshape.175.gain_ref, f32[1,768]{1,0:T(1,128)} %reshape.177.shift_ref, bf16[768,1152]{1,0:T(8,128)(2,1)} %copy-done.8, ...), custom_call_target="tpu_custom_call" | custom-call | flops 3623878656 | bytes 11010048 | tf_op jit(solution)/shard_map/project_norm/pallas_call | solution.py:79
  35.1 8.3 %collective-permute-done = bf16[192,1152]{1,0:T(8,128)(2,1)} collective-permute-done((bf16[192,1152]{1,0:T(8,128)(2,1)}, bf16[192,1152]{1,0:T(8,128)(2,1)}, u32[]{:S(2)}, u32[]{:S(2)}) %collective-permute-start) | collective-permute-done | bytes 442400 | tf_op jit(solution)/shard_map/ppermute | solution.py:995
  43.4 2.7 collective-permute-start.1
  46.1 16.7 %attend_forward.2 = (bf16[2,8,48,2048]{3,2,1,0:T(8,128)(2,1)}, f32[2,8,1,2048]{3,2,1,0:T(1,128)}) custom-call(f32[1,2048]{1,0:T(1,128)} %add_select_fusion.mask_ref, bf16[2,3,8,48,2048]{4,3,2,1,0:T(8,128)(2,1)} %bitcast.21), custom_call_target="tpu_custom_call" | custom-call | flops 10737418240 | bytes 6291456 | tf_op jit(solution)/shard_map/attend_forward/pallas_call | solution.py:190
  72.9 4.1 collective-permute-done.7
  77.0 2.1 maximum_select_fusion.1.grad_ref
  79.1 8.5 %collective-permute-done.2 = bf16[384,1152]{1,0:T(8,128)(2,1)S(1)} collective-permute-done((bf16[384,1152]{1,0:T(8,128)(2,1)S(1)}, bf16[384,1152]{1,0:T(8,128)(2,1)S(1)}, u32[]{:S(2)}, u32[]{:S(2)}) %collective-permute-start.2) | collective-permute-done | bytes 884768 | tf_op jit(solution)/shard_map/ppermute | solution.py:1000
  89.5 8.0 %project.1 = bf16[2,1152,2048]{2,1,0:T(8,128)(2,1)} custom-call(bf16[2,1152,2048]{2,1,0:T(8,128)(2,1)} %get-tuple-element.53._, bf16[2048,768]{1,0:T(8,128)(2,1)} %get-tuple-element.54.x_ref.x_hbm, bf16[768,1152]{1,0:T(8,128)(2,1)} %maximum_select_fusion.5.w_ref.w2_hbm, f32[1152,1]{1,0:T(8,128)} %reshape.188.b_ref), custom_call_target="tpu_custom_call", output_to_operand_aliasing={{}: (0, {})} | custom-call | flops 3623878656 | bytes 7864320 | tf_op jit(solution)/shard_map/project/pallas_call | solution.py:107
  97.5 16.9 %attend_forward.3 = (bf16[2,8,48,2048]{3,2,1,0:T(8,128)(2,1)}, f32[2,8,1,2048]{3,2,1,0:T(1,128)}) custom-call(f32[1,2048]{1,0:T(1,128)} %add_select_fusion.mask_ref, bf16[2,3,8,48,2048]{4,3,2,1,0:T(8,128)(2,1)} %bitcast.22, bf16[2,8,48,2048]{3,2,1,0:T(8,128)(2,1)} %get-tuple-element.55.refs_0_, ...), custom_call_target="tpu_custom_call", output_to_operand_aliasing={{0}: (2, {}), {1}: (3, {})} | custom-call | flops 10737418240 | bytes 6291456 | tf_op jit(solution)/shard_map/attend_forward/pallas_call | solution.py:190
  114.5 8.6 %middle.1 = (f32[2048,768]{1,0:T(8,128)}, bf16[2048,768]{1,0:T(8,128)(2,1)}) custom-call(bf16[2048,768]{1,0:T(8,128)(2,1)} %get-tuple-element.59.tok_ref.tok_hbm, bf16[768,2048]{1,0:T(8,128)(2,1)} %bitcast.24, bf16[768,768]{1,0:T(8,128)(2,1)} %pad_maximum_fusion.w_ref, f32[1,768]{1,0:T(1,128)} %reshape.179.b_ref, f32[1,768]{1,0:T(1,128)} %reshape.181.gain_ref, ...), custom_call_target="tpu_custom_call" | custom-call | flops 2415919104 | bytes 18874368 | tf_op jit(solution)/shard_map/middle/pallas_call | solution.py:510
  123.1 3.1 maximum_select_fusion.4.down_ref
  126.2 12.1 %collective-permute-done.10 = bf16[384,1536]{1,0:T(8,128)(2,1)} collective-permute-done((bf16[384,1536]{1,0:T(8,128)(2,1)S(1)}, bf16[384,1536]{1,0:T(8,128)(2,1)}, u32[]{:S(2)}, u32[]{:S(2)}) %collective-permute-start.10) | collective-permute-done | bytes 1179680 | tf_op jit(solution)/shard_map/ppermute | solution.py:1000
  138.3 3.0 maximum_select_fusion.3.up_ref
  141.3 40.2 %feed.2 = (f32[2048,768]{1,0:T(8,128)}, f32[2048,768]{1,0:T(8,128)}, bf16[768,1536]{1,0:T(8,128)(2,1)}, bf16[1536,768]{1,0:T(8,128)(2,1)}, f32[1,1536]{1,0:T(1,128)}) custom-call(bf16[2048,768]{1,0:T(8,128)(2,1)} %get-tuple-element.64.mid_ref, bf16[2048,768]{1,0:T(8,128)(2,1)} %maximum_select_fusion.1.grad_ref, ...), custom_call_target="tpu_custom_call" | custom-call | flops 28991029248 | bytes 31457280 | tf_op jit(solution)/shard_map/feed/pallas_call | solution.py:590
  190.0 48.3 %feed.3 = (f32[2048,768]{1,0:T(8,128)}, f32[2048,768]{1,0:T(8,128)}, bf16[768,1536]{1,0:T(8,128)(2,1)}, bf16[1536,768]{1,0:T(8,128)(2,1)}, f32[1,1536]{1,0:T(1,128)}) custom-call(bf16[2048,768]{1,0:T(8,128)(2,1)} %get-tuple-element.64.mid_ref, bf16[2048,768]{1,0:T(8,128)(2,1)} %maximum_select_fusion.1.grad_ref, bf16[768,1536]{1,0:T(8,128)(2,1)} %up_ref.1, ...), custom_call_target="tpu_custom_call" | custom-call | flops 28991029248 | bytes 31457280 | tf_op jit(solution)/shard_map/feed/pallas_call | solution.py:590
  238.3 22.0 %branch.1 = (bf16[2048,768]{1,0:T(8,128)(2,1)}, f32[2048,768]{1,0:T(8,128)}, bf16[768,2048]{1,0:T(8,128)(2,1)}, bf16[768,384]{1,0:T(8,128)(2,1)}, bf16[768,384]{1,0:T(8,128)(2,1)}, /*index=5*/f32[8,768]{1,0:T(8,128)}) custom-call(f32[2048,768]{1,0:T(8,128)} %get-tuple-element.60.resid_ref, f32[2048,768]{1,0:T(8,128)} %get-tuple-element.65.sum1_ref, ...), custom_call_target="tpu_custom_call" | custom-call | flops 4831838208 | bytes 50331648 | tf_op jit(solution)/shard_map/branch/pallas_call | solution.py:658
  262.8 155.5 %tail.1 = (f32[1024,768]{1,0:T(8,128)}, f32[16,768]{1,0:T(8,128)}, bf16[1024,768]{1,0:T(8,128)(2,1)}, bf16[768,1536]{1,0:T(8,128)(2,1)}, bf16[1536,768]{1,0:T(8,...) custom-call(f32[1,2048]{1,0:T(1,128)} %add_select_fusion.mask_ref, ...), custom_call_target="tpu_custom_call" | custom-call | flops 53687091200 | bytes 25165824 | tf_op jit(solution)/shard_map/tail/pallas_call | solution.py:957
  430.2 2.8 convert_element_type.62
  433.0 2.5 convert_element_type.63
  435.5 2.1 maximum_select_fusion.2
  438.6 3.1 maximum_select_fusion
  (122 shorter events, 52.7 us)
Async XLA Ops:
  0.7 8.9 %copy-start.9 = (bf16[768,384]{1,0:T(8,128)(2,1)S(1)}, bf16[768,384]{1,0:T(8,128)(2,1)}, u32[]{:S(2)}) copy-start(bf16[768,384]{1,0:T(8,128)(2,1)} %param.24) | copy-start | bytes 1769476
  0.7 9.0 %copy-start.10 = (bf16[768,384]{1,0:T(8,128)(2,1)S(1)}, bf16[768,384]{1,0:T(8,128)(2,1)}, u32[]{:S(2)}) copy-start(bf16[768,384]{1,0:T(8,128)(2,1)} %param.26) | copy-start | bytes 1769476
  1.5 20.0 %collective-permute-start.3 = (f32[2304]{0:T(1024)S(1)}, f32[2304]{0:T(1024)S(1)}, u32[]{:S(2)}, u32[]{:S(2)}) collective-permute-start(f32[2304]{0:T(1024)S(1)} %maximum_convert_fusion), channel_id=1, source_target_pairs={{0,1},{1,0},{2,3},{3,2},{4,5},{5,4},{6,7},{7,6},{8,9},{9,8},{10,11... | collective-permute-start | bytes 27656 | tf_op jit(solution)/shard_map/ppermute | solution.py:995
  3.7 19.0 %collective-permute-start.4 = (bf16[96,768]{1,0:T(8,128)(2,1)S(1)}, bf16[96,768]{1,0:T(8,128)(2,1)S(1)}, u32[]{:S(2)}, u32[]{:S(2)}) collective-permute-start(bf16[96,768]{1,0:T(8,128)(2,1)S(1)} %constant_dynamic-slice_fusion.6), channel_id=1, source_target_pairs={{0,1},{1,0},{2,3},{3,2},{4,5},{5,4},{6,7},{7,6},{8,9},{9,8},{10,11... | collective-permute-start | bytes 442376 | tf_op jit(solution)/shard_map/ppermute | solution.py:995
  4.0 5.7 %copy-start.11 = (bf16[768,384]{1,0:T(8,128)(2,1)S(1)}, bf16[768,384]{1,0:T(8,128)(2,1)}, u32[]{:S(2)}) copy-start(bf16[768,384]{1,0:T(8,128)(2,1)} %param.27) | copy-start | bytes 1769476
  6.1 58.3 %collective-permute-start.8 = (bf16[192,1536]{1,0:T(8,128)(2,1)}, bf16[192,1536]{1,0:T(8,128)(2,1)}, u32[]{:S(2)}, u32[]{:S(2)}) collective-permute-start(bf16[192,1536]{1,0:T(8,128)(2,1)} %constant_dynamic-slice_fusion.3), channel_id=1, source_target_pairs={{0,1},{1,0},{2,3},{3,2},{4,5},{5,4},{6,7},{7,6},{8,9},{9,8},{10,11... | collective-permute-start | bytes 1769480 | tf_op jit(solution)/shard_map/ppermute | solution.py:995
  9.4 5.1 %copy-start.20 = (s32[8]{0:T(128)S(1)}, s32[8]{0:T(128)}, u32[]{:S(2)}) copy-start(s32[8]{0:T(128)} %param.21) | copy-start | bytes 100
  9.4 36.7 %collective-permute-start.11 = (bf16[384,768]{1,0:T(8,128)(2,1)}, bf16[384,768]{1,0:T(8,128)(2,1)}, u32[]{:S(2)}, u32[]{:S(2)}) collective-permute-start(bf16[384,768]{1,0:T(8,128)(2,1)} %constant_dynamic-slice_fusion.2), channel_id=1, source_target_pairs={{0,1},{1,0},{2,3},{3,2},{4,5},{5,4},{6,7},{7,6},{8,9},{9,8},{10,11... | collective-permute-start | bytes 1769480 | tf_op jit(solution)/shard_map/ppermute | solution.py:995
  12.0 31.4 %collective-permute-start = (bf16[192,1152]{1,0:T(8,128)(2,1)}, bf16[192,1152]{1,0:T(8,128)(2,1)}, u32[]{:S(2)}, u32[]{:S(2)}) collective-permute-start(bf16[192,1152]{1,0:T(8,128)(2,1)} %constant_dynamic-slice_fusion.7), channel_id=1, source_target_pairs={{0,1},{1,0},{2,3},{3,2},{4,5},{5,4},{6,7},{7,6},{8,9},{9,8},{10,11... | collective-permute-start | bytes 1327112 | tf_op jit(solution)/shard_map/ppermute | solution.py:995
  15.3 5.1 %copy-start.15 = (bf16[768]{0:T(1024)(128)(2,1)S(1)}, bf16[768]{0:T(1024)(128)(2,1)}, u32[]{:S(2)}) copy-start(bf16[768]{0:T(1024)(128)(2,1)} %param.30) | copy-start | bytes 4612
  15.3 5.6 %copy-start.16 = (bf16[768]{0:T(1024)(128)(2,1)S(1)}, bf16[768]{0:T(1024)(128)(2,1)}, u32[]{:S(2)}) copy-start(bf16[768]{0:T(1024)(128)(2,1)} %param.32) | copy-start | bytes 4612
  21.5 55.5 %collective-permute-start.7 = (bf16[1024,768]{1,0:T(8,128)(2,1)}, bf16[1024,768]{1,0:T(8,128)(2,1)S(1)}, u32[]{:S(2)}, u32[]{:S(2)}) collective-permute-start(bf16[1024,768]{1,0:T(8,128)(2,1)} %get-tuple-element.131), channel_id=1, source_target_pairs={{0,1},{1,0},{2,3},{3,2},{4,5},{5,4},{6,7},{7,6},{8,9},{9,8},{10,11... | collective-permute-start | bytes 4718600 | tf_op jit(solution)/shard_map/ppermute | solution.py:995
  22.8 12.0 %collective-permute-start.5 = (bf16[96,768]{1,0:T(8,128)(2,1)S(1)}, bf16[96,768]{1,0:T(8,128)(2,1)S(1)}, u32[]{:S(2)}, u32[]{:S(2)}) collective-permute-start(bf16[96,768]{1,0:T(8,128)(2,1)S(1)} %collective-permute-done.4), channel_id=1, source_target_pairs={{0,2},{2,0},{4,6},{6,4},{8,10},{10,8},{12,14},{14,12},{16,18},{18,... | collective-permute-start | bytes 442376 | tf_op jit(solution)/shard_map/ppermute | solution.py:1000
  34.8 31.8 %collective-permute-start.6 = (bf16[192,768]{1,0:T(8,128)(2,1)S(1)}, bf16[192,768]{1,0:T(8,128)(2,1)S(1)}, u32[]{:S(2)}, u32[]{:S(2)}) collective-permute-start(bf16[192,768]{1,0:T(8,128)(2,1)S(1)} %maximum_select_fusion.10), channel_id=1, source_target_pairs={{0,4},{2,6},{4,0},{6,2},{8,12},{10,14},{12,8},{14,10},{16,20},{18,... | collective-permute-start | bytes 884744 | tf_op jit(solution)/shard_map/ppermute | solution.py:1000
  43.4 21.5 %collective-permute-start.1 = (bf16[192,1152]{1,0:T(8,128)(2,1)}, bf16[192,1152]{1,0:T(8,128)(2,1)S(1)}, u32[]{:S(2)}, u32[]{:S(2)}) collective-permute-start(bf16[192,1152]{1,0:T(8,128)(2,1)} %collective-permute-done), channel_id=1, source_target_pairs={{0,2},{2,0},{4,6},{6,4},{8,10},{10,8},{12,14},{14,12},{16,18},{18,... | collective-permute-start | bytes 1327112 | tf_op jit(solution)/shard_map/ppermute | solution.py:1000
  46.1 21.9 %collective-permute-start.12 = (bf16[384,768]{1,0:T(8,128)(2,1)}, bf16[384,768]{1,0:T(8,128)(2,1)S(1)}, u32[]{:S(2)}, u32[]{:S(2)}) collective-permute-start(bf16[384,768]{1,0:T(8,128)(2,1)} %collective-permute-done.11), channel_id=1, source_target_pairs={{0,2},{2,0},{4,6},{6,4},{8,10},{10,8},{12,14},{14,12},{16,18},{18,... | collective-permute-start | bytes 1769480 | tf_op jit(solution)/shard_map/ppermute | solution.py:1000
  64.4 6.4 %collective-permute-start.9 = (bf16[192,1536]{1,0:T(8,128)(2,1)}, bf16[192,1536]{1,0:T(8,128)(2,1)S(1)}, u32[]{:S(2)}, u32[]{:S(2)}) collective-permute-start(bf16[192,1536]{1,0:T(8,128)(2,1)} %collective-permute-done.8), channel_id=1, source_target_pairs={{0,2},{2,0},{4,6},{6,4},{8,10},{10,8},{12,14},{14,12},{16,18},{18,... | collective-permute-start | bytes 1769480 | tf_op jit(solution)/shard_map/ppermute | solution.py:1000
  66.3 21.3 %collective-permute-start.2 = (bf16[384,1152]{1,0:T(8,128)(2,1)S(1)}, bf16[384,1152]{1,0:T(8,128)(2,1)S(1)}, u32[]{:S(2)}, u32[]{:S(2)}) collective-permute-start(bf16[384,1152]{1,0:T(8,128)(2,1)S(1)} %maximum_select_fusion.8), channel_id=1, source_target_pairs={{0,4},{2,6},{4,0},{6,2},{8,12},{10,14},{12,8},{14,10},{16,20},{18,... | collective-permute-start | bytes 2654216 | tf_op jit(solution)/shard_map/ppermute | solution.py:1000
  69.5 53.6 %collective-permute-start.13 = (bf16[768,768]{1,0:T(8,128)(2,1)S(1)}, bf16[768,768]{1,0:T(8,128)(2,1)}, u32[]{:S(2)}, u32[]{:S(2)}) collective-permute-start(bf16[768,768]{1,0:T(8,128)(2,1)S(1)} %maximum_select_fusion.7), channel_id=1, source_target_pairs={{0,4},{2,6},{4,0},{6,2},{8,12},{10,14},{12,8},{14,10},{16,20},{18,... | collective-permute-start | bytes 3538952 | tf_op jit(solution)/shard_map/ppermute | solution.py:1000
  72.6 65.7 %collective-permute-start.10 = (bf16[384,1536]{1,0:T(8,128)(2,1)S(1)}, bf16[384,1536]{1,0:T(8,128)(2,1)}, u32[]{:S(2)}, u32[]{:S(2)}) collective-permute-start(bf16[384,1536]{1,0:T(8,128)(2,1)S(1)} %maximum_select_fusion.6), channel_id=1, source_target_pairs={{0,4},{2,6},{4,0},{6,2},{8,12},{10,14},{12,8},{14,10},{16,20},{18,... | collective-permute-start | bytes 3538952 | tf_op jit(solution)/shard_map/ppermute | solution.py:1000
  183.1 3.3 collective-permute-start.14
  184.0 4.1 collective-permute-start.15
  188.4 73.4 %collective-permute-start.16 = (bf16[384,1536]{1,0:T(8,128)(2,1)S(1)}, bf16[384,1536]{1,0:T(8,128)(2,1)S(1)}, u32[]{:S(2)}, u32[]{:S(2)}) collective-permute-start(bf16[384,1536]{1,0:T(8,128)(2,1)S(1)} %fusion.1), channel_id=1, source_target_pairs={{0,1},{1,0},{2,3},{3,2},{4,5},{5,4},{6,7},{7,6},{8,9},{9,8},{10,11... | collective-permute-start | bytes 3538952 | tf_op jit(solution)/shard_map/ppermute | solution.py:995
  189.7 72.1 %collective-permute-start.17 = (bf16[768,768]{1,0:T(8,128)(2,1)S(1)}, bf16[768,768]{1,0:T(8,128)(2,1)}, u32[]{:S(2)}, u32[]{:S(2)}) collective-permute-start(bf16[768,768]{1,0:T(8,128)(2,1)S(1)} %bitcast.28), channel_id=1, source_target_pairs={{0,1},{1,0},{2,3},{3,2},{4,5},{5,4},{6,7},{7,6},{8,9},{9,8},{10,11... | collective-permute-start | bytes 3538952 | tf_op jit(solution)/shard_map/ppermute | solution.py:995
  (15 other events, 45.3 us)

commit v2 on v1

--- a/solution.py
+++ b/solution.py
@@ -52,76 +52,6 @@
     return inv * (grad_hat - mean_grad - hat * mean_both)
 
 
-def project_norm_kernel(rank_ref, tok_ref, gain_ref, shift_ref, w_ref, b_ref, x_ref, own_ref, qkv_ref):
-    hat, _ = norm_parts(tok_ref[...].astype(F32))
-    normed = (hat * gain_ref[...] + shift_ref[...]).astype(BF16)
-    x_ref[...] = normed
-    own_ref[...] = tok_ref[...]
-    qkv_ref[0] = (contract(w_ref[...], normed, 0, 1) + b_ref[...]).astype(BF16)
-
-
-def project_kernel(_, x_ref, w_ref, b_ref, qkv_ref):
-    qkv_ref[0] = (contract(w_ref[...], x_ref[...], 0, 1) + b_ref[...]).astype(BF16)
-
-
-def own_row_block(per_part):
-    def index(i, rank_ref):
-        part = i // per_part
-        return (part * 2 * per_part + rank_ref[0] * per_part + i % per_part, 0)
-
-    return index
-
-
-def project_norm(rank, tokens, gain, shift, w_cat, b_col, rows, block):
-    width, out = w_cat.shape
-    per_part = LEN_L // block
-    by_row = pl.BlockSpec((block, width), lambda i, _: (i, 0))
-    return pl.pallas_call(
-        project_norm_kernel,
-        grid_spec=pltpu.PrefetchScalarGridSpec(
-            num_scalar_prefetch=1,
-            grid=(rows // block,),
-            in_specs=[
-                pl.BlockSpec((block, width), own_row_block(per_part)),
-                whole((1, width)),
-                whole((1, width)),
-                whole((width, out)),
-                whole((out, 1)),
-            ],
-            out_specs=[by_row, by_row, pl.BlockSpec((1, out, block), lambda i, _: (0, 0, i))],
-        ),
-        out_shape=[
-            jax.ShapeDtypeStruct((rows, width), BF16),
-            jax.ShapeDtypeStruct((rows, width), BF16),
-            jax.ShapeDtypeStruct((2, out, rows), BF16),
-        ],
-        compiler_params=params(),
-        cost_estimate=cost(2 * rows * width * out, 4 * rows * width + 2 * out * rows),
-        name="project_norm",
-    )(rank, tokens, gain, shift, w_cat, b_col)
-
-
-def project(both, normed, w_cat, b_col, block):
-    rows, width = normed.shape
-    out = w_cat.shape[1]
-    return pl.pallas_call(
-        project_kernel,
-        grid=(rows // block,),
-        in_specs=[
-            pl.BlockSpec(memory_space=pl.ANY),
-            pl.BlockSpec((block, width), lambda i: (i, 0)),
-            whole((width, out)),
-            whole((out, 1)),
-        ],
-        out_specs=pl.BlockSpec((1, out, block), lambda i: (1, 0, i)),
-        out_shape=jax.ShapeDtypeStruct(both.shape, BF16),
-        input_output_aliases={0: 0},
-        compiler_params=params(),
-        cost_estimate=cost(2 * rows * width * out, 2 * rows * width + 2 * out * rows),
-        name="project",
-    )(both, normed, w_cat, b_col)
-
-
 def three_terms(value):
     high = value.astype(BF16).astype(F32)
     rest = value - high
@@ -143,71 +73,8 @@
     return [high, (wide - high.astype(F32)).astype(BF16)]
 
 
-def attend_forward_kernel(mask_ref, qkv_ref, *refs, block):
-    out_ref, log_ref = refs[-2:]
-    heads, rows = qkv_ref.shape[2], qkv_ref.shape[4]
-    work = []
-    for head in range(heads):
-        work += [(head, 0, LEN_L, at, block) for at in range(0, LEN_L, block)]
-        work += [(head, start, LEN_S, 0, LEN_S) for start in range(LEN_L, rows, LEN_S)]
-
-    def scores(item):
-        head, start, count, at, size = item
-        every = slice(start, start + count)
-        keys = qkv_ref[0, 1, head, :, every]
-        key_rows = jnp.concatenate([keys, keys, extra_rows([mask_ref[:, every]], count)], 0)
-        query = scaled_query(qkv_ref[0, 0, head, :, start + at : start + at + size])
-        query_rows = jnp.concatenate([*query, jnp.ones((16, size), BF16)], 0)
-        return contract(key_rows, query_rows, 0, 0)
-
-    def finish(item, score):
-        head, start, count, at, size = item
-        here = slice(start + at, start + at + size)
-        values = qkv_ref[0, 2, head, :, start : start + count]
-        value_rows = jnp.concatenate([values, jnp.ones((16, count), BF16)], 0)
-        top = jnp.max(score, axis=0, keepdims=True)
-        weights = jnp.exp2(score - top).astype(BF16)
-        mixed = contract(value_rows, weights, 1, 0)
-        total = mixed[HEAD_DIM : HEAD_DIM + 1]
-        out_ref[0, head, :, here] = (mixed[:HEAD_DIM] * (1.0 / total)).astype(BF16)
-        log_ref[0, head, :, here] = top + jnp.log2(total)
-
-    score = scores(work[0])
-    for place, item in enumerate(work):
-        later = scores(work[place + 1]) if place + 1 < len(work) else None
-        finish(item, score)
-        score = later
-
-
 def pair_count(heads, rows):
     return heads * (LEN_L**2 + (rows - LEN_L) * LEN_S)
-
-
-def attend_forward(mask, qkv, part, earlier=(), block=1024):
-    _, _, heads, _, rows = qkv.shape
-    group = HEAD_GROUP
-    pairs = pair_count(heads, rows)
-    return pl.pallas_call(
-        functools.partial(attend_forward_kernel, block=block),
-        grid=(heads // group,),
-        in_specs=[
-            whole((1, rows)),
-            pl.BlockSpec((1, 3, group, HEAD_DIM, rows), lambda h: (part, 0, h, 0, 0)),
-            *(pl.BlockSpec(memory_space=pl.ANY) for _ in earlier),
-        ],
-        out_specs=[
-            pl.BlockSpec((1, group, HEAD_DIM, rows), lambda h: (part, h, 0, 0)),
-            pl.BlockSpec((1, group, 1, rows), lambda h: (part, h, 0, 0)),
-        ],
-        out_shape=[
-            jax.ShapeDtypeStruct((2, heads, HEAD_DIM, rows), BF16),
-            jax.ShapeDtypeStruct((2, heads, 1, rows), F32),
-        ],
-        input_output_aliases={2: 0, 3: 1} if earlier else {},
-        compiler_params=params(),
-        cost_estimate=cost(pairs * 2 * 512, 8 * heads * HEAD_DIM * rows, pairs),
-        name="attend_forward",
-    )(mask, qkv, *earlier)
 
 
 class Place:
@@ -494,39 +361,358 @@
         return self.sums[2] + self.got[3] + self.got[4] + self.got[5]
 
 
-def middle_kernel(
-    tok_ref, att_ref, w_ref, b_ref, gain_ref, shift_ref, resid_ref, mid_ref
+class Fetch:
+    def __init__(self, place, own, got, refs, deep):
+        self.place, self.own, self.got, self.deep = place, own, got, deep
+        self.send, self.recv = refs
+        self.half = own.shape[0] // 2
+        self.quarter = self.half // 2
+        self.count = self.quarter // 2 if deep else self.quarter
+        self.core_at = place.core * self.half
+        self.x_at = self.core_at + place.x * self.quarter
+        odd = place.z % 2
+        self.at = self.x_at + odd * self.count if deep else self.x_at
+        self.z_at = self.x_at + (1 - odd) * self.count
+        self.z_device = place.at(z=place.z + 1 - 2 * odd)
+
+    @staticmethod
+    def buffers():
+        return [pltpu.SemaphoreType.DMA((5,)), pltpu.SemaphoreType.DMA((5,))]
+
+    def copy(self, source, start, count, place, device):
+        there = part(self.got, start, count)
+        here = part(source, start, count)
+        return send_to(here, there, self.send.at[place], self.recv.at[place], device)
+
+    def partner_copy(self):
+        return self.copy(self.own, self.at, self.count, 0, self.place.partner())
+
+    def z_copy(self):
+        return self.copy(self.got, self.at, self.count, 1, self.z_device)
+
+    def x_copies(self):
+        copies = [self.copy(self.got, self.at, self.count, 2, self.place.across_x())]
+        if self.deep:
+            copies.append(self.copy(self.got, self.z_at, self.count, 3, self.place.across_x()))
+        return copies
+
+    def core_copy(self):
+        return self.copy(self.got, self.core_at, self.half, 4, self.place.across_core())
+
+    def begin(self):
+        self.partner_copy().start()
+
+    def share(self):
+        self.partner_copy().wait()
+        if self.deep:
+            self.z_copy().start()
+        self.x_copies()[0].start()
+
+    def more_x(self):
+        self.z_copy().wait()
+        self.x_copies()[1].start()
+
+    def to_core(self):
+        for copy in self.x_copies():
+            copy.wait()
+        self.core_copy().start()
+
+    def end(self):
+        self.core_copy().wait()
+
+
+FRONT_BLOCK = 512
+
+
+def front_kernel(
+    mask_ref, gain_ref, shift_ref, bout_ref, gain2_ref, shift2_ref, bias_ref,
+    tok_hbm, wq_hbm, wk_hbm, wv_hbm, wout_hbm, wup_hbm, wdown_hbm, cot_hbm,
+    x_out, qkv_out, att_out, log_out, resid_out, mid_out,
+    cat_hbm, wout_all_hbm, up2_hbm, down2_hbm, grads_hbm, bias2_hbm, tok_out,
+    tok_ref, x_ref, qkv_ref, att_ref, cat_ref, wout_ref, bias2_ref, load_sem, out_sem, swap_send,
+    swap_recv, *scratch, heads, block,
 ):
-    resid = tok_ref[...].astype(F32) + contract(att_ref[...], w_ref[...], 0, 0) + b_ref[...]
-    resid_ref[...] = resid
-    hat, _ = norm_parts(resid)
-    mid_ref[...] = (hat * gain_ref[...] + shift_ref[...]).astype(BF16)
-
-
-def middle(tokens, attended, w_out, b_out, gain, shift, block):
-    heads_width, rows = attended.shape
-    width = w_out.shape[1]
-    by_row = pl.BlockSpec((block, width), lambda i: (i, 0))
+    step = pl.program_id(0)
+    place = Place()
+    half = heads * HEAD_DIM
+    rows = tok_ref.shape[0]
+    blocks = rows // FRONT_BLOCK
+    pairs = heads // HEAD_GROUP
+    base = [0, blocks, blocks + pairs, 2 * blocks + pairs, 2 * blocks + 2 * pairs]
+
+    sems = [scratch[2 * i : 2 * i + 2] for i in range(6)]
+    mine = [wq_hbm, wk_hbm, wv_hbm]
+    projections = [
+        Fetch(place, own, cat_ref.at[1, :, pl.ds(i * half, half)], sems[i], False)
+        for i, own in enumerate(mine)
+    ]
+    fetch_out = Fetch(place, wout_hbm, wout_ref.at[pl.ds(half, half)], sems[3], False)
+    fetch_up = Fetch(place, wup_hbm, up2_hbm, sems[4], True)
+    fetch_down = Fetch(place, wdown_hbm, down2_hbm, sems[5], True)
+    bias_copy = send_to(
+        bias_ref, bias2_ref, swap_send.at[0], swap_recv.at[0], place.partner()
+    )
+    here = pl.ds(pl.multiple_of(place.rank * LEN_L, LEN_L), LEN_L)
+    theirs = pl.ds(pl.multiple_of((1 - place.rank) * LEN_L, LEN_L), LEN_L)
+    cot_copy = send_to(
+        cot_hbm.at[theirs], grads_hbm.at[here], swap_send.at[1], swap_recv.at[1], place.partner()
+    )
+
+    def token_rows(i):
+        start = pl.multiple_of(i * 2 * LEN_L + place.rank * LEN_L, LEN_L)
+        return tok_hbm.at[pl.ds(start, LEN_L)]
+
+    token_loads = [
+        pltpu.make_async_copy(token_rows(i), tok_ref.at[pl.ds(i * LEN_L, LEN_L)], load_sem.at[i])
+        for i in (0, 1)
+    ]
+    weight_loads = [
+        pltpu.make_async_copy(
+            own, cat_ref.at[0, :, pl.ds(i * half, half)], load_sem.at[2 + i]
+        )
+        for i, own in enumerate(mine)
+    ]
+    out_load = pltpu.make_async_copy(wout_hbm, wout_ref.at[pl.ds(0, half)], load_sem.at[5])
+    kept_copy = pltpu.make_async_copy(cot_hbm.at[here], grads_hbm.at[here], out_sem.at[0])
+    stores = [
+        pltpu.make_async_copy(cat_ref, cat_hbm, out_sem.at[1]),
+        pltpu.make_async_copy(wout_ref, wout_all_hbm, out_sem.at[2]),
+        pltpu.make_async_copy(bias2_ref, bias2_hbm, out_sem.at[3]),
+        pltpu.make_async_copy(tok_ref, tok_out, out_sem.at[4]),
+    ]
+
+    @pl.when(step == 0)
+    def _():
+        for copy in (*token_loads, *weight_loads, out_load):
+            copy.start()
+        place.greet()
+        for one in projections:
+            one.begin()
+        bias_copy.start()
+        fetch_out.begin()
+        for copy in token_loads:
+            copy.wait()
+        for copy in weight_loads:
+            copy.wait()
+
+    def at_step(when):
+        return pl.when(step == when)
+
+    @at_step(base[1] - 1)
+    def _():
+        fetch_up.begin()
+        fetch_down.begin()
+
+    @at_step(base[1] + 1)
+    def _():
+        for one in (*projections, fetch_out):
+            one.share()
+
+    @at_step(base[2] - 1)
+    def _():
+        for one in (*projections, fetch_out):
+            one.to_core()
+
+    @at_step(base[2])
+    def _():
+        for one in (*projections, fetch_out):
+            one.end()
+        bias_copy.wait()
+        out_load.wait()
+        for copy in stores:
+            copy.start()
+        kept_copy.start()
+        fetch_up.share()
+        fetch_down.share()
+        cot_copy.start()
+
+    @at_step(base[3] + 2)
+    def _():
+        fetch_up.more_x()
+        fetch_down.more_x()
+
+    @at_step(base[4] + 2)
+    def _():
+        fetch_up.to_core()
+        fetch_down.to_core()
+
+    def project(which, i, bias):
+        at = pl.ds(pl.multiple_of(i * FRONT_BLOCK, FRONT_BLOCK), FRONT_BLOCK)
+        column = jnp.transpose(bias[:, : 3 * half])[:, :1]
+        value = (contract(cat_ref[which], x_ref[at, :], 0, 1) + column).astype(BF16)
+        qkv_ref[:, at] = value
+        qkv_out[0] = value
+
+    @pl.when(step < base[1])
+    def _():
+        at = pl.ds(pl.multiple_of(step * FRONT_BLOCK, FRONT_BLOCK), FRONT_BLOCK)
+        hat, _ = norm_parts(tok_ref[at, :].astype(F32))
+        normed = (hat * gain_ref[...] + shift_ref[...]).astype(BF16)
+        x_ref[at, :] = normed
+        x_out[...] = normed
+        project(0, step, bias_ref[...])
+
+    @pl.when(jnp.logical_and(step >= base[2], step < base[3]))
+    def _():
+        project(1, step - base[2], bias2_ref[...])
+
+    own_part = jnp.logical_and(step >= base[1], step < base[2])
+    other_part = jnp.logical_and(step >= base[3], step < base[4])
+
+    @pl.when(jnp.logical_or(own_part, other_part))
+    def _():
+        second = (step >= base[3]).astype(jnp.int32)
+        pair = step - base[1] - second * (base[3] - base[1])
+        attend_pair(mask_ref, qkv_ref, att_ref, att_out, log_out, pair, second, heads, block)
+
+    @pl.when(step >= base[4])
+    def _():
+        i = step - base[4]
+        at = pl.ds(pl.multiple_of(i * FRONT_BLOCK, FRONT_BLOCK), FRONT_BLOCK)
+        product = contract(att_ref[:, at], wout_ref[...], 0, 0)
+        resid = tok_ref[at, :].astype(F32) + product + bout_ref[...]
+        resid_out[...] = resid
+        hat, _ = norm_parts(resid)
+        mid_out[...] = (hat * gain2_ref[...] + shift2_ref[...]).astype(BF16)
+
+    @pl.when(step == base[4] + blocks - 1)
+    def _():
+        for one in (fetch_up, fetch_down):
+            one.end()
+        cot_copy.wait()
+        kept_copy.wait()
+        for copy in stores:
+            copy.wait()
+
+
+def attend_pair(mask_ref, qkv_ref, att_ref, att_out, log_out, pair, second, heads, block):
+    rows = qkv_ref.shape[1]
+    half = heads * HEAD_DIM
+    first = pair * HEAD_GROUP
+    work = []
+    for head in range(HEAD_GROUP):
+        work += [(head, 0, LEN_L, at, block) for at in range(0, LEN_L, block)]
+        work += [(head, start, LEN_S, 0, LEN_S) for start in range(LEN_L, rows, LEN_S)]
+
+    def load(which, head, columns):
+        start = pl.multiple_of(which * half + (first + head) * HEAD_DIM, HEAD_DIM)
+        return qkv_ref[pl.ds(start, HEAD_DIM), columns]
+
+    def scores(item):
+        head, start, count, at, size = item
+        every = slice(start, start + count)
+        keys = load(1, head, every)
+        key_rows = jnp.concatenate([keys, keys, extra_rows([mask_ref[:, every]], count)], 0)
+        query = scaled_query(load(0, head, slice(start + at, start + at + size)))
+        query_rows = jnp.concatenate([*query, jnp.ones((16, size), BF16)], 0)
+        return contract(key_rows, query_rows, 0, 0)
+
+    def finish(item, score):
+        head, start, count, at, size = item
+        here = slice(start + at, start + at + size)
+        values = load(2, head, slice(start, start + count))
+        value_rows = jnp.concatenate([values, jnp.ones((16, count), BF16)], 0)
+        top = jnp.max(score, axis=0, keepdims=True)
+        weights = jnp.exp2(score - top).astype(BF16)
+        mixed = contract(value_rows, weights, 1, 0)
+        total = mixed[HEAD_DIM : HEAD_DIM + 1]
+        result = (mixed[:HEAD_DIM] * (1.0 / total)).astype(BF16)
+        att_out[0, head, :, here] = result
+        start = pl.multiple_of(second * half + (first + head) * HEAD_DIM, HEAD_DIM)
+        att_ref[pl.ds(start, HEAD_DIM), here] = result
+        log_out[0, head, :, here] = top + jnp.log2(total)
+
+    score = scores(work[0])
+    for place, item in enumerate(work):
+        later = scores(work[place + 1]) if place + 1 < len(work) else None
+        finish(item, score)
+        score = later
+
+
+def front(
+    mask, gain, shift, b_out, gain2, shift2, bias, tokens, w_query, w_key, w_value, w_out, w_up,
+    w_down, cotangent, heads, block=1024,
+):
+    width = tokens.shape[1]
+    rows = tokens.shape[0] // 2
+    half = heads * HEAD_DIM
+    hidden = w_up.shape[1]
+    blocks, pairs = rows // FRONT_BLOCK, heads // HEAD_GROUP
+    base = [0, blocks, blocks + pairs, 2 * blocks + pairs, 2 * blocks + 2 * pairs]
+    anywhere = pl.BlockSpec(memory_space=pl.ANY)
+
+    def row_block(first):
+        return lambda s: (jnp.clip(s - first, 0, blocks - 1), 0)
+
+    def qkv_block(s):
+        late = (s >= base[2]).astype(jnp.int32)
+        return late, 0, jnp.clip(s - late * base[2], 0, blocks - 1)
+
+    def head_block(s):
+        late = (s >= base[3]).astype(jnp.int32)
+        return late, jnp.clip(s - base[1] - late * (base[3] - base[1]), 0, pairs - 1), 0, 0
+
+    by_row = lambda first: pl.BlockSpec((FRONT_BLOCK, width), row_block(first))
+    bias_rows, bias_width = bias.shape
+    pair_total = pair_count(2 * heads, rows)
     return pl.pallas_call(
-        middle_kernel,
-        grid=(rows // block,),
+        functools.partial(front_kernel, heads=heads, block=block),
+        grid=(base[4] + blocks,),
         in_specs=[
-            by_row,
-            pl.BlockSpec((heads_width, block), lambda i: (0, i)),
-            whole((heads_width, width)),
-            whole((1, width)),
-            whole((1, width)),
-            whole((1, width)),
-        ],
-        out_specs=[by_row, by_row],
+            whole((1, rows)),
+            *(whole((1, width)) for _ in range(5)),
+            whole(bias.shape),
+        ]
+        + [anywhere] * 8,
+        out_specs=[
+            by_row(0),
+            pl.BlockSpec((1, 3 * half, FRONT_BLOCK), qkv_block),
+            pl.BlockSpec((1, HEAD_GROUP, HEAD_DIM, rows), head_block),
+            pl.BlockSpec((1, HEAD_GROUP, 1, rows), head_block),
+            by_row(base[4]),
+            by_row(base[4]),
+        ]
+        + [anywhere] * 7,
         out_shape=[
+            jax.ShapeDtypeStruct((rows, width), BF16),
+            jax.ShapeDtypeStruct((2, 3 * half, rows), BF16),
+            jax.ShapeDtypeStruct((2, heads, HEAD_DIM, rows), BF16),
+            jax.ShapeDtypeStruct((2, heads, 1, rows), F32),
             jax.ShapeDtypeStruct((rows, width), F32),
             jax.ShapeDtypeStruct((rows, width), BF16),
+            jax.ShapeDtypeStruct((2, width, 3 * half), BF16),
+            jax.ShapeDtypeStruct((2 * half, width), BF16),
+            jax.ShapeDtypeStruct((width, hidden), BF16),
+            jax.ShapeDtypeStruct((hidden, width), BF16),
+            jax.ShapeDtypeStruct((rows, width), BF16),
+            jax.ShapeDtypeStruct((bias_rows, bias_width), F32),
+            jax.ShapeDtypeStruct((rows, width), BF16),
         ],
-        compiler_params=params(),
-        cost_estimate=cost(2 * rows * width * heads_width, 12 * rows * width),
-        name="middle",
-    )(tokens, attended, w_out, b_out, gain, shift)
+        scratch_shapes=[
+            pltpu.VMEM((rows, width), BF16),
+            pltpu.VMEM((rows, width), BF16),
+            pltpu.VMEM((3 * half, rows), BF16),
+            pltpu.VMEM((2 * half, rows), BF16),
+            pltpu.VMEM((2, width, 3 * half), BF16),
+            pltpu.VMEM((2 * half, width), BF16),
+            pltpu.VMEM((bias_rows, bias_width), F32),
+            pltpu.SemaphoreType.DMA((6,)),
+            pltpu.SemaphoreType.DMA((5,)),
+            pltpu.SemaphoreType.DMA((2,)),
+            pltpu.SemaphoreType.DMA((2,)),
+        ]
+        + [ref for _ in range(6) for ref in Fetch.buffers()],
+        compiler_params=pltpu.CompilerParams(
+            vmem_limit_bytes=VMEM_LIMIT, collective_id=1, has_side_effects=True
+        ),
+        cost_estimate=cost(
+            pair_total * 2 * 512 + 14 * rows * width * half, 40 * rows * width, pair_total
+        ),
+        name="front",
+    )(
+        mask, gain, shift, b_out, gain2, shift2, bias, tokens, w_query, w_key, w_value, w_out,
+        w_up, w_down, cotangent,
+    )
 
 
 ERFC_TERMS = (0.254829592, -0.284496736, 1.421413741, -1.453152027, 1.061405429)
@@ -691,7 +877,7 @@
 
 def tail_kernel(
     mask_ref, qkv_ref, att_ref, log_ref, gatt_ref, gain_ref, small2_ref, dbup1_ref, dbup2_ref,
-    wout2_ref, x_hbm, w_hbm, w2_hbm, tok_hbm, gresid_hbm, up_hbm, down_hbm, wout_hbm, seen_up,
+    wout2_ref, x_hbm, w_hbm, tok_hbm, gresid_hbm, up_hbm, down_hbm, wout_hbm, seen_up,
     seen_down, out_hbm,
     gtok_ref, small_ref, got_hbm, gup_hbm, gdown_hbm, gout_hbm, gcat_hbm, got_out,
     d_ref, x_ref, w_ref, tok_ref, gresid_ref, dw_ref, dw2_ref, sent_ref, own_small, other_small,
@@ -738,8 +924,7 @@
 
     loads = [
         pltpu.make_async_copy(x_hbm, x_ref, load_sem.at[0]),
-        pltpu.make_async_copy(w_hbm, w_ref.at[0], load_sem.at[1]),
-        pltpu.make_async_copy(w2_hbm, w_ref.at[1], load_sem.at[2]),
+        pltpu.make_async_copy(w_hbm, w_ref, load_sem.at[1]),
     ]
 
     def row_start(i):
@@ -914,11 +1099,11 @@
 
 
 def tail(
-    mask, qkv, att, log_total, gatt, gain, small2, dbup1, dbup2, dwout2, normed, w_cat, w_cat2,
+    mask, qkv, att, log_total, gatt, gain, small2, dbup1, dbup2, dwout2, normed, w_cat,
     tokens, gresid, dup, ddown, dwout, seen_up, seen_down, out_rows, block=256,
 ):
     _, _, heads, _, rows = qkv.shape
-    width, out = w_cat.shape
+    _, width, out = w_cat.shape
     anywhere = pl.BlockSpec(memory_space=pl.ANY)
     last = 2 * heads - 1
 
@@ -943,7 +1128,7 @@
         pltpu.VMEM((rows // 2, width), BF16),
         pltpu.VMEM((SmallSum.ROWS, width), F32),
         pltpu.VMEM((SmallSum.ROWS, width), F32),
-        pltpu.SemaphoreType.DMA((3,)),
+        pltpu.SemaphoreType.DMA((2,)),
         pltpu.SemaphoreType.DMA((2, 2)),
         pltpu.SemaphoreType.DMA((3,)),
         pltpu.SemaphoreType.DMA((3,)),
@@ -961,7 +1146,7 @@
             whole((1, rows)), all_three, one, row, one, whole((1, width)), whole((8, width)),
             whole((1, 2 * width)), whole((1, 2 * width)), whole(dwout.shape),
         ]
-        + [anywhere] * 11,
+        + [anywhere] * 10,
         out_specs=[
             pl.BlockSpec(
                 (TAIL_BLOCK, width), lambda h: (jnp.maximum(h - first_rows - 2, 0), 0)
@@ -986,7 +1171,7 @@
         cost_estimate=cost(pairs * 5 * 512, 32 * heads * HEAD_DIM * rows, pairs),
         name="tail",
     )(
-        mask, qkv, att, log_total, gatt, gain, small2, dbup1, dbup2, dwout2, normed, w_cat, w_cat2,
+        mask, qkv, att, log_total, gatt, gain, small2, dbup1, dbup2, dwout2, normed, w_cat,
         tokens, gresid, dup, ddown, dwout, seen_up, seen_down, out_rows,
     )
 
@@ -1011,16 +1196,6 @@
 def half_of(array, second):
     size = array.shape[0] // 2
     return lax.dynamic_slice_in_dim(array, jnp.where(second, size, 0), size, 0)
-
-
-def fetch_other(array, bits):
-    piece = array
-    for bit in reversed(bits):
-        piece = half_of(piece, dp_bit(bit))
-    piece = swap_tp(piece)
-    for bit in bits:
-        piece = joined(piece, swap_dp(piece, bit), dp_bit(bit))
-    return piece
 
 
 def add_low(left, right):
@@ -1058,48 +1233,28 @@
     )
     mask = jnp.where(valid, 0.0, -1e30).astype(F32).reshape(1, -1)
     row = lambda vector: vector.astype(F32).reshape(1, -1)
-    core, xbit = 1, 2
-
-    w_cat = jnp.concatenate([w_query, w_key, w_value], axis=1)
-    w_cat2 = fetch_other(w_cat, [core, xbit])
-    bias = jnp.concatenate([b_query, b_value, b_up]).astype(F32)
-    bias2 = swap_tp(bias)
-
-    def column(packed):
-        return jnp.concatenate(
-            [packed[:half], jnp.zeros((half,), F32), packed[half : 2 * half]]
-        ).reshape(-1, 1)
-
-    w_out2 = fetch_other(w_out, [core, xbit])
-    w_up2 = fetch_other(w_up, [core, xbit])
-    w_down2 = fetch_other(w_down, [core, xbit])
-    kept = half_of(cotangent, second)
-    got = swap_tp(half_of(cotangent, ~second))
-    grads = joined(kept, got, second)
-
-    normed, own_tokens, qkv = project_norm(
-        rank_arr, tokens, row(ln1_gain), row(ln1_bias), w_cat, column(bias), rows, 512
-    )
-    parts = (2, 3, heads, HEAD_DIM, rows)
-    att = attend_forward(mask, qkv.reshape(parts), 0)
-    qkv = project(qkv, normed, w_cat2, column(bias2), 512).reshape(parts)
-    att, log_total = attend_forward(mask, qkv, 1, att)
+    biases = jnp.concatenate([b_query, jnp.zeros_like(b_query), b_value, b_up]).astype(F32)
+    bias = jnp.broadcast_to(biases.reshape(1, -1), (8, biases.shape[0]))
+
+    (normed, qkv, att, log_total, resid, mid, w_cat, w_out_all, w_up2, w_down2, grads, bias2,
+     own_tokens) = front(
+        mask, row(ln1_gain), row(ln1_bias), row(b_out), row(ln2_gain), row(ln2_bias), bias,
+        tokens, w_query, w_key, w_value, w_out, w_up, w_down, cotangent, heads,
+    )
+    qkv = qkv.reshape(2, 3, heads, HEAD_DIM, rows)
     attended = att.reshape(2 * half, rows)
-    w_out_all = jnp.concatenate([w_out, w_out2], axis=0)
-    resid, mid = middle(
-        own_tokens, attended, w_out_all, row(b_out), row(ln2_gain), row(ln2_bias), 512
-    )
-    sum2, gmid2, dup2, ddown2, dbup2 = feed(mid, grads, w_up2, row(bias2[2 * half :]), w_down2)
+    up_bias = bias[:1, 3 * half :], bias2[:1, 3 * half :]
+    sum2, gmid2, dup2, ddown2, dbup2 = feed(mid, grads, w_up2, up_bias[1], w_down2)
     mid, both_up, both_down = lax.optimization_barrier((mid, over_cores(dup2), over_cores(ddown2, 2)))
     seen_up, seen_down = swap_tp(both_up), swap_tp(both_down)
-    sum1, gmid1, dup1, ddown1, dbup1 = feed(mid, grads, w_up, row(bias[2 * half :]), w_down)
+    sum1, gmid1, dup1, ddown1, dbup1 = feed(mid, grads, w_up, up_bias[0], w_down)
     out, gresid, gatt, dwout1, dwout2, small2 = branch(
         resid, (sum1, sum2), (gmid1, gmid2), grads, row(ln2_gain), row(b_down), w_out_all,
         attended, 512,
     )
     gtok, small, got_tok, grad_up, grad_down, grad_out_t, grad_cat, got_out = tail(
         mask, qkv, att, log_total, gatt.reshape(2, heads, HEAD_DIM, rows), row(ln1_gain), small2,
-        dbup1, dbup2, dwout2, normed, w_cat, w_cat2, own_tokens, gresid, dup1, ddown1, dwout1,
+        dbup1, dbup2, dwout2, normed, w_cat, own_tokens, gresid, dup1, ddown1, dwout1,
         seen_up, seen_down, out,
     )
     result = joined(half_of(out, second), got_out, second)

time: 451 us -> 403 us (0.89)
  the two profiles are of different devices: /device:TPU:27 before, /device:TPU:25 now
where the time goes in v2:
time: 403 us; the launch traced here: 396 us
  Pallas kernels  343 us (85%)
  local copies, waits for them, and re-layouts  27.4 us (7%)
  other arithmetic  21 us (5%)
    pallas_call x1, Pallas kernels, tail(): pl.pallas_call(functools.partial(tail_kernel, heads=heads, block=block),...  156 us
    pallas_call x1, Pallas kernels, front(): pl.pallas_call(functools.partial(front_kernel, heads=heads, block=block),...  84.6 us
    pallas_call x2, Pallas kernels, feed(): pl.pallas_call(functools.partial(feed_kernel, chunk=chunk), grid=(hidden...  80.6 us
    pallas_call x1, Pallas kernels, branch(): pl.pallas_call(branch_kernel, grid=(rows // block,), in_specs=[by_row] *...  22 us
  transfers between devices with their start and end apart: 4, of which 1 were waited for; matrix products, arithmetic and copies ran while one was open for 1% of the time, Pallas kernels for 16%

profile of v2, /device:TPU:25, one launch (start us, length us, event | category | flops | bytes accessed | tf_op | source)
XLA Modules:
  0.0 396.5 jit_solution(582958192733684449)
XLA Ops:
  3.4 1.3 reshape.211.gain_ref
  4.7 1.3 reshape.217.gain2_ref.gain_ref
  5.9 1.3 reshape.213.shift_ref
  11.7 84.6 %front.1 = (bf16[2048,768]{1,0:T(8,128)(2,1)}, bf16[2,1152,2048]{2,1,0:T(8,128)(2,1)}, bf16[2,8,48,2048]{3,2,1,0:T(8,128)(2,1)}, f32[2,8,1,2048]{3,2,1,0:T(1,128...) custom-call(f32[1,2048]{1,0:T(1,128)} %add_select_fusion.mask_ref, ...), custom_call_target="tpu_custom_call" | custom-call | flops 29930553344 | bytes 62914560 | tf_op jit(solution)/shard_map/front/pallas_call | solution.py:658
  96.3 1.4 slice.45.b_ref
  97.7 40.3 %feed.2 = (f32[2048,768]{1,0:T(8,128)}, f32[2048,768]{1,0:T(8,128)}, bf16[768,1536]{1,0:T(8,128)(2,1)}, bf16[1536,768]{1,0:T(8,128)(2,1)}, f32[1,1536]{1,0:T(1,128)}) custom-call(bf16[2048,768]{1,0:T(8,128)(2,1)} %get-tuple-element.68.mid_ref, bf16[2048,768]{1,0:T(8,128)(2,1)} %get-tuple-element.62.grad_ref, bf16[768,1536]{1,0:T(8,128)(2,1)} %get-tuple-element.63.up_ref, ...), custom_call_target="tpu_custom_call" | custom-call | flops 28991029248 | bytes 31457280 | tf_op jit(solution)/shard_map/feed/pallas_call | solution.py:776
  138.0 2.5 constant_dynamic-slice_fusion.1
  143.0 1.6 collective-permute-done.1
  144.6 1.9 add_convert_fusion
  146.5 1.5 fusion.1
  148.1 1.3 collective-permute-start.2
  149.6 40.3 %feed.3 = (f32[2048,768]{1,0:T(8,128)}, f32[2048,768]{1,0:T(8,128)}, bf16[768,1536]{1,0:T(8,128)(2,1)}, bf16[1536,768]{1,0:T(8,128)(2,1)}, f32[1,1536]{1,0:T(1,128)}) custom-call(bf16[2048,768]{1,0:T(8,128)(2,1)} %get-tuple-element.68.mid_ref, bf16[2048,768]{1,0:T(8,128)(2,1)} %get-tuple-element.62.grad_ref, bf16[768,1536]{1,0:T(8,128)(2,1)} %up_ref.1, ...), custom_call_target="tpu_custom_call" | custom-call | flops 28991029248 | bytes 31457280 | tf_op jit(solution)/shard_map/feed/pallas_call | solution.py:776
  189.9 22.0 %branch.1 = (bf16[2048,768]{1,0:T(8,128)(2,1)}, f32[2048,768]{1,0:T(8,128)}, bf16[768,2048]{1,0:T(8,128)(2,1)}, bf16[768,384]{1,0:T(8,128)(2,1)}, bf16[768,384]{1,0:T(8,128)(2,1)}, /*index=5*/f32[8,768]{1,0:T(8,128)}) custom-call(f32[2048,768]{1,0:T(8,128)} %get-tuple-element.60.resid_ref, f32[2048,768]{1,0:T(8,128)} %get-tuple-element.69.sum1_ref, ...), custom_call_target="tpu_custom_call" | custom-call | flops 4831838208 | bytes 50331648 | tf_op jit(solution)/shard_map/branch/pallas_call | solution.py:844
  212.0 2.7 constant_dynamic-slice_fusion
  216.0 155.6 %tail.1 = (f32[1024,768]{1,0:T(8,128)}, f32[16,768]{1,0:T(8,128)}, bf16[1024,768]{1,0:T(8,128)(2,1)}, bf16[768,1536]{1,0:T(8,128)(2,1)}, bf16[1536,768]{1,0:T(8,...) custom-call(f32[1,2048]{1,0:T(1,128)} %add_select_fusion.mask_ref, ...), custom_call_target="tpu_custom_call" | custom-call | flops 53687091200 | bytes 25165824 | tf_op jit(solution)/shard_map/tail/pallas_call | solution.py:1142
  371.6 1.6 slice_reduce_fusion
  374.0 1.3 slice_reduce_fusion.6
  375.3 1.8 convert_element_type.66
  377.4 2.8 convert_element_type.70
  380.3 2.5 convert_element_type.71
  382.8 1.9 fusion.3
  385.8 2.7 copy.36
  389.0 5.1 %maximum_select_fusion = f32[2048,768]{1,0:T(8,128)} fusion(f32[1024,768]{1,0:T(8,128)} %get-tuple-element.91, f32[1024,768]{1,0:T(8,128)S(1)} %convert_element_type.66, pred[]{:T(512)S(6)} %eq.3), kind=kLoop, calls=%fused_computation | loop fusion | flops 4718592 | bytes 12582913 | tf_op jit(solution)/shard_map/jit(_where)/select_n | solution.py:1193
  394.1 2.1 maximum_select_fusion.1
  (46 shorter events, 14.1 us)
Async XLA Ops:
  138.0 3.7 copy-start.4
  138.0 3.8 copy-start.7
  138.0 4.4 %copy-start.8 = (bf16[768]{0:T(1024)(128)(2,1)S(1)}, bf16[768]{0:T(1024)(128)(2,1)}, u32[]{:S(2)}) copy-start(bf16[768]{0:T(1024)(128)(2,1)} %param.36) | copy-start | bytes 4612
  140.5 4.1 %collective-permute-start.1 = (bf16[2,384,768]{2,1,0:T(8,128)(2,1)}, bf16[2,384,768]{2,1,0:T(8,128)(2,1)}, u32[]{:S(2)}, u32[]{:S(2)}) collective-permute-start(bf16[2,384,768]{2,1,0:T(8,128)(2,1)} %constant_dynamic-slice_fusion.1), channel_id=1, source_target_pairs={{0,2},{2,0},{4,6},{6,4},{8,10},{10,8},{12,14},{14,12},{16,18},{18,... | collective-permute-start | bytes 3538952 | tf_op jit(solution)/shard_map/ppermute | solution.py:1185
  141.7 4.8 %collective-permute-start = (bf16[1,384,1536]{2,1,0:T(8,128)(2,1)S(1)}, bf16[1,384,1536]{2,1,0:T(8,128)(2,1)}, u32[]{:S(2)}, u32[]{:S(2)}) collective-permute-start(bf16[1,384,1536]{2,1,0:T(8,128)(2,1)S(1)} %dynamic-slice_bitcast_fusion), channel_id=1, source_target_pairs={{0,2},{2,0},{4,6},{6,4},{8,10},{10,8},{12,14},{14,12},{16,18},{18,... | collective-permute-start | bytes 3538952 | tf_op jit(solution)/shard_map/ppermute | solution.py:1185
  148.1 66.6 %collective-permute-start.2 = (bf16[384,1536]{1,0:T(8,128)(2,1)S(1)}, bf16[384,1536]{1,0:T(8,128)(2,1)S(1)}, u32[]{:S(2)}, u32[]{:S(2)}) collective-permute-start(bf16[384,1536]{1,0:T(8,128)(2,1)S(1)} %fusion.1), channel_id=1, source_target_pairs={{0,1},{1,0},{2,3},{3,2},{4,5},{5,4},{6,7},{7,6},{8,9},{9,8},{10,11... | collective-permute-start | bytes 3538952 | tf_op jit(solution)/shard_map/ppermute | solution.py:1180
  149.4 65.3 %collective-permute-start.3 = (bf16[768,768]{1,0:T(8,128)(2,1)S(1)}, bf16[768,768]{1,0:T(8,128)(2,1)S(1)}, u32[]{:S(2)}, u32[]{:S(2)}) collective-permute-start(bf16[768,768]{1,0:T(8,128)(2,1)S(1)} %bitcast.22), channel_id=1, source_target_pairs={{0,1},{1,0},{2,3},{3,2},{4,5},{5,4},{6,7},{7,6},{8,9},{9,8},{10,11... | collective-permute-start | bytes 3538952 | tf_op jit(solution)/shard_map/ppermute | solution.py:1180
  214.6 1.0 copy-start.9
  214.6 1.4 copy-start.10
  375.3 2.1 copy-start.3
  377.4 2.8 copy-start.2
  380.3 2.5 copy-start
  382.8 1.9 copy-start.6
  389.0 5.1 %copy-start.1 = (bf16[1024,768]{1,0:T(8,128)(2,1)S(1)}, bf16[1024,768]{1,0:T(8,128)(2,1)}, u32[]{:S(2)}) copy-start(bf16[1024,768]{1,0:T(8,128)(2,1)} %constant_dynamic-slice_fusion) | copy-start | bytes 4718596
  389.0 5.1 %copy-start.5 = (bf16[1024,768]{1,0:T(8,128)(2,1)S(1)}, bf16[1024,768]{1,0:T(8,128)(2,1)}, u32[]{:S(2)}) copy-start(bf16[1024,768]{1,0:T(8,128)(2,1)} %get-tuple-element.89) | copy-start | bytes 4718596

commit v3 on v2

--- a/solution.py
+++ b/solution.py
@@ -145,7 +145,7 @@
 class PlaneSum:
     def __init__(self, place, own, seen, out, refs):
         self.place, self.own, self.seen, self.out = place, own, seen, out
-        (self.acc, self.seen_here, self.from_core, self.from_x, self.from_z,
+        (self.acc, self.seen_here, self.from_core, self.from_x, self.from_z, self.whole,
          self.send, self.recv, self.local) = refs
         self.rows = own.shape[0]
 
@@ -157,9 +157,10 @@
             pltpu.VMEM((rows // 2, width), BF16),
             pltpu.VMEM((rows // 4, width), BF16),
             pltpu.VMEM((3, rows // 16, width), BF16),
+            pltpu.VMEM((rows // 2, width), BF16),
             pltpu.SemaphoreType.DMA((10,)),
             pltpu.SemaphoreType.DMA((10,)),
-            pltpu.SemaphoreType.DMA((3,)),
+            pltpu.SemaphoreType.DMA((4,)),
         ]
 
     def copy(self, source, target, place, device):
@@ -196,10 +197,7 @@
     def piece(self):
         count = self.rows // 16
         inside = self.place.x * 4 * count + self.place.z * count
-        return (
-            part(self.acc, inside, count),
-            part(self.out, self.place.core * 8 * count + inside, count),
-        )
+        return part(self.acc, inside, count), part(self.whole, inside, count)
 
     def keep_copy(self):
         mine, there = self.piece()
@@ -213,13 +211,18 @@
 
     def back_x_copy(self):
         count = self.rows // 4
-        there = part(self.out, self.place.core * 2 * count + self.place.x * count, count)
+        there = part(self.whole, self.place.x * count, count)
         return self.copy(there, there, 8, self.place.across_x())
 
     def back_core_copy(self):
         count = self.rows // 2
         there = part(self.out, self.place.core * count, count)
-        return self.copy(there, there, 9, self.place.across_core())
+        return self.copy(self.whole, there, 9, self.place.across_core())
+
+    def store_copy(self):
+        count = self.rows // 2
+        there = part(self.out, self.place.core * count, count)
+        return pltpu.make_async_copy(self.whole, there, self.local.at[3])
 
     def begin(self):
         self.core_copy().start()
@@ -259,9 +262,11 @@
     def back_to_core(self):
         self.back_x_copy().wait()
         self.back_core_copy().start()
+        self.store_copy().start()
 
     def end(self):
         self.back_core_copy().wait()
+        self.store_copy().wait()
 
 
 class PartnerTerm:
@@ -429,8 +434,8 @@
     tok_hbm, wq_hbm, wk_hbm, wv_hbm, wout_hbm, wup_hbm, wdown_hbm, cot_hbm,
     x_out, qkv_out, att_out, log_out, resid_out, mid_out,
     cat_hbm, wout_all_hbm, up2_hbm, down2_hbm, grads_hbm, bias2_hbm, tok_out,
-    tok_ref, x_ref, qkv_ref, att_ref, cat_ref, wout_ref, bias2_ref, load_sem, out_sem, swap_send,
-    swap_recv, *scratch, heads, block,
+    tok_ref, x_ref, qkv_ref, att_ref, cat_ref, wout_ref, bias2_ref, up2_ref, down2_ref, grads_ref,
+    load_sem, out_sem, swap_send, swap_recv, *scratch, heads, block,
 ):
     step = pl.program_id(0)
     place = Place()
@@ -447,15 +452,15 @@
         for i, own in enumerate(mine)
     ]
     fetch_out = Fetch(place, wout_hbm, wout_ref.at[pl.ds(half, half)], sems[3], False)
-    fetch_up = Fetch(place, wup_hbm, up2_hbm, sems[4], True)
-    fetch_down = Fetch(place, wdown_hbm, down2_hbm, sems[5], True)
+    fetch_up = Fetch(place, wup_hbm, up2_ref, sems[4], True)
+    fetch_down = Fetch(place, wdown_hbm, down2_ref, sems[5], True)
     bias_copy = send_to(
         bias_ref, bias2_ref, swap_send.at[0], swap_recv.at[0], place.partner()
     )
     here = pl.ds(pl.multiple_of(place.rank * LEN_L, LEN_L), LEN_L)
     theirs = pl.ds(pl.multiple_of((1 - place.rank) * LEN_L, LEN_L), LEN_L)
     cot_copy = send_to(
-        cot_hbm.at[theirs], grads_hbm.at[here], swap_send.at[1], swap_recv.at[1], place.partner()
+        cot_hbm.at[theirs], grads_ref.at[here], swap_send.at[1], swap_recv.at[1], place.partner()
     )
 
     def token_rows(i):
@@ -473,12 +478,17 @@
         for i, own in enumerate(mine)
     ]
     out_load = pltpu.make_async_copy(wout_hbm, wout_ref.at[pl.ds(0, half)], load_sem.at[5])
-    kept_copy = pltpu.make_async_copy(cot_hbm.at[here], grads_hbm.at[here], out_sem.at[0])
+    kept_copy = pltpu.make_async_copy(cot_hbm.at[here], grads_ref.at[here], out_sem.at[0])
     stores = [
         pltpu.make_async_copy(cat_ref, cat_hbm, out_sem.at[1]),
         pltpu.make_async_copy(wout_ref, wout_all_hbm, out_sem.at[2]),
         pltpu.make_async_copy(bias2_ref, bias2_hbm, out_sem.at[3]),
         pltpu.make_async_copy(tok_ref, tok_out, out_sem.at[4]),
+    ]
+    last_stores = [
+        pltpu.make_async_copy(grads_ref, grads_hbm, out_sem.at[5]),
+        pltpu.make_async_copy(up2_ref, up2_hbm, out_sem.at[6]),
+        pltpu.make_async_copy(down2_ref, down2_hbm, out_sem.at[7]),
     ]
 
     @pl.when(step == 0)
@@ -579,9 +589,12 @@
     def _():
         for one in (fetch_up, fetch_down):
             one.end()
+        for copy in last_stores[1:]:
+            copy.start()
         cot_copy.wait()
         kept_copy.wait()
-        for copy in stores:
+        last_stores[0].start()
+        for copy in (*stores, *last_stores):
             copy.wait()
 
 
@@ -696,8 +709,11 @@
             pltpu.VMEM((2, width, 3 * half), BF16),
             pltpu.VMEM((2 * half, width), BF16),
             pltpu.VMEM((bias_rows, bias_width), F32),
+            pltpu.VMEM((width, hidden), BF16),
+            pltpu.VMEM((hidden, width), BF16),
+            pltpu.VMEM((rows, width), BF16),
             pltpu.SemaphoreType.DMA((6,)),
-            pltpu.SemaphoreType.DMA((5,)),
+            pltpu.SemaphoreType.DMA((8,)),
             pltpu.SemaphoreType.DMA((2,)),
             pltpu.SemaphoreType.DMA((2,)),
         ]
@@ -865,14 +881,20 @@
 TAIL_BLOCK = 512
 SUM_ACTIONS = ("begin", "along_x", "along_z", "back_along_z", "back_along_x", "back_to_core")
 SUM_STEPS = (
-    (0, 1, 3, 7, 9, 11),
-    (0, 3, 5, 11, 13, 15),
-    (0, 5, 9, 15, 17, 19),
-    (0, 7, 13, 17, 20, 99),
-    (0, 4, 6, 8, 10, 13),
-    (17, 18, 20, 99, 99, 99),
+    (0, 1, 4, 12, 14, 16),
+    (0, 3, 6, 14, 16, 18),
+    (0, 5, 8, 16, 18, 20),
+    (0, 7, 10, 18, 20),
+    (0, 9, 12, 15, 17, 19),
+    (None, 17, 19),
+    (None, 17, 20),
+    (None, 17),
 )
-LAST = 99
+LAST_ACTIONS = (
+    (7, "along_z"), 0, (5, "back_along_z"), 1, (6, "back_along_z"), (3, "back_to_core"), 2,
+    (7, "back_along_z"), (5, "back_along_x"), (6, "back_along_x"), (7, "back_along_x"),
+    (5, "back_to_core"), (6, "back_to_core"), (7, "back_to_core"),
+)
 
 
 def tail_kernel(
@@ -880,19 +902,20 @@
     wout2_ref, x_hbm, w_hbm, tok_hbm, gresid_hbm, up_hbm, down_hbm, wout_hbm, seen_up,
     seen_down, out_hbm,
     gtok_ref, small_ref, got_hbm, gup_hbm, gdown_hbm, gout_hbm, gcat_hbm, got_out,
-    d_ref, x_ref, w_ref, tok_ref, gresid_ref, dw_ref, dw2_ref, sent_ref, own_small, other_small,
-    load_sem, row_sem, tok_send, tok_recv, *scratch, heads, block,
+    d_ref, x_ref, w_ref, tok_ref, gresid_ref, dw_ref, dw2_ref, seen_cat, sent_ref, own_small,
+    other_small, load_sem, row_sem, tok_send, tok_recv, *scratch, heads, block,
 ):
     step = pl.program_id(0)
     place = Place()
     first_rows = 2 * heads + 1
+    last_step = first_rows + 3
     width = x_ref.shape[1]
     half = heads * HEAD_DIM
     halves = width
 
     groups = []
     at = 0
-    for count in [8] * 6 + [3, 3, 4]:
+    for count in [9] * 8 + [3, 3, 4]:
         groups.append(scratch[at : at + count])
         at += count
     columns = lambda ref, i: ref.at[:, pl.ds(i * halves, halves)]
@@ -913,14 +936,20 @@
         for i in (0, 1)
     ]
     sums.append(PlaneSum(place, wout_hbm, None, gout_hbm, groups[4]))
-    sums.append(PlaneSum(place, dw_ref, None, gcat_hbm, groups[5]))
-    cat_term = PartnerTerm(place, dw2_ref, groups[5][1], groups[6])
-    out_term = PartnerTerm(place, wout2_ref, groups[4][1], groups[7])
-    small = SmallSum(place, own_small, other_small, groups[8])
+    third = lambda ref, i: ref.at[:, pl.ds(i * half, half)]
+    cat_sums = [
+        PlaneSum(
+            place, third(dw_ref, i), None, third(gcat_hbm, i),
+            (groups[5 + i][0], third(seen_cat, i), *groups[5 + i][2:]),
+        )
+        for i in range(3)
+    ]
+    cat_term = PartnerTerm(place, dw2_ref, seen_cat, groups[8])
+    out_term = PartnerTerm(place, wout2_ref, groups[4][1], groups[9])
+    small = SmallSum(place, own_small, other_small, groups[10])
     theirs = pl.ds(pl.multiple_of((1 - place.rank) * LEN_L, LEN_L), LEN_L)
-    out_copy = send_to(
-        out_hbm.at[theirs], got_out, tok_send.at[2], tok_recv.at[2], place.partner()
-    )
+    out_load = pltpu.make_async_copy(out_hbm.at[theirs], sent_ref, load_sem.at[2])
+    out_copy = send_to(sent_ref, got_out, tok_send.at[2], tok_recv.at[2], place.partner())
 
     loads = [
         pltpu.make_async_copy(x_hbm, x_ref, load_sem.at[0]),
@@ -945,11 +974,10 @@
             sent_ref.at[there], got_hbm.at[there], tok_send.at[i], tok_recv.at[i], place.partner()
         )
 
-    def weight_gradient(source, target):
-        for i in range(3):
-            here = pl.ds(i * half, half)
-            product = contract(x_ref[...], d_ref[source, here, :], 0, 1)
-            target[:, here] = product.astype(BF16)
+    def weight_gradient(source, target, i):
+        here = pl.ds(i * half, half)
+        product = contract(x_ref[...], d_ref[source, here, :], 0, 1)
+        target[:, here] = product.astype(BF16)
 
     def bias_rows(source, target):
         ones = jnp.ones((16, d_ref.shape[2]), BF16)
@@ -957,22 +985,25 @@
             row = contract(ones, d_ref[source, pl.ds(which * half, half), :], 1, 1)
             target[8:9, pl.ds(i * half, half)] = row[:1]
 
-    last_step = first_rows + 3
     events = {}
+    sums += cat_sums
     for one, times in zip(sums, SUM_STEPS):
         for when, action in zip(times, SUM_ACTIONS):
+            if when is None:
+                continue
             events.setdefault(when, []).append(getattr(one, action))
-    late = events.pop(LAST, [])
 
     for when in sorted(events):
 
         @pl.when(step == when)
         def _(when=when):
             if when == 0:
+                out_load.start()
                 place.greet()
                 out_term.begin()
             if when == 1:
                 out_term.to_partner()
+                out_load.wait()
                 out_copy.start()
             if when == 4:
                 out_term.end()
@@ -988,7 +1019,8 @@
     def _():
         for copy in loads:
             copy.wait()
-        weight_gradient(1, dw2_ref)
+        for i in range(3):
+            weight_gradient(1, dw2_ref, i)
         cat_term.begin()
 
     @pl.when(step == heads + 1)
@@ -1007,8 +1039,12 @@
         for copy in row_loads(0):
             copy.start()
         cat_term.end()
-        weight_gradient(0, dw_ref)
+        out_copy.wait()
+        for i in range(3):
+            weight_gradient(0, dw_ref, i)
+            cat_sums[i].begin()
         bias_rows(0, own_small)
+
 
     for i in range(4):
 
@@ -1041,14 +1077,13 @@
             own_small[6 + i : 7 + i] = dbup1_ref[:, pl.ds(i * width, width)]
             other_small[6 + i : 7 + i] = dbup2_ref[:, pl.ds(i * width, width)]
         small.begin()
-        late_steps = iter(late)
-        small.over_cores()
-        small.over_x()
-        small.over_z()
-        for action in late_steps:
-            action()
+        small_actions = (small.over_cores, small.over_x, small.over_z)
+        for item in LAST_ACTIONS:
+            if isinstance(item, int):
+                small_actions[item]()
+            else:
+                getattr(sums[item[0]], item[1])()
         small_ref[...] = small.end()
-        out_copy.wait()
         for i in (0, 1):
             token_copy(i).wait()
         for one in sums:
@@ -1116,7 +1151,7 @@
     )
     one = pl.BlockSpec((1, 1, HEAD_DIM, rows), lambda h: (*head(h), 0, 0))
     row = pl.BlockSpec((1, 1, 1, rows), lambda h: (*head(h), 0, 0))
-    sum_shapes = [(width, width)] * 4 + [dwout.shape, (width, out)]
+    sum_shapes = [(width, width)] * 4 + [dwout.shape] + [(width, out // 3)] * 3
     scratch = [
         pltpu.VMEM((2, out, rows), BF16),
         pltpu.VMEM((rows, width), BF16),
@@ -1125,10 +1160,11 @@
         pltpu.VMEM((2, TAIL_BLOCK, width), F32),
         pltpu.VMEM((width, out), BF16),
         pltpu.VMEM((width, out), BF16),
+        pltpu.VMEM((width // 2, out), BF16),
         pltpu.VMEM((rows // 2, width), BF16),
         pltpu.VMEM((SmallSum.ROWS, width), F32),
         pltpu.VMEM((SmallSum.ROWS, width), F32),
-        pltpu.SemaphoreType.DMA((2,)),
+        pltpu.SemaphoreType.DMA((3,)),
         pltpu.SemaphoreType.DMA((2, 2)),
         pltpu.SemaphoreType.DMA((3,)),
         pltpu.SemaphoreType.DMA((3,)),

time: 403 us -> 385 us (0.955)
  the two profiles are of different devices: /device:TPU:25 before, /device:TPU:0 now
where the time goes in v3:
time: 385 us; the launch traced here: 379 us
  Pallas kernels  325 us (84%)
  local copies, waits for them, and re-layouts  27.4 us (7%)
  other arithmetic  21 us (5%)
    pallas_call x1, Pallas kernels, tail(): pl.pallas_call(functools.partial(tail_kernel, heads=heads, block=block),...  147 us
    pallas_call x2, Pallas kernels, feed(): pl.pallas_call(functools.partial(feed_kernel, chunk=chunk), grid=(hidden...  80.6 us
    pallas_call x1, Pallas kernels, front(): pl.pallas_call(functools.partial(front_kernel, heads=heads, block=block),...  75.9 us
    pallas_call x1, Pallas kernels, branch(): pl.pallas_call(branch_kernel, grid=(rows // block,), in_specs=[by_row] *...  22.1 us
  transfers between devices with their start and end apart: 4, of which 1 were waited for; matrix products, arithmetic and copies ran while one was open for 2% of the time, Pallas kernels for 16%

profile of v3, /device:TPU:0, one launch (start us, length us, event | category | flops | bytes accessed | tf_op | source)
XLA Modules:
  0.0 378.9 jit_solution(14835200026758420196)
XLA Ops:
  3.4 1.3 reshape.211.gain_ref
  4.7 1.3 reshape.217.gain2_ref.gain_ref
  5.9 1.3 reshape.213.shift_ref
  11.7 75.9 %front.1 = (bf16[2048,768]{1,0:T(8,128)(2,1)}, bf16[2,1152,2048]{2,1,0:T(8,128)(2,1)}, bf16[2,8,48,2048]{3,2,1,0:T(8,128)(2,1)}, f32[2,8,1,2048]{3,2,1,0:T(1,128...) custom-call(f32[1,2048]{1,0:T(1,128)} %add_select_fusion.mask_ref, ...), custom_call_target="tpu_custom_call" | custom-call | flops 29930553344 | bytes 62914560 | tf_op jit(solution)/shard_map/front/pallas_call | solution.py:671
  87.6 1.4 slice.45.b_ref
  89.0 40.3 %feed.2 = (f32[2048,768]{1,0:T(8,128)}, f32[2048,768]{1,0:T(8,128)}, bf16[768,1536]{1,0:T(8,128)(2,1)}, bf16[1536,768]{1,0:T(8,128)(2,1)}, f32[1,1536]{1,0:T(1,128)}) custom-call(bf16[2048,768]{1,0:T(8,128)(2,1)} %get-tuple-element.68.mid_ref, bf16[2048,768]{1,0:T(8,128)(2,1)} %get-tuple-element.62.grad_ref, bf16[768,1536]{1,0:T(8,128)(2,1)} %get-tuple-element.63.up_ref, ...), custom_call_target="tpu_custom_call" | custom-call | flops 28991029248 | bytes 31457280 | tf_op jit(solution)/shard_map/feed/pallas_call | solution.py:792
  129.3 2.5 constant_dynamic-slice_fusion.1
  133.7 1.5 collective-permute-done.1
  135.1 1.9 add_convert_fusion
  137.1 1.5 fusion.1
  139.2 1.5 collective-permute-start.3
  140.7 40.3 %feed.3 = (f32[2048,768]{1,0:T(8,128)}, f32[2048,768]{1,0:T(8,128)}, bf16[768,1536]{1,0:T(8,128)(2,1)}, bf16[1536,768]{1,0:T(8,128)(2,1)}, f32[1,1536]{1,0:T(1,128)}) custom-call(bf16[2048,768]{1,0:T(8,128)(2,1)} %get-tuple-element.68.mid_ref, bf16[2048,768]{1,0:T(8,128)(2,1)} %get-tuple-element.62.grad_ref, bf16[768,1536]{1,0:T(8,128)(2,1)} %up_ref.1, ...), custom_call_target="tpu_custom_call" | custom-call | flops 28991029248 | bytes 31457280 | tf_op jit(solution)/shard_map/feed/pallas_call | solution.py:792
  181.0 22.1 %branch.1 = (bf16[2048,768]{1,0:T(8,128)(2,1)}, f32[2048,768]{1,0:T(8,128)}, bf16[768,2048]{1,0:T(8,128)(2,1)}, bf16[768,384]{1,0:T(8,128)(2,1)}, bf16[768,384]{1,0:T(8,128)(2,1)}, /*index=5*/f32[8,768]{1,0:T(8,128)}) custom-call(f32[2048,768]{1,0:T(8,128)} %get-tuple-element.60.resid_ref, f32[2048,768]{1,0:T(8,128)} %get-tuple-element.69.sum1_ref, ...), custom_call_target="tpu_custom_call" | custom-call | flops 4831838208 | bytes 50331648 | tf_op jit(solution)/shard_map/branch/pallas_call | solution.py:860
  203.1 2.7 constant_dynamic-slice_fusion
  207.2 146.8 %tail.1 = (f32[1024,768]{1,0:T(8,128)}, f32[16,768]{1,0:T(8,128)}, bf16[1024,768]{1,0:T(8,128)(2,1)}, bf16[768,1536]{1,0:T(8,128)(2,1)}, bf16[1536,768]{1,0:T(8,...) custom-call(f32[1,2048]{1,0:T(1,128)} %add_select_fusion.mask_ref, ...), custom_call_target="tpu_custom_call" | custom-call | flops 53687091200 | bytes 25165824 | tf_op jit(solution)/shard_map/tail/pallas_call | solution.py:1178
  354.0 1.6 slice_reduce_fusion
  356.3 1.3 slice_reduce_fusion.6
  357.7 1.8 convert_element_type.66
  359.8 2.8 convert_element_type.70
  362.6 2.5 convert_element_type.71
  365.2 1.9 fusion.3
  368.1 2.7 copy.36
  371.4 5.1 %maximum_select_fusion = f32[2048,768]{1,0:T(8,128)} fusion(f32[1024,768]{1,0:T(8,128)} %get-tuple-element.91, f32[1024,768]{1,0:T(8,128)S(1)} %convert_element_type.66, pred[]{:T(512)S(6)} %eq.3), kind=kLoop, calls=%fused_computation | loop fusion | flops 4718592 | bytes 12582913 | tf_op jit(solution)/shard_map/jit(_where)/select_n | solution.py:1229
  376.5 2.1 maximum_select_fusion.1
  (46 shorter events, 13.8 us)
Async XLA Ops:
  129.3 2.6 copy-start.4
  129.3 3.2 copy-start.7
  129.3 3.8 %copy-start.8 = (bf16[768]{0:T(1024)(128)(2,1)S(1)}, bf16[768]{0:T(1024)(128)(2,1)}, u32[]{:S(2)}) copy-start(bf16[768]{0:T(1024)(128)(2,1)} %param.36) | copy-start | bytes 4612
  131.8 3.3 collective-permute-start.1
  131.9 5.1 %collective-permute-start = (bf16[1,384,1536]{2,1,0:T(8,128)(2,1)S(1)}, bf16[1,384,1536]{2,1,0:T(8,128)(2,1)}, u32[]{:S(2)}, u32[]{:S(2)}) collective-permute-start(bf16[1,384,1536]{2,1,0:T(8,128)(2,1)S(1)} %dynamic-slice_bitcast_fusion), channel_id=1, source_target_pairs={{0,2},{2,0},{4,6},{6,4},{8,10},{10,8},{12,14},{14,12},{16,18},{18,... | collective-permute-start | bytes 3538952 | tf_op jit(solution)/shard_map/ppermute | solution.py:1221
  138.6 67.1 %collective-permute-start.2 = (bf16[384,1536]{1,0:T(8,128)(2,1)S(1)}, bf16[384,1536]{1,0:T(8,128)(2,1)S(1)}, u32[]{:S(2)}, u32[]{:S(2)}) collective-permute-start(bf16[384,1536]{1,0:T(8,128)(2,1)S(1)} %fusion.1), channel_id=1, source_target_pairs={{0,1},{1,0},{2,3},{3,2},{4,5},{5,4},{6,7},{7,6},{8,9},{9,8},{10,11... | collective-permute-start | bytes 3538952 | tf_op jit(solution)/shard_map/ppermute | solution.py:1216
  139.2 66.6 %collective-permute-start.3 = (bf16[768,768]{1,0:T(8,128)(2,1)S(1)}, bf16[768,768]{1,0:T(8,128)(2,1)S(1)}, u32[]{:S(2)}, u32[]{:S(2)}) collective-permute-start(bf16[768,768]{1,0:T(8,128)(2,1)S(1)} %bitcast.22), channel_id=1, source_target_pairs={{0,1},{1,0},{2,3},{3,2},{4,5},{5,4},{6,7},{7,6},{8,9},{9,8},{10,11... | collective-permute-start | bytes 3538952 | tf_op jit(solution)/shard_map/ppermute | solution.py:1216
  205.8 1.0 copy-start.9
  205.8 1.4 copy-start.10
  357.7 2.1 copy-start.3
  359.8 2.8 copy-start.2
  362.6 2.5 copy-start
  365.2 1.9 copy-start.6
  371.4 5.1 %copy-start.1 = (bf16[1024,768]{1,0:T(8,128)(2,1)S(1)}, bf16[1024,768]{1,0:T(8,128)(2,1)}, u32[]{:S(2)}) copy-start(bf16[1024,768]{1,0:T(8,128)(2,1)} %constant_dynamic-slice_fusion) | copy-start | bytes 4718596
  371.4 5.1 %copy-start.5 = (bf16[1024,768]{1,0:T(8,128)(2,1)S(1)}, bf16[1024,768]{1,0:T(8,128)(2,1)}, u32[]{:S(2)}) copy-start(bf16[1024,768]{1,0:T(8,128)(2,1)} %get-tuple-element.89) | copy-start | bytes 4718596

commit v4 on v3

--- a/solution.py
+++ b/solution.py
@@ -15,7 +15,7 @@
 BF16 = jnp.bfloat16
 LOG2E = math.log2(math.e)
 SCALE = HEAD_DIM ** (-0.5)
-VMEM_LIMIT = 58 << 20
+VMEM_LIMIT = 60 << 20
 HEAD_GROUP = 2
 
 
@@ -128,7 +128,7 @@
 
 
 def add_rows(target, start, count, terms):
-    tile = 48
+    tile = 48 if count % 48 == 0 else 32
 
     def body(i, _):
         at = pl.multiple_of(i * tile, 16)
@@ -747,122 +747,188 @@
     return value * below, below + value * bell * (1.0 / math.sqrt(2.0 * math.pi))
 
 
-def feed_kernel(
-    mid_ref, grad_ref, up_ref, b_ref, down_ref, sum_ref, gmid_ref, dup_ref, ddown_ref, db_ref,
-    act_ref, gpre_ref, *, chunk,
+HIDDEN_BLOCK = 512
+MID_BLOCK = 512
+MID_CHUNK = 512
+
+
+def mid_kernel(
+    mid_ref, grad_ref, bias_ref, resid_ref, gain_ref, bdown_ref, w_ref, att_ref,
+    up2_hbm, up_hbm, down2_hbm, down_hbm,
+    out_ref, gresid_ref, gatt_ref, dw_own_ref, dw_other_ref, small_ref, db_ref,
+    dup_hbm, ddown_hbm, seen_up, seen_down,
+    sum_ref, gmid_ref, act_ref, gpre_ref, up_ref, down_ref, dup_ref, ddown_ref, acc_ref,
+    load_sem, store_sem, *scratch, blocks,
 ):
-    @pl.when(pl.program_id(0) == 0)
-    def _():
-        sum_ref[...] = jnp.zeros_like(sum_ref)
-        gmid_ref[...] = jnp.zeros_like(gmid_ref)
-
-    rows = mid_ref.shape[0]
-    up, down, bias = up_ref[...], down_ref[...], b_ref[...]
-
-    def products(at):
-        here = slice(at, at + chunk)
-        return (
-            contract(mid_ref[here], up, 1, 0) + bias,
-            contract(grad_ref[here], down, 1, 1),
+    step = pl.program_id(0)
+    place = Place()
+    rows, width = mid_ref.shape
+    cut = lambda ref, i: ref.at[:, pl.ds(i * HIDDEN_BLOCK, HIDDEN_BLOCK)]
+    take = lambda ref, i, count: ref.at[pl.ds(i * count, count)]
+    terms = []
+    for i in range(blocks):
+        refs = [scratch[6 * i : 6 * i + 3], scratch[6 * i + 3 : 6 * i + 6]]
+        terms.append(
+            (
+                PartnerTerm(place, dup_ref.at[i], cut(seen_up, i), refs[0]),
+                PartnerTerm(
+                    place, ddown_ref.at[i], take(seen_down, i, HIDDEN_BLOCK // 2), refs[1]
+                ),
+            )
         )
 
-    now = products(0)
-    db = None
-    for at in range(0, rows, chunk):
-        here = slice(at, at + chunk)
-        later = products(at + chunk) if at + chunk < rows else None
-        value, slope = gelu_and_slope(now[0])
-        act = value.astype(BF16)
-        gpre = (slope * now[1]).astype(BF16)
-        act_ref[here] = act
-        gpre_ref[here] = gpre
-        part = jnp.sum(gpre.astype(F32), axis=0, keepdims=True)
-        db = part if db is None else db + part
-        sum_ref[here] += contract(act, down, 1, 0)
-        gmid_ref[here] += contract(gpre, up, 1, 1)
-        now = later
-    db_ref[...] = db
-    ddown_ref[...] = contract(act_ref[...], grad_ref[...], 0, 0).astype(BF16)
-    dup_ref[...] = contract(mid_ref[...], gpre_ref[...], 0, 0).astype(BF16)
-
-
-def feed(mid, grads, w_up, b_up, w_down, block=512, chunk=512):
-    rows, width = mid.shape
-    hidden = w_up.shape[1]
-    return pl.pallas_call(
-        functools.partial(feed_kernel, chunk=chunk),
-        grid=(hidden // block,),
-        in_specs=[
-            whole((rows, width)),
-            whole((rows, width)),
-            pl.BlockSpec((width, block), lambda j: (0, j)),
-            pl.BlockSpec((1, block), lambda j: (0, j)),
-            pl.BlockSpec((block, width), lambda j: (j, 0)),
-        ],
-        out_specs=[
-            whole((rows, width)),
-            whole((rows, width)),
-            pl.BlockSpec((width, block), lambda j: (0, j)),
-            pl.BlockSpec((block, width), lambda j: (j, 0)),
-            pl.BlockSpec((1, block), lambda j: (0, j)),
-        ],
-        out_shape=[
-            jax.ShapeDtypeStruct((rows, width), F32),
-            jax.ShapeDtypeStruct((rows, width), F32),
-            jax.ShapeDtypeStruct((width, hidden), BF16),
-            jax.ShapeDtypeStruct((hidden, width), BF16),
-            jax.ShapeDtypeStruct((1, hidden), F32),
-        ],
-        scratch_shapes=[pltpu.VMEM((rows, block), BF16), pltpu.VMEM((rows, block), BF16)],
-        compiler_params=params(),
-        cost_estimate=cost(12 * rows * width * hidden, 20 * rows * width, 2 * rows * hidden),
-        name="feed",
-    )(mid, grads, w_up, b_up, w_down)
-
-
-def branch_kernel(
-    resid_ref, sum1_ref, sum2_ref, gmid1_ref, gmid2_ref, grad_ref, gain_ref, bdown_ref, w_ref,
-    att_ref, out_ref, gresid_ref, gatt_ref, dw_own_ref, dw_other_ref, small_ref, acc_ref,
-):
-    @pl.when(pl.program_id(0) == 0)
-    def _():
-        acc_ref[...] = jnp.zeros_like(acc_ref)
-        small_ref[...] = jnp.zeros_like(small_ref)
-
-    resid = resid_ref[...]
-    grads = grad_ref[...].astype(F32)
-    out_ref[...] = (resid + sum1_ref[...] + sum2_ref[...] + bdown_ref[...]).astype(BF16)
-    gmid = gmid1_ref[...] + gmid2_ref[...]
-    hat, inv = norm_parts(resid)
-    gresid = grads + norm_back(hat, inv, gmid * gain_ref[...])
-    gresid_ref[...] = gresid
-    branch = gresid.astype(BF16)
-    gatt_ref[...] = contract(w_ref[...], branch, 1, 1).astype(BF16)
-    acc_ref[...] += contract(branch, att_ref[...], 0, 1)
-    small_ref[0:1] += jnp.sum(gmid * hat, axis=0, keepdims=True)
-    small_ref[1:2] += jnp.sum(gmid, axis=0, keepdims=True)
-    small_ref[2:3] += jnp.sum(gresid, axis=0, keepdims=True)
-    small_ref[3:4] += jnp.sum(grads, axis=0, keepdims=True)
-
-    @pl.when(pl.program_id(0) == pl.num_programs(0) - 1)
+    def loads(at):
+        up, down = (up2_hbm, down2_hbm) if at < blocks else (up_hbm, down_hbm)
+        i, slot = at % blocks, at % 2
+        return [
+            pltpu.make_async_copy(cut(up, i), up_ref.at[slot], load_sem.at[slot, 0]),
+            pltpu.make_async_copy(
+                take(down, i, HIDDEN_BLOCK), down_ref.at[slot], load_sem.at[slot, 1]
+            ),
+        ]
+
+    def stores(i):
+        return [
+            pltpu.make_async_copy(dup_ref.at[i], cut(dup_hbm, i), store_sem.at[i, 0]),
+            pltpu.make_async_copy(
+                ddown_ref.at[i], take(ddown_hbm, i, HIDDEN_BLOCK), store_sem.at[i, 1]
+            ),
+        ]
+
+    for at in range(2 * blocks + 1):
+
+        @pl.when(step == at)
+        def _(at=at):
+            if at == 0:
+                for copy in loads(0):
+                    copy.start()
+                place.greet()
+                sum_ref[...] = jnp.zeros_like(sum_ref)
+                gmid_ref[...] = jnp.zeros_like(gmid_ref)
+            if at < 2 * blocks:
+                for copy in loads(at):
+                    copy.wait()
+            if at + 1 < 2 * blocks:
+                for copy in loads(at + 1):
+                    copy.start()
+            if 2 <= at < blocks + 2:
+                for one in terms[at - 2]:
+                    one.to_partner()
+            if 1 <= at < blocks + 1:
+                for one in terms[at - 1]:
+                    one.begin()
+            if at > blocks:
+                for copy in stores(at - blocks - 1):
+                    copy.start()
+            if at == 2 * blocks:
+                acc_ref[...] = jnp.zeros_like(acc_ref)
+                small_ref[...] = jnp.zeros_like(small_ref)
+
+    @pl.when(step < 2 * blocks)
+    def _():
+        up, down, bias = up_ref[step % 2], down_ref[step % 2], bias_ref[0]
+
+        def products(at):
+            here = slice(at, at + MID_CHUNK)
+            return (
+                contract(mid_ref[here], up, 1, 0) + bias,
+                contract(grad_ref[here], down, 1, 1),
+            )
+
+        now = products(0)
+        db = None
+        for at in range(0, rows, MID_CHUNK):
+            here = slice(at, at + MID_CHUNK)
+            later = products(at + MID_CHUNK) if at + MID_CHUNK < rows else None
+            value, slope = gelu_and_slope(now[0])
+            act = value.astype(BF16)
+            gpre = (slope * now[1]).astype(BF16)
+            act_ref[here] = act
+            gpre_ref[here] = gpre
+            term = jnp.sum(gpre.astype(F32), axis=0, keepdims=True)
+            db = term if db is None else db + term
+            sum_ref[here] += contract(act, down, 1, 0)
+            gmid_ref[here] += contract(gpre, up, 1, 1)
+            now = later
+        db_ref[0] = db
+        slot = lax.rem(step, blocks)
+        ddown_ref[slot] = contract(act_ref[...], grad_ref[...], 0, 0).astype(BF16)
+        dup_ref[slot] = contract(mid_ref[...], gpre_ref[...], 0, 0).astype(BF16)
+
+    @pl.when(step >= 2 * blocks)
+    def _():
+        start = (step - 2 * blocks) * MID_BLOCK
+        here = pl.ds(pl.multiple_of(start, MID_BLOCK), MID_BLOCK)
+        resid = resid_ref[...]
+        grads = grad_ref[here, :].astype(F32)
+        out_ref[...] = (resid + sum_ref[here, :] + bdown_ref[...]).astype(BF16)
+        gmid = gmid_ref[here, :]
+        hat, inv = norm_parts(resid)
+        gresid = grads + norm_back(hat, inv, gmid * gain_ref[...])
+        gresid_ref[...] = gresid
+        branch = gresid.astype(BF16)
+        gatt_ref[...] = contract(w_ref[...], branch, 1, 1).astype(BF16)
+        acc_ref[...] += contract(branch, att_ref[...], 0, 1)
+        small_ref[0:1] += jnp.sum(gmid * hat, axis=0, keepdims=True)
+        small_ref[1:2] += jnp.sum(gmid, axis=0, keepdims=True)
+        small_ref[2:3] += jnp.sum(gresid, axis=0, keepdims=True)
+        small_ref[3:4] += jnp.sum(grads, axis=0, keepdims=True)
+
+    @pl.when(step == pl.num_programs(0) - 1)
     def _():
         half = dw_own_ref.shape[1]
         dw_own_ref[...] = acc_ref[:, :half].astype(BF16)
         dw_other_ref[...] = acc_ref[:, half:].astype(BF16)
-
-
-def branch(resid, sums, gmids, grads, gain, b_down, w_out, attended, block):
-    rows, width = resid.shape
+        for i in range(blocks):
+            for copy in stores(i):
+                copy.wait()
+            for one in terms[i]:
+                one.end()
+
+
+def mid_part(mid, grads, biases, resid, gain, b_down, w_out, attended, up2, up, down2, down):
+    rows, width = mid.shape
+    hidden = up.shape[1]
+    blocks = hidden // HIDDEN_BLOCK
+    first = 2 * blocks
     heads_width = attended.shape[0]
-    by_row = pl.BlockSpec((block, width), lambda i: (i, 0))
-    columns = pl.BlockSpec((heads_width, block), lambda i: (0, i))
+    anywhere = pl.BlockSpec(memory_space=pl.ANY)
+    once = lambda shape: pl.BlockSpec(
+        shape, lambda *_: (0,) * len(shape), pipeline_mode=pl.Buffered(1)
+    )
+    row_step = lambda s: jnp.maximum(s - first, 0)
+    by_row = pl.BlockSpec((MID_BLOCK, width), lambda s: (row_step(s), 0))
+    columns = pl.BlockSpec((heads_width, MID_BLOCK), lambda s: (0, row_step(s)))
+    by_hidden = pl.BlockSpec((1, 1, HIDDEN_BLOCK), lambda s: (jnp.minimum(s, first - 1), 0, 0))
     half = (width, heads_width // 2)
+    scratch = [
+        pltpu.VMEM((rows, width), F32),
+        pltpu.VMEM((rows, width), F32),
+        pltpu.VMEM((rows, HIDDEN_BLOCK), BF16),
+        pltpu.VMEM((rows, HIDDEN_BLOCK), BF16),
+        pltpu.VMEM((2, width, HIDDEN_BLOCK), BF16),
+        pltpu.VMEM((2, HIDDEN_BLOCK, width), BF16),
+        pltpu.VMEM((blocks, width, HIDDEN_BLOCK), BF16),
+        pltpu.VMEM((blocks, HIDDEN_BLOCK, width), BF16),
+        pltpu.VMEM((width, heads_width), F32),
+        pltpu.SemaphoreType.DMA((2, 2)),
+        pltpu.SemaphoreType.DMA((blocks, 2)),
+    ]
+    for _ in range(blocks):
+        scratch += PartnerTerm.buffers(width, HIDDEN_BLOCK)
+        scratch += PartnerTerm.buffers(HIDDEN_BLOCK, width)
     return pl.pallas_call(
-        branch_kernel,
-        grid=(rows // block,),
-        in_specs=[by_row] * 6
-        + [whole((1, width)), whole((1, width)), whole((heads_width, width)), columns],
-        out_specs=[by_row, by_row, columns, whole(half), whole(half), whole((8, width))],
+        functools.partial(mid_kernel, blocks=blocks),
+        grid=(first + rows // MID_BLOCK,),
+        in_specs=[
+            once((rows, width)), once((rows, width)), by_hidden, by_row, whole((1, width)),
+            whole((1, width)), once((heads_width, width)), columns,
+        ]
+        + [anywhere] * 4,
+        out_specs=[
+            by_row, by_row, columns, whole(half), whole(half), whole((8, width)), by_hidden,
+        ]
+        + [anywhere] * 4,
         out_shape=[
             jax.ShapeDtypeStruct((rows, width), BF16),
             jax.ShapeDtypeStruct((rows, width), F32),
@@ -870,30 +936,41 @@
             jax.ShapeDtypeStruct(half, BF16),
             jax.ShapeDtypeStruct(half, BF16),
             jax.ShapeDtypeStruct((8, width), F32),
+            jax.ShapeDtypeStruct((first, 1, HIDDEN_BLOCK), F32),
+            jax.ShapeDtypeStruct((width, hidden), BF16),
+            jax.ShapeDtypeStruct((hidden, width), BF16),
+            jax.ShapeDtypeStruct((width // 2, hidden), BF16),
+            jax.ShapeDtypeStruct((hidden // 2, width), BF16),
         ],
-        scratch_shapes=[pltpu.VMEM((width, heads_width), F32)],
-        compiler_params=params(),
-        cost_estimate=cost(4 * rows * width * heads_width, 32 * rows * width),
-        name="branch",
-    )(resid, *sums, *gmids, grads, gain, b_down, w_out, attended)
+        scratch_shapes=scratch,
+        compiler_params=pltpu.CompilerParams(
+            vmem_limit_bytes=VMEM_LIMIT, collective_id=2, has_side_effects=True
+        ),
+        cost_estimate=cost(
+            24 * rows * width * hidden + 4 * rows * width * heads_width, 60 * rows * width,
+            4 * rows * hidden,
+        ),
+        name="mid",
+    )(mid, grads, biases, resid, gain, b_down, w_out, attended, up2, up, down2, down)
 
 
 TAIL_BLOCK = 512
 SUM_ACTIONS = ("begin", "along_x", "along_z", "back_along_z", "back_along_x", "back_to_core")
 SUM_STEPS = (
-    (0, 1, 4, 12, 14, 16),
-    (0, 3, 6, 14, 16, 18),
-    (0, 5, 8, 16, 18, 20),
-    (0, 7, 10, 18, 20),
-    (0, 9, 12, 15, 17, 19),
+    (0, 1, 4, 11, 14, 16),
+    (0, 3, 6, 13, 15, 17),
+    (0, 5, 8, 14, 16, 18),
+    (0, 6, 9, 15, 17, 19),
+    (0, 8, 10, 17, 19, 20),
+    (0, 10, 12, 16, 18, 20),
     (None, 17, 19),
     (None, 17, 20),
     (None, 17),
 )
 LAST_ACTIONS = (
-    (7, "along_z"), 0, (5, "back_along_z"), 1, (6, "back_along_z"), (3, "back_to_core"), 2,
-    (7, "back_along_z"), (5, "back_along_x"), (6, "back_along_x"), (7, "back_along_x"),
-    (5, "back_to_core"), (6, "back_to_core"), (7, "back_to_core"),
+    (8, "along_z"), 0, (6, "back_along_z"), 1, (7, "back_along_z"), 2,
+    (8, "back_along_z"), (6, "back_along_x"), (7, "back_along_x"), (8, "back_along_x"),
+    (6, "back_to_core"), (7, "back_to_core"), (8, "back_to_core"),
 )
 
 
@@ -915,7 +992,7 @@
 
     groups = []
     at = 0
-    for count in [9] * 8 + [3, 3, 4]:
+    for count in [9] * 9 + [3, 3, 4]:
         groups.append(scratch[at : at + count])
         at += count
     columns = lambda ref, i: ref.at[:, pl.ds(i * halves, halves)]
@@ -924,7 +1001,7 @@
         PlaneSum(place, columns(up_hbm, i), columns(seen_up, i), columns(gup_hbm, i), groups[i])
         for i in (0, 1)
     ]
-    down_rows = down_hbm.shape[0] // 2
+    down_rows = HIDDEN_BLOCK
     sums += [
         PlaneSum(
             place,
@@ -933,20 +1010,20 @@
             rows_of(gdown_hbm, i, down_rows),
             groups[2 + i],
         )
-        for i in (0, 1)
+        for i in range(3)
     ]
-    sums.append(PlaneSum(place, wout_hbm, None, gout_hbm, groups[4]))
+    sums.append(PlaneSum(place, wout_hbm, None, gout_hbm, groups[5]))
     third = lambda ref, i: ref.at[:, pl.ds(i * half, half)]
     cat_sums = [
         PlaneSum(
             place, third(dw_ref, i), None, third(gcat_hbm, i),
-            (groups[5 + i][0], third(seen_cat, i), *groups[5 + i][2:]),
+            (groups[6 + i][0], third(seen_cat, i), *groups[6 + i][2:]),
         )
         for i in range(3)
     ]
-    cat_term = PartnerTerm(place, dw2_ref, seen_cat, groups[8])
-    out_term = PartnerTerm(place, wout2_ref, groups[4][1], groups[9])
-    small = SmallSum(place, own_small, other_small, groups[10])
+    cat_term = PartnerTerm(place, dw2_ref, seen_cat, groups[9])
+    out_term = PartnerTerm(place, wout2_ref, groups[5][1], groups[10])
+    small = SmallSum(place, own_small, other_small, groups[11])
     theirs = pl.ds(pl.multiple_of((1 - place.rank) * LEN_L, LEN_L), LEN_L)
     out_load = pltpu.make_async_copy(out_hbm.at[theirs], sent_ref, load_sem.at[2])
     out_copy = send_to(sent_ref, got_out, tok_send.at[2], tok_recv.at[2], place.partner())
@@ -1099,38 +1176,62 @@
     def store(which, columns, value):
         d_ref[source, pl.ds(which * half + head_at, HEAD_DIM), columns] = value.astype(BF16)
 
+    work = []
     images = [(0, LEN_L, block)] + [(at, LEN_S, LEN_S) for at in range(LEN_L, rows, LEN_S)]
     for start, count, size in images:
-        every = slice(start, start + count)
-        keys = qkv_ref[0, 1, 0, :, every]
-        values = qkv_ref[0, 2, 0, :, every]
-        ones = jnp.ones((1, count), F32)
-        key_rows = jnp.concatenate(
-            [keys, keys, extra_rows([ones, ones, ones, mask_ref[:, every]], count)], 0
+        work += [(start, count, at, size) for at in range(start, start + count, size)]
+    kept = {}
+
+    def operands(start, count):
+        if start not in kept:
+            every = slice(start, start + count)
+            keys = qkv_ref[0, 1, 0, :, every]
+            values = qkv_ref[0, 2, 0, :, every]
+            ones = jnp.ones((1, count), F32)
+            key_rows = jnp.concatenate(
+                [keys, keys, extra_rows([ones, ones, ones, mask_ref[:, every]], count)], 0
+            )
+            value_rows = jnp.concatenate([values, extra_rows([ones, ones, ones], count)], 0)
+            kept[start] = keys, key_rows, value_rows
+        return kept[start]
+
+    def products(item):
+        start, count, at, size = item
+        here = slice(at, at + size)
+        _, key_rows, value_rows = operands(start, count)
+        query = qkv_ref[0, 0, 0, :, here]
+        grads = gatt_ref[0, 0, :, here]
+        inner = jnp.sum(
+            grads.astype(F32) * att_ref[0, 0, :, here].astype(F32), axis=0, keepdims=True
         )
-        value_rows = jnp.concatenate([values, extra_rows([ones, ones, ones], count)], 0)
-        grad_values = grad_keys = None
-        for at in range(start, start + count, size):
-            here = slice(at, at + size)
-            query = qkv_ref[0, 0, 0, :, here]
-            grads = gatt_ref[0, 0, :, here]
-            inner = jnp.sum(
-                grads.astype(F32) * att_ref[0, 0, :, here].astype(F32), axis=0, keepdims=True
-            )
-            terms = three_terms(-log_ref[0, 0, :, here]) + [jnp.ones((1, size), F32)]
-            query_rows = jnp.concatenate([*scaled_query(query), extra_rows(terms, size)], 0)
-            grad_rows = jnp.concatenate([grads, extra_rows(three_terms(-inner), size)], 0)
-            score = contract(query_rows, key_rows, 0, 0)
-            grad_probs = contract(grad_rows, value_rows, 0, 0)
-            probs = jnp.exp2(score)
-            grad_score = (probs * grad_probs).astype(BF16)
-            part_values = contract(grads, probs.astype(BF16), 1, 0)
-            part_keys = contract(query, grad_score, 1, 0)
-            grad_values = part_values if grad_values is None else grad_values + part_values
-            grad_keys = part_keys if grad_keys is None else grad_keys + part_keys
-            store(0, here, contract(keys, grad_score, 1, 1) * SCALE)
-        store(1, every, grad_keys * SCALE)
-        store(2, every, grad_values)
+        terms = three_terms(-log_ref[0, 0, :, here]) + [jnp.ones((1, size), F32)]
+        query_rows = jnp.concatenate([*scaled_query(query), extra_rows(terms, size)], 0)
+        grad_rows = jnp.concatenate([grads, extra_rows(three_terms(-inner), size)], 0)
+        return contract(query_rows, key_rows, 0, 0), contract(grad_rows, value_rows, 0, 0)
+
+    sums = {}
+    now = products(work[0])
+    for place, item in enumerate(work):
+        later = products(work[place + 1]) if place + 1 < len(work) else None
+        start, count, at, size = item
+        here = slice(at, at + size)
+        keys = operands(start, count)[0]
+        query = qkv_ref[0, 0, 0, :, here]
+        grads = gatt_ref[0, 0, :, here]
+        score, grad_probs = now
+        probs = jnp.exp2(score)
+        grad_score = (probs * grad_probs).astype(BF16)
+        part_values = contract(grads, probs.astype(BF16), 1, 0)
+        part_keys = contract(query, grad_score, 1, 0)
+        store(0, here, contract(keys, grad_score, 1, 1) * SCALE)
+        if start in sums:
+            part_keys, part_values = sums[start][0] + part_keys, sums[start][1] + part_values
+        sums[start] = part_keys, part_values
+        if at + size == start + count:
+            every = slice(start, start + count)
+            store(1, every, part_keys * SCALE)
+            store(2, every, part_values)
+        now = later
 
 
 def tail(
@@ -1151,7 +1252,7 @@
     )
     one = pl.BlockSpec((1, 1, HEAD_DIM, rows), lambda h: (*head(h), 0, 0))
     row = pl.BlockSpec((1, 1, 1, rows), lambda h: (*head(h), 0, 0))
-    sum_shapes = [(width, width)] * 4 + [dwout.shape] + [(width, out // 3)] * 3
+    sum_shapes = [(width, width)] * 2 + [(HIDDEN_BLOCK, width)] * 3 + [dwout.shape] + [(width, out // 3)] * 3
     scratch = [
         pltpu.VMEM((2, out, rows), BF16),
         pltpu.VMEM((rows, width), BF16),
@@ -1212,19 +1313,6 @@
     )
 
 
-def swap_tp(array):
-    return lax.ppermute(array, "tp", [(0, 1), (1, 0)])
-
-
-def swap_dp(array, bit):
-    count = lax.axis_size("dp")
-    return lax.ppermute(array, "dp", [(i, i ^ bit) for i in range(count)])
-
-
-def dp_bit(bit):
-    return (lax.axis_index("dp") & bit) != 0
-
-
 def joined(mine, theirs, second):
     return jnp.where(second, jnp.concatenate([theirs, mine], 0), jnp.concatenate([mine, theirs], 0))
 
@@ -1232,19 +1320,6 @@
 def half_of(array, second):
     size = array.shape[0] // 2
     return lax.dynamic_slice_in_dim(array, jnp.where(second, size, 0), size, 0)
-
-
-def add_low(left, right):
-    return (left.astype(F32) + right.astype(F32)).astype(BF16)
-
-
-def over_cores(other, chunks=1):
-    second = dp_bit(1)
-    split = other.reshape(chunks, other.shape[0] // chunks, other.shape[1])
-    half = split.shape[1] // 2
-    take = lambda which: lax.dynamic_slice_in_dim(split, jnp.where(which, half, 0), half, 1)
-    both = add_low(take(second), swap_dp(take(~second), 1))
-    return both.reshape(-1, other.shape[1])
 
 
 def by_images(
@@ -1279,15 +1354,12 @@
     )
     qkv = qkv.reshape(2, 3, heads, HEAD_DIM, rows)
     attended = att.reshape(2 * half, rows)
-    up_bias = bias[:1, 3 * half :], bias2[:1, 3 * half :]
-    sum2, gmid2, dup2, ddown2, dbup2 = feed(mid, grads, w_up2, up_bias[1], w_down2)
-    mid, both_up, both_down = lax.optimization_barrier((mid, over_cores(dup2), over_cores(ddown2, 2)))
-    seen_up, seen_down = swap_tp(both_up), swap_tp(both_down)
-    sum1, gmid1, dup1, ddown1, dbup1 = feed(mid, grads, w_up, up_bias[0], w_down)
-    out, gresid, gatt, dwout1, dwout2, small2 = branch(
-        resid, (sum1, sum2), (gmid1, gmid2), grads, row(ln2_gain), row(b_down), w_out_all,
-        attended, 512,
-    )
+    up_bias = jnp.concatenate([bias2[:1, 3 * half :], bias[:1, 3 * half :]], 1)
+    (out, gresid, gatt, dwout1, dwout2, small2, db_up, dup1, ddown1, seen_up, seen_down) = mid_part(
+        mid, grads, up_bias.reshape(-1, 1, HIDDEN_BLOCK), resid, row(ln2_gain), row(b_down),
+        w_out_all, attended, w_up2, w_up, w_down2, w_down,
+    )
+    dbup2, dbup1 = db_up.reshape(2, 1, -1)
     gtok, small, got_tok, grad_up, grad_down, grad_out_t, grad_cat, got_out = tail(
         mask, qkv, att, log_total, gatt.reshape(2, heads, HEAD_DIM, rows), row(ln1_gain), small2,
         dbup1, dbup2, dwout2, normed, w_cat, own_tokens, gresid, dup1, ddown1, dwout1,

time: 385 us -> 367 us (0.953)
  local copies, waits for them, and re-layouts: 27.4 us -> 18.7 us
  other arithmetic: 21 us -> 17 us
    pallas_call x3 -> x1, Pallas kernels: 103 us -> 91.7 us  [mid_part(): pl.pallas_call(functools.partial(mid_kernel, blocks=blocks), grid=(first...]
    pallas_call x1, Pallas kernels: 147 us -> 156 us  [tail(): pl.pallas_call(functools.partial(tail_kernel, heads=heads, block=block),...]
  transfers between devices with their start and end apart: 4 -> 0, of which waited for: 1 -> 0; matrix products, arithmetic and copies ran while one was open for 2% -> 0% of each run, Pallas kernels for 16% -> 0%
where the time goes in v4:
time: 367 us; the launch traced here: 361 us
  Pallas kernels  324 us (88%)
  local copies, waits for them, and re-layouts  18.7 us (5%)
  other arithmetic  17 us (5%)
    pallas_call x1, Pallas kernels, tail(): pl.pallas_call(functools.partial(tail_kernel, heads=heads, block=block),...  156 us
    pallas_call x1, Pallas kernels, mid_part(): pl.pallas_call(functools.partial(mid_kernel, blocks=blocks), grid=(first...  91.7 us
    pallas_call x1, Pallas kernels, front(): pl.pallas_call(functools.partial(front_kernel, heads=heads, block=block),...  76 us

profile of v4, /device:TPU:0, one launch (start us, length us, event | category | flops | bytes accessed | tf_op | source)
XLA Modules:
  0.0 360.8 jit_solution(14758158496224090852)
XLA Ops:
  0.7 0.7 dynamic_slice.10
  1.5 1.2 dynamic_slice.9
  2.7 0.6 iota_compare_fusion.1
  4.0 1.3 reshape.203.gain_ref
  5.3 1.3 reshape.209.gain2_ref.gain_ref
  6.5 0.7 maximum_convert_fusion
  7.3 0.6 broadcast_in_dim.21.bias_ref
  7.9 1.3 reshape.205.shift_ref
  9.2 1.3 reshape.207.bout_ref
  10.4 1.3 reshape.211.shift2_ref
  11.7 76.0 %front.1 = (bf16[2048,768]{1,0:T(8,128)(2,1)}, bf16[2,1152,2048]{2,1,0:T(8,128)(2,1)}, bf16[2,8,48,2048]{3,2,1,0:T(8,128)(2,1)}, f32[2,8,1,2048]{3,2,1,0:T(1,128...) custom-call(f32[1,2048]{1,0:T(1,128)} %add_select_fusion.mask_ref, ...), custom_call_target="tpu_custom_call" | custom-call | flops 29930553344 | bytes 62914560 | tf_op jit(solution)/shard_map/front/pallas_call | solution.py:671
  87.7 0.8 slice.47
  89.8 91.7 %mid.1 = (bf16[2048,768]{1,0:T(8,128)(2,1)}, f32[2048,768]{1,0:T(8,128)}, bf16[768,2048]{1,0:T(8,128)(2,1)}, bf16[768,384]{1,0:T(8,128)(2,1)}, bf16[768,384]{1,0...) custom-call(bf16[2048,768]{1,0:T(8,128)(2,1)} %get-tuple-element.52., ...), custom_call_target="tpu_custom_call" | custom-call | flops 62813896704 | bytes 94371840 | tf_op jit(solution)/shard_map/mid/pallas_call | solution.py:920
  181.4 1.3 fusion.2
  182.8 156.5 %tail.1 = (f32[1024,768]{1,0:T(8,128)}, f32[16,768]{1,0:T(8,128)}, bf16[1024,768]{1,0:T(8,128)(2,1)}, bf16[768,1536]{1,0:T(8,128)(2,1)}, bf16[1536,768]{1,0:T(8,...) custom-call(f32[1,2048]{1,0:T(1,128)} %add_select_fusion.mask_ref, ...), custom_call_target="tpu_custom_call" | custom-call | flops 53687091200 | bytes 25165824 | tf_op jit(solution)/shard_map/tail/pallas_call | solution.py:1279
  339.2 1.6 convert_element_type.38
  340.9 5.1 %maximum_select_fusion = f32[2048,768]{1,0:T(8,128)} fusion(f32[1024,768]{1,0:T(8,128)} %get-tuple-element.75, f32[1024,768]{1,0:T(8,128)S(1)} %convert_element_type.38, pred[]{:T(512)S(6)} %eq.3), kind=kLoop, calls=%fused_computation | loop fusion | flops 4718592 | bytes 12582913 | tf_op jit(solution)/shard_map/jit(_where)/select_n | solution.py:1317
  346.0 2.8 convert_element_type.42
  348.8 2.5 convert_element_type.43
  351.4 1.9 fusion.1
  353.3 1.6 constant_dynamic-slice_fusion
  355.1 2.1 maximum_select_fusion.1
  357.3 1.4 copy.36
  358.7 0.6 slice_reduce_fusion
  (28 shorter events, 3.5 us)
Async XLA Ops:
  11.7 76.9 %copy-start.5 = (bf16[1536]{0:T(1024)(128)(2,1)S(1)}, bf16[1536]{0:T(1024)(128)(2,1)}, u32[]{:S(2)}) copy-start(bf16[1536]{0:T(1024)(128)(2,1)} %param.34) | copy-start | bytes 9220
  11.7 77.5 %copy-start.7 = (bf16[768]{0:T(1024)(128)(2,1)S(1)}, bf16[768]{0:T(1024)(128)(2,1)}, u32[]{:S(2)}) copy-start(bf16[768]{0:T(1024)(128)(2,1)} %param.36) | copy-start | bytes 4612
  340.9 5.1 %copy-start.2 = (bf16[768,1536]{1,0:T(8,128)(2,1)S(1)}, bf16[768,1536]{1,0:T(8,128)(2,1)}, u32[]{:S(2)}) copy-start(bf16[768,1536]{1,0:T(8,128)(2,1)} %get-tuple-element.79) | copy-start | bytes 7077892
  346.0 2.8 copy-start.1
  348.8 2.5 copy-start
  353.3 1.9 copy-start.3
  355.1 2.1 copy-start.4
  357.2 1.5 copy-start.6

commit v5 on v4

--- a/solution.py
+++ b/solution.py
@@ -224,10 +224,17 @@
         there = part(self.out, self.place.core * count, count)
         return pltpu.make_async_copy(self.whole, there, self.local.at[3])
 
+    def begin_own(self):
+        self.core_copy().start()
+        self.local_copies()[0].start()
+
+    def begin_seen(self):
+        for copy in self.local_copies()[1:]:
+            copy.start()
+
     def begin(self):
-        self.core_copy().start()
-        for copy in self.local_copies():
-            copy.start()
+        self.begin_own()
+        self.begin_seen()
 
     def along_x(self):
         self.core_copy().wait()
@@ -310,16 +317,17 @@
 class SmallSum:
     ROWS = 16
 
-    def __init__(self, place, own, other, refs):
-        self.place, self.own, self.other = place, own, other
-        self.sums, self.got, self.send, self.recv = refs
+    def __init__(self, place, pair, refs):
+        self.place, self.pair = place, pair
+        self.sums, self.got, self.got_own, self.send, self.recv = refs
 
     @staticmethod
     def buffers(width):
         rows = SmallSum.ROWS
         return [
-            pltpu.VMEM((3, rows, width), F32),
-            pltpu.VMEM((6, rows, width), F32),
+            pltpu.VMEM((3, 2, rows, width), F32),
+            pltpu.VMEM((5, 2, rows, width), F32),
+            pltpu.VMEM((rows, width), F32),
             pltpu.SemaphoreType.DMA((6,)),
             pltpu.SemaphoreType.DMA((6,)),
         ]
@@ -327,43 +335,46 @@
     def copy(self, source, place, device):
         return send_to(source, self.got.at[place], self.send.at[place], self.recv.at[place], device)
 
-    def partner_copy(self):
-        return self.copy(self.other, 0, self.place.partner())
-
     def core_copy(self):
-        return self.copy(self.sums.at[0], 1, self.place.across_core())
+        return self.copy(self.pair, 0, self.place.across_core())
 
     def x_copy(self):
-        return self.copy(self.sums.at[1], 2, self.place.across_x())
+        return self.copy(self.sums.at[0], 1, self.place.across_x())
 
     def z_copies(self):
         return [
-            self.copy(self.sums.at[2], 2 + step, self.place.along_z(step)) for step in (1, 2, 3)
+            self.copy(self.sums.at[1], 1 + step, self.place.along_z(step)) for step in (1, 2, 3)
         ]
 
+    def partner_copy(self):
+        return send_to(
+            self.sums.at[2, 1], self.got_own, self.send.at[5], self.recv.at[5],
+            self.place.partner(),
+        )
+
     def begin(self):
-        self.partner_copy().start()
-
-    def over_cores(self):
-        self.partner_copy().wait()
-        self.sums[0] = self.own[...] + self.got[0]
         self.core_copy().start()
 
     def over_x(self):
         self.core_copy().wait()
-        self.sums[1] = self.sums[0] + self.got[1]
+        self.sums[0] = self.pair[...] + self.got[0]
         self.x_copy().start()
 
     def over_z(self):
         self.x_copy().wait()
-        self.sums[2] = self.sums[1] + self.got[2]
+        self.sums[1] = self.sums[0] + self.got[1]
         for copy in self.z_copies():
             copy.start()
 
-    def end(self):
+    def over_tp(self):
         for copy in self.z_copies():
             copy.wait()
-        return self.sums[2] + self.got[3] + self.got[4] + self.got[5]
+        self.sums[2] = self.sums[1] + self.got[2] + self.got[3] + self.got[4]
+        self.partner_copy().start()
+
+    def end(self):
+        self.partner_copy().wait()
+        return self.sums[2, 0] + self.got_own[...]
 
 
 class Fetch:
@@ -430,8 +441,7 @@
 
 
 def front_kernel(
-    mask_ref, gain_ref, shift_ref, bout_ref, gain2_ref, shift2_ref, bias_ref,
-    tok_hbm, wq_hbm, wk_hbm, wv_hbm, wout_hbm, wup_hbm, wdown_hbm, cot_hbm,
+    mask_ref, vec_ref, bias_ref, tok_hbm, wq_hbm, wk_hbm, wv_hbm, wout_hbm, wup_hbm, wdown_hbm, cot_hbm,
     x_out, qkv_out, att_out, log_out, resid_out, mid_out,
     cat_hbm, wout_all_hbm, up2_hbm, down2_hbm, grads_hbm, bias2_hbm, tok_out,
     tok_ref, x_ref, qkv_ref, att_ref, cat_ref, wout_ref, bias2_ref, up2_ref, down2_ref, grads_ref,
@@ -439,6 +449,9 @@
 ):
     step = pl.program_id(0)
     place = Place()
+    gain_ref, shift_ref, bout_ref, gain2_ref, shift2_ref = (
+        vec_ref.at[pl.ds(i, 1)] for i in range(5)
+    )
     half = heads * HEAD_DIM
     rows = tok_ref.shape[0]
     blocks = rows // FRONT_BLOCK
@@ -643,8 +656,8 @@
 
 
 def front(
-    mask, gain, shift, b_out, gain2, shift2, bias, tokens, w_query, w_key, w_value, w_out, w_up,
-    w_down, cotangent, heads, block=1024,
+    mask, vectors, bias, tokens, w_query, w_key, w_value, w_out, w_up, w_down, cotangent, heads,
+    block=1024,
 ):
     width = tokens.shape[1]
     rows = tokens.shape[0] // 2
@@ -673,7 +686,7 @@
         grid=(base[4] + blocks,),
         in_specs=[
             whole((1, rows)),
-            *(whole((1, width)) for _ in range(5)),
+            whole((8, width)),
             whole(bias.shape),
         ]
         + [anywhere] * 8,
@@ -726,8 +739,7 @@
         ),
         name="front",
     )(
-        mask, gain, shift, b_out, gain2, shift2, bias, tokens, w_query, w_key, w_value, w_out,
-        w_up, w_down, cotangent,
+        mask, vectors, bias, tokens, w_query, w_key, w_value, w_out, w_up, w_down, cotangent,
     )
 
 
@@ -749,14 +761,16 @@
 
 HIDDEN_BLOCK = 512
 MID_BLOCK = 512
+HIDDEN_ORDER = ((1, 0), (0, 0), (1, 1), (1, 2), (0, 1), (0, 2))
+SLOTS = 4
 MID_CHUNK = 512
 
 
 def mid_kernel(
-    mid_ref, grad_ref, bias_ref, resid_ref, gain_ref, bdown_ref, w_ref, att_ref,
+    mid_ref, grad_ref, bias_ref, resid_ref, vec_ref, w_ref, att_ref,
     up2_hbm, up_hbm, down2_hbm, down_hbm,
     out_ref, gresid_ref, gatt_ref, dw_own_ref, dw_other_ref, small_ref, db_ref,
-    dup_hbm, ddown_hbm, seen_up, seen_down,
+    dup_hbm, ddown_hbm, seen_up, seen_down, gup_hbm, gdown_hbm,
     sum_ref, gmid_ref, act_ref, gpre_ref, up_ref, down_ref, dup_ref, ddown_ref, acc_ref,
     load_sem, store_sem, *scratch, blocks,
 ):
@@ -768,18 +782,30 @@
     terms = []
     for i in range(blocks):
         refs = [scratch[6 * i : 6 * i + 3], scratch[6 * i + 3 : 6 * i + 6]]
+        slot = HIDDEN_ORDER.index((1, i)) % SLOTS
         terms.append(
             (
-                PartnerTerm(place, dup_ref.at[i], cut(seen_up, i), refs[0]),
+                PartnerTerm(place, dup_ref.at[slot], cut(seen_up, i), refs[0]),
                 PartnerTerm(
-                    place, ddown_ref.at[i], take(seen_down, i, HIDDEN_BLOCK // 2), refs[1]
+                    place, ddown_ref.at[slot], take(seen_down, i, HIDDEN_BLOCK // 2), refs[1]
                 ),
             )
         )
 
+    first_sums = [
+        PlaneSum(
+            place, dup_ref.at[1], cut(seen_up, 0), gup_hbm, scratch[6 * blocks : 6 * blocks + 9]
+        ),
+        PlaneSum(
+            place, ddown_ref.at[1], take(seen_down, 0, HIDDEN_BLOCK // 2), gdown_hbm,
+            scratch[6 * blocks + 9 :],
+        ),
+    ]
+
     def loads(at):
-        up, down = (up2_hbm, down2_hbm) if at < blocks else (up_hbm, down_hbm)
-        i, slot = at % blocks, at % 2
+        side, i = HIDDEN_ORDER[at]
+        up, down = (up2_hbm, down2_hbm) if side else (up_hbm, down_hbm)
+        slot = at % 2
         return [
             pltpu.make_async_copy(cut(up, i), up_ref.at[slot], load_sem.at[slot, 0]),
             pltpu.make_async_copy(
@@ -788,12 +814,16 @@
         ]
 
     def stores(i):
+        slot = HIDDEN_ORDER.index((0, i)) % SLOTS
         return [
-            pltpu.make_async_copy(dup_ref.at[i], cut(dup_hbm, i), store_sem.at[i, 0]),
+            pltpu.make_async_copy(dup_ref.at[slot], cut(dup_hbm, i), store_sem.at[i, 0]),
             pltpu.make_async_copy(
-                ddown_ref.at[i], take(ddown_hbm, i, HIDDEN_BLOCK), store_sem.at[i, 1]
+                ddown_ref.at[slot], take(ddown_hbm, i, HIDDEN_BLOCK), store_sem.at[i, 1]
             ),
         ]
+
+    to_core = {3: terms[1], 4: terms[2]}
+    to_partner = {1: terms[0], 4: terms[1], 5: terms[2]}
 
     for at in range(2 * blocks + 1):
 
@@ -811,15 +841,32 @@
             if at + 1 < 2 * blocks:
                 for copy in loads(at + 1):
                     copy.start()
-            if 2 <= at < blocks + 2:
-                for one in terms[at - 2]:
-                    one.to_partner()
-            if 1 <= at < blocks + 1:
-                for one in terms[at - 1]:
-                    one.begin()
-            if at > blocks:
-                for copy in stores(at - blocks - 1):
+            for one in to_partner.get(at, ()):
+                one.to_partner()
+            for one in to_core.get(at, ()):
+                one.begin()
+            if at >= 1 and HIDDEN_ORDER[at - 1] in ((0, 1), (0, 2)):
+                for copy in stores(HIDDEN_ORDER[at - 1][1]):
                     copy.start()
+            if at == 2:
+                for one in first_sums:
+                    one.begin_own()
+            if at == 3:
+                for one in terms[0]:
+                    one.end()
+                for one in first_sums:
+                    one.begin_seen()
+                for one in first_sums:
+                    one.along_x()
+            if at == 4:
+                for one in first_sums:
+                    one.along_z()
+            if at == 5:
+                for one in first_sums:
+                    one.back_along_z()
+            if at == 6:
+                for one in first_sums:
+                    one.back_along_x()
             if at == 2 * blocks:
                 acc_ref[...] = jnp.zeros_like(acc_ref)
                 small_ref[...] = jnp.zeros_like(small_ref)
@@ -851,9 +898,14 @@
             gmid_ref[here] += contract(gpre, up, 1, 1)
             now = later
         db_ref[0] = db
-        slot = lax.rem(step, blocks)
+        slot = lax.rem(step, SLOTS)
         ddown_ref[slot] = contract(act_ref[...], grad_ref[...], 0, 0).astype(BF16)
         dup_ref[slot] = contract(mid_ref[...], gpre_ref[...], 0, 0).astype(BF16)
+
+    @pl.when(step == 0)
+    def _():
+        for one in terms[0]:
+            one.begin()
 
     @pl.when(step >= 2 * blocks)
     def _():
@@ -861,10 +913,10 @@
         here = pl.ds(pl.multiple_of(start, MID_BLOCK), MID_BLOCK)
         resid = resid_ref[...]
         grads = grad_ref[here, :].astype(F32)
-        out_ref[...] = (resid + sum_ref[here, :] + bdown_ref[...]).astype(BF16)
+        out_ref[...] = (resid + sum_ref[here, :] + vec_ref[5:6]).astype(BF16)
         gmid = gmid_ref[here, :]
         hat, inv = norm_parts(resid)
-        gresid = grads + norm_back(hat, inv, gmid * gain_ref[...])
+        gresid = grads + norm_back(hat, inv, gmid * vec_ref[3:4])
         gresid_ref[...] = gresid
         branch = gresid.astype(BF16)
         gatt_ref[...] = contract(w_ref[...], branch, 1, 1).astype(BF16)
@@ -876,17 +928,21 @@
 
     @pl.when(step == pl.num_programs(0) - 1)
     def _():
+        for one in first_sums:
+            one.back_to_core()
         half = dw_own_ref.shape[1]
         dw_own_ref[...] = acc_ref[:, :half].astype(BF16)
         dw_other_ref[...] = acc_ref[:, half:].astype(BF16)
-        for i in range(blocks):
+        for i in range(1, blocks):
             for copy in stores(i):
                 copy.wait()
             for one in terms[i]:
                 one.end()
-
-
-def mid_part(mid, grads, biases, resid, gain, b_down, w_out, attended, up2, up, down2, down):
+        for one in first_sums:
+            one.end()
+
+
+def mid_part(mid, grads, biases, resid, vectors, w_out, attended, up2, up, down2, down):
     rows, width = mid.shape
     hidden = up.shape[1]
     blocks = hidden // HIDDEN_BLOCK
@@ -908,8 +964,8 @@
         pltpu.VMEM((rows, HIDDEN_BLOCK), BF16),
         pltpu.VMEM((2, width, HIDDEN_BLOCK), BF16),
         pltpu.VMEM((2, HIDDEN_BLOCK, width), BF16),
-        pltpu.VMEM((blocks, width, HIDDEN_BLOCK), BF16),
-        pltpu.VMEM((blocks, HIDDEN_BLOCK, width), BF16),
+        pltpu.VMEM((SLOTS, width, HIDDEN_BLOCK), BF16),
+        pltpu.VMEM((SLOTS, HIDDEN_BLOCK, width), BF16),
         pltpu.VMEM((width, heads_width), F32),
         pltpu.SemaphoreType.DMA((2, 2)),
         pltpu.SemaphoreType.DMA((blocks, 2)),
@@ -917,18 +973,19 @@
     for _ in range(blocks):
         scratch += PartnerTerm.buffers(width, HIDDEN_BLOCK)
         scratch += PartnerTerm.buffers(HIDDEN_BLOCK, width)
+    scratch += PlaneSum.buffers(width, HIDDEN_BLOCK) + PlaneSum.buffers(HIDDEN_BLOCK, width)
     return pl.pallas_call(
         functools.partial(mid_kernel, blocks=blocks),
         grid=(first + rows // MID_BLOCK,),
         in_specs=[
-            once((rows, width)), once((rows, width)), by_hidden, by_row, whole((1, width)),
-            whole((1, width)), once((heads_width, width)), columns,
+            once((rows, width)), once((rows, width)), by_hidden, by_row, whole((8, width)),
+            once((heads_width, width)), columns,
         ]
         + [anywhere] * 4,
         out_specs=[
             by_row, by_row, columns, whole(half), whole(half), whole((8, width)), by_hidden,
         ]
-        + [anywhere] * 4,
+        + [anywhere] * 6,
         out_shape=[
             jax.ShapeDtypeStruct((rows, width), BF16),
             jax.ShapeDtypeStruct((rows, width), F32),
@@ -941,6 +998,8 @@
             jax.ShapeDtypeStruct((hidden, width), BF16),
             jax.ShapeDtypeStruct((width // 2, hidden), BF16),
             jax.ShapeDtypeStruct((hidden // 2, width), BF16),
+            jax.ShapeDtypeStruct((width, HIDDEN_BLOCK), BF16),
+            jax.ShapeDtypeStruct((HIDDEN_BLOCK, width), BF16),
         ],
         scratch_shapes=scratch,
         compiler_params=pltpu.CompilerParams(
@@ -951,36 +1010,35 @@
             4 * rows * hidden,
         ),
         name="mid",
-    )(mid, grads, biases, resid, gain, b_down, w_out, attended, up2, up, down2, down)
+    )(mid, grads, biases, resid, vectors, w_out, attended, up2, up, down2, down)
 
 
 TAIL_BLOCK = 512
 SUM_ACTIONS = ("begin", "along_x", "along_z", "back_along_z", "back_along_x", "back_to_core")
 SUM_STEPS = (
-    (0, 1, 4, 11, 14, 16),
-    (0, 3, 6, 13, 15, 17),
-    (0, 5, 8, 14, 16, 18),
-    (0, 6, 9, 15, 17, 19),
-    (0, 8, 10, 17, 19, 20),
-    (0, 10, 12, 16, 18, 20),
+    (0, 1, 3, 6, 9, 11),
+    (0, 2, 5, 8, 11, 13),
+    (0, 4, 6, 10, 13, 15),
+    (0, 5, 8, 12, 14, 16),
+    (0, 8, 10, 13, 15, 17),
     (None, 17, 19),
     (None, 17, 20),
     (None, 17),
 )
 LAST_ACTIONS = (
-    (8, "along_z"), 0, (6, "back_along_z"), 1, (7, "back_along_z"), 2,
-    (8, "back_along_z"), (6, "back_along_x"), (7, "back_along_x"), (8, "back_along_x"),
-    (6, "back_to_core"), (7, "back_to_core"), (8, "back_to_core"),
+    (7, "along_z"), 0, (5, "back_along_z"), 1, (6, "back_along_z"), 2,
+    (7, "back_along_z"), (5, "back_along_x"), (6, "back_along_x"), (7, "back_along_x"),
+    (5, "back_to_core"), (6, "back_to_core"), (7, "back_to_core"),
 )
 
 
 def tail_kernel(
-    mask_ref, qkv_ref, att_ref, log_ref, gatt_ref, gain_ref, small2_ref, dbup1_ref, dbup2_ref,
+    mask_ref, qkv_ref, att_ref, log_ref, gatt_ref, vec_ref, small2_ref, dbup1_ref, dbup2_ref,
     wout2_ref, x_hbm, w_hbm, tok_hbm, gresid_hbm, up_hbm, down_hbm, wout_hbm, seen_up,
     seen_down, out_hbm,
     gtok_ref, small_ref, got_hbm, gup_hbm, gdown_hbm, gout_hbm, gcat_hbm, got_out,
-    d_ref, x_ref, w_ref, tok_ref, gresid_ref, dw_ref, dw2_ref, seen_cat, sent_ref, own_small,
-    other_small, load_sem, row_sem, tok_send, tok_recv, *scratch, heads, block,
+    d_ref, x_ref, w_ref, tok_ref, gresid_ref, dw_ref, dw2_ref, seen_cat, sent_ref, pair_ref,
+    load_sem, row_sem, tok_send, tok_recv, *scratch, heads, block,
 ):
     step = pl.program_id(0)
     place = Place()
@@ -988,31 +1046,29 @@
     last_step = first_rows + 3
     width = x_ref.shape[1]
     half = heads * HEAD_DIM
-    halves = width
 
     groups = []
     at = 0
-    for count in [9] * 9 + [3, 3, 4]:
+    for count in [9] * 5 + [0] + [9] * 3 + [3, 3, 5]:
         groups.append(scratch[at : at + count])
         at += count
-    columns = lambda ref, i: ref.at[:, pl.ds(i * halves, halves)]
+    columns = lambda ref, i: ref.at[:, pl.ds(i * HIDDEN_BLOCK, HIDDEN_BLOCK)]
     rows_of = lambda ref, i, count: ref.at[pl.ds(i * count, count)]
     sums = [
-        PlaneSum(place, columns(up_hbm, i), columns(seen_up, i), columns(gup_hbm, i), groups[i])
-        for i in (0, 1)
+        PlaneSum(place, columns(up_hbm, i), columns(seen_up, i), columns(gup_hbm, i - 1), groups[i])
+        for i in (1, 2)
     ]
-    down_rows = HIDDEN_BLOCK
     sums += [
         PlaneSum(
             place,
-            rows_of(down_hbm, i, down_rows),
-            rows_of(seen_down, i, down_rows // 2),
-            rows_of(gdown_hbm, i, down_rows),
+            rows_of(down_hbm, i, HIDDEN_BLOCK),
+            rows_of(seen_down, i, HIDDEN_BLOCK // 2),
+            rows_of(gdown_hbm, i - 1, HIDDEN_BLOCK),
             groups[2 + i],
         )
-        for i in range(3)
+        for i in (1, 2)
     ]
-    sums.append(PlaneSum(place, wout_hbm, None, gout_hbm, groups[5]))
+    sums.append(PlaneSum(place, wout_hbm, None, gout_hbm, groups[0]))
     third = lambda ref, i: ref.at[:, pl.ds(i * half, half)]
     cat_sums = [
         PlaneSum(
@@ -1022,11 +1078,19 @@
         for i in range(3)
     ]
     cat_term = PartnerTerm(place, dw2_ref, seen_cat, groups[9])
-    out_term = PartnerTerm(place, wout2_ref, groups[5][1], groups[10])
-    small = SmallSum(place, own_small, other_small, groups[11])
+    out_term = PartnerTerm(place, wout2_ref, groups[0][1], groups[10])
+    own_small, other_small = pair_ref.at[0], pair_ref.at[1]
+    small = SmallSum(place, pair_ref, groups[11])
     theirs = pl.ds(pl.multiple_of((1 - place.rank) * LEN_L, LEN_L), LEN_L)
     out_load = pltpu.make_async_copy(out_hbm.at[theirs], sent_ref, load_sem.at[2])
-    out_copy = send_to(sent_ref, got_out, tok_send.at[2], tok_recv.at[2], place.partner())
+    piece = LEN_L // 4
+    out_copies = [
+        send_to(
+            sent_ref.at[pl.ds(i * piece, piece)], got_out.at[pl.ds(i * piece, piece)],
+            tok_send.at[2 + i], tok_recv.at[2 + i], place.partner(),
+        )
+        for i in range(4)
+    ]
 
     loads = [
         pltpu.make_async_copy(x_hbm, x_ref, load_sem.at[0]),
@@ -1081,8 +1145,13 @@
             if when == 1:
                 out_term.to_partner()
                 out_load.wait()
-                out_copy.start()
-            if when == 4:
+                out_copies[0].start()
+                out_copies[1].start()
+            if when == 3:
+                out_copies[2].start()
+            if when == 13:
+                out_copies[3].start()
+            if when == 8:
                 out_term.end()
             for action in events[when]:
                 action()
@@ -1116,7 +1185,6 @@
         for copy in row_loads(0):
             copy.start()
         cat_term.end()
-        out_copy.wait()
         for i in range(3):
             weight_gradient(0, dw_ref, i)
             cat_sums[i].begin()
@@ -1129,6 +1197,9 @@
         def _(i=i):
             for copy in row_loads(i):
                 copy.wait()
+            if i == 0:
+                for copy in out_copies:
+                    copy.wait()
             if i < 3:
                 for copy in row_loads(i + 1):
                     copy.start()
@@ -1136,7 +1207,7 @@
             gin = contract(d_ref[0, :, here], w_ref[0], 0, 1)
             gin += contract(d_ref[1, :, here], w_ref[1], 0, 1)
             hat, inv = norm_parts(tok_ref[i % 2].astype(F32))
-            gtok = gresid_ref[i % 2] + norm_back(hat, inv, gin * gain_ref[...])
+            gtok = gresid_ref[i % 2] + norm_back(hat, inv, gin * vec_ref[0:1])
             own_small[0:1] += jnp.sum(gin * hat, axis=0, keepdims=True)
             own_small[1:2] += jnp.sum(gin, axis=0, keepdims=True)
             if i < 2:
@@ -1154,7 +1225,7 @@
             own_small[6 + i : 7 + i] = dbup1_ref[:, pl.ds(i * width, width)]
             other_small[6 + i : 7 + i] = dbup2_ref[:, pl.ds(i * width, width)]
         small.begin()
-        small_actions = (small.over_cores, small.over_x, small.over_z)
+        small_actions = (small.over_x, small.over_z, small.over_tp)
         for item in LAST_ACTIONS:
             if isinstance(item, int):
                 small_actions[item]()
@@ -1235,7 +1306,7 @@
 
 
 def tail(
-    mask, qkv, att, log_total, gatt, gain, small2, dbup1, dbup2, dwout2, normed, w_cat,
+    mask, qkv, att, log_total, gatt, vectors, small2, dbup1, dbup2, dwout2, normed, w_cat,
     tokens, gresid, dup, ddown, dwout, seen_up, seen_down, out_rows, block=256,
 ):
     _, _, heads, _, rows = qkv.shape
@@ -1252,7 +1323,7 @@
     )
     one = pl.BlockSpec((1, 1, HEAD_DIM, rows), lambda h: (*head(h), 0, 0))
     row = pl.BlockSpec((1, 1, 1, rows), lambda h: (*head(h), 0, 0))
-    sum_shapes = [(width, width)] * 2 + [(HIDDEN_BLOCK, width)] * 3 + [dwout.shape] + [(width, out // 3)] * 3
+    sum_shapes = [dwout.shape] + [(width, HIDDEN_BLOCK)] * 2 + [(HIDDEN_BLOCK, width)] * 2 + [(width, out // 3)] * 3
     scratch = [
         pltpu.VMEM((2, out, rows), BF16),
         pltpu.VMEM((rows, width), BF16),
@@ -1263,12 +1334,11 @@
         pltpu.VMEM((width, out), BF16),
         pltpu.VMEM((width // 2, out), BF16),
         pltpu.VMEM((rows // 2, width), BF16),
-        pltpu.VMEM((SmallSum.ROWS, width), F32),
-        pltpu.VMEM((SmallSum.ROWS, width), F32),
+        pltpu.VMEM((2, SmallSum.ROWS, width), F32),
         pltpu.SemaphoreType.DMA((3,)),
         pltpu.SemaphoreType.DMA((2, 2)),
-        pltpu.SemaphoreType.DMA((3,)),
-        pltpu.SemaphoreType.DMA((3,)),
+        pltpu.SemaphoreType.DMA((6,)),
+        pltpu.SemaphoreType.DMA((6,)),
     ]
     for shape in sum_shapes:
         scratch += PlaneSum.buffers(*shape)
@@ -1280,7 +1350,7 @@
         functools.partial(tail_kernel, heads=heads, block=block),
         grid=(first_rows + 4,),
         in_specs=[
-            whole((1, rows)), all_three, one, row, one, whole((1, width)), whole((8, width)),
+            whole((1, rows)), all_three, one, row, one, whole((8, width)), whole((8, width)),
             whole((1, 2 * width)), whole((1, 2 * width)), whole(dwout.shape),
         ]
         + [anywhere] * 10,
@@ -1295,8 +1365,8 @@
             jax.ShapeDtypeStruct((rows // 2, width), F32),
             jax.ShapeDtypeStruct((SmallSum.ROWS, width), F32),
             jax.ShapeDtypeStruct((rows // 2, width), BF16),
-            jax.ShapeDtypeStruct(dup.shape, BF16),
-            jax.ShapeDtypeStruct(ddown.shape, BF16),
+            jax.ShapeDtypeStruct((width, dup.shape[1] - HIDDEN_BLOCK), BF16),
+            jax.ShapeDtypeStruct((ddown.shape[0] - HIDDEN_BLOCK, width), BF16),
             jax.ShapeDtypeStruct(dwout.shape, BF16),
             jax.ShapeDtypeStruct((width, out), BF16),
             jax.ShapeDtypeStruct((rows // 2, width), BF16),
@@ -1308,7 +1378,7 @@
         cost_estimate=cost(pairs * 5 * 512, 32 * heads * HEAD_DIM * rows, pairs),
         name="tail",
     )(
-        mask, qkv, att, log_total, gatt, gain, small2, dbup1, dbup2, dwout2, normed, w_cat,
+        mask, qkv, att, log_total, gatt, vectors, small2, dbup1, dbup2, dwout2, normed, w_cat,
         tokens, gresid, dup, ddown, dwout, seen_up, seen_down, out_rows,
     )
 
@@ -1343,25 +1413,34 @@
         ]
     )
     mask = jnp.where(valid, 0.0, -1e30).astype(F32).reshape(1, -1)
-    row = lambda vector: vector.astype(F32).reshape(1, -1)
+    vectors = jnp.stack(
+        [ln1_gain, ln1_bias, b_out, ln2_gain, ln2_bias, b_down, b_down, b_down]
+    ).astype(F32)
     biases = jnp.concatenate([b_query, jnp.zeros_like(b_query), b_value, b_up]).astype(F32)
     bias = jnp.broadcast_to(biases.reshape(1, -1), (8, biases.shape[0]))
 
     (normed, qkv, att, log_total, resid, mid, w_cat, w_out_all, w_up2, w_down2, grads, bias2,
      own_tokens) = front(
-        mask, row(ln1_gain), row(ln1_bias), row(b_out), row(ln2_gain), row(ln2_bias), bias,
-        tokens, w_query, w_key, w_value, w_out, w_up, w_down, cotangent, heads,
+        mask, vectors, bias, tokens, w_query, w_key, w_value, w_out, w_up, w_down, cotangent, heads,
     )
     qkv = qkv.reshape(2, 3, heads, HEAD_DIM, rows)
     attended = att.reshape(2 * half, rows)
-    up_bias = jnp.concatenate([bias2[:1, 3 * half :], bias[:1, 3 * half :]], 1)
-    (out, gresid, gatt, dwout1, dwout2, small2, db_up, dup1, ddown1, seen_up, seen_down) = mid_part(
-        mid, grads, up_bias.reshape(-1, 1, HIDDEN_BLOCK), resid, row(ln2_gain), row(b_down),
-        w_out_all, attended, w_up2, w_up, w_down2, w_down,
-    )
-    dbup2, dbup1 = db_up.reshape(2, 1, -1)
+    up_bias = [
+        rows_of.reshape(-1, 1, HIDDEN_BLOCK)
+        for rows_of in (bias[0, 3 * half :], bias2[0, 3 * half :])
+    ]
+    up_bias = jnp.stack([up_bias[side][i] for side, i in HIDDEN_ORDER])
+    (out, gresid, gatt, dwout1, dwout2, small2, db_up, dup1, ddown1, seen_up, seen_down,
+     first_up, first_down) = mid_part(
+        mid, grads, up_bias, resid, vectors, w_out_all,
+        attended, w_up2, w_up, w_down2, w_down,
+    )
+    dbup1, dbup2 = (
+        jnp.concatenate([db_up[at] for at, (own, _) in enumerate(HIDDEN_ORDER) if own == side], 1)
+        for side in (0, 1)
+    )
     gtok, small, got_tok, grad_up, grad_down, grad_out_t, grad_cat, got_out = tail(
-        mask, qkv, att, log_total, gatt.reshape(2, heads, HEAD_DIM, rows), row(ln1_gain), small2,
+        mask, qkv, att, log_total, gatt.reshape(2, heads, HEAD_DIM, rows), vectors, small2,
         dbup1, dbup2, dwout2, normed, w_cat, own_tokens, gresid, dup1, ddown1, dwout1,
         seen_up, seen_down, out,
     )
@@ -1382,9 +1461,9 @@
         small[4],
         small[2],
         small[3],
-        grad_up.astype(F32),
+        jnp.concatenate([first_up, grad_up], 1).astype(F32),
         small[6:8].reshape(-1),
-        grad_down.astype(F32),
+        jnp.concatenate([first_down, grad_down], 0).astype(F32),
         small[5],
     )
 

time: 367 us -> 351 us (0.956)
  the two profiles are of different devices: /device:TPU:0 before, /device:TPU:9 now
where the time goes in v5:
time: 351 us; the launch traced here: 345 us
  Pallas kernels  309 us (88%)
  other arithmetic  17.7 us (5%)
  local copies, waits for them, and re-layouts  17.3 us (5%)
    pallas_call x1, Pallas kernels, tail(): pl.pallas_call(functools.partial(tail_kernel, heads=heads, block=block),...  136 us
    pallas_call x1, Pallas kernels, mid_part(): pl.pallas_call(functools.partial(mid_kernel, blocks=blocks), grid=(first...  100 us
    pallas_call x1, Pallas kernels, front(): pl.pallas_call(functools.partial(front_kernel, heads=heads, block=block),...  72 us
    select_n x2, other arithmetic, joined(): jnp.where(second, jnp.concatenate([theirs, mine], 0), jnp.concatenate([mi...  7.19 us

profile of v5, /device:TPU:9, one launch (start us, length us, event | category | flops | bytes accessed | tf_op | source)
XLA Modules:
  0.0 344.9 jit_solution(404960981251895378)
XLA Ops:
  0.7 0.7 dynamic_slice.10
  1.5 1.2 dynamic_slice.9
  2.7 0.6 iota_compare_fusion.1
  4.0 0.7 stack.26
  4.7 0.7 stack.27
  5.4 0.7 stack.28
  6.1 0.7 stack.29
  6.7 0.7 stack.30
  7.4 0.7 stack.31
  8.8 0.7 fusion.5
  10.2 72.0 %front.1 = (bf16[2048,768]{1,0:T(8,128)(2,1)}, bf16[2,1152,2048]{2,1,0:T(8,128)(2,1)}, bf16[2,8,48,2048]{3,2,1,0:T(8,128)(2,1)}, f32[2,8,1,2048]{3,2,1,0:T(1,128...) custom-call(f32[1,2048]{1,0:T(1,128)} %add_select_fusion.mask_ref, ...), custom_call_target="tpu_custom_call" | custom-call | flops 29930553344 | bytes 62914560 | tf_op jit(solution)/shard_map/front/pallas_call | solution.py:684
  82.2 0.7 constant_dynamic-update-slice_fusion.5
  83.0 0.7 constant_dynamic-update-slice_fusion.3
  83.7 0.7 constant_dynamic-update-slice_fusion.2
  85.1 100.4 %mid.1 = (bf16[2048,768]{1,0:T(8,128)(2,1)}, f32[2048,768]{1,0:T(8,128)}, bf16[768,2048]{1,0:T(8,128)(2,1)}, bf16[768,384]{1,0:T(8,128)(2,1)}, bf16[768,384]{1,0...) custom-call(bf16[2048,768]{1,0:T(8,128)(2,1)} %get-tuple-element.54., ...), custom_call_target="tpu_custom_call" | custom-call | flops 62813896704 | bytes 94371840 | tf_op jit(solution)/shard_map/mid/pallas_call | solution.py:977
  185.5 0.7 slice_bitcast_fusion.5
  186.8 136.4 %tail.1 = (f32[1024,768]{1,0:T(8,128)}, f32[16,768]{1,0:T(8,128)}, bf16[1024,768]{1,0:T(8,128)(2,1)}, bf16[768,1024]{1,0:T(8,128)(2,1)}, bf16[1024,768]{1,0:T(8,...) custom-call(f32[1,2048]{1,0:T(1,128)} %add_select_fusion.mask_ref, ...), custom_call_target="tpu_custom_call" | custom-call | flops 53687091200 | bytes 25165824 | tf_op jit(solution)/shard_map/tail/pallas_call | solution.py:1349
  323.2 4.1 %maximum_convert_fusion.1 = f32[1536,768]{1,0:T(8,128)} fusion(bf16[1024,768]{1,0:T(8,128)(2,1)} %get-tuple-element.84, bf16[512,768]{1,0:T(8,128)(2,1)S(1)} %copy-done.5), kind=kLoop, calls=%fused_computation.3 | loop fusion | flops 4718592 | bytes 7077888 | tf_op jit(solution)/shard_map/convert_element_type | solution.py:1466
  327.3 2.8 maximum_convert_fusion
  330.4 5.1 %maximum_select_fusion = f32[2048,768]{1,0:T(8,128)} fusion(f32[1024,768]{1,0:T(8,128)} %get-tuple-element.77, f32[1024,768]{1,0:T(8,128)S(1)} %convert_element_type.37, pred[]{:T(512)S(6)} %eq.3), kind=kLoop, calls=%fused_computation | loop fusion | flops 4718592 | bytes 12582913 | tf_op jit(solution)/shard_map/jit(_where)/select_n | solution.py:1387
  335.5 1.9 fusion.4
  337.3 1.6 constant_dynamic-slice_fusion
  339.2 2.1 maximum_select_fusion.1
  341.4 1.4 copy.36
  (46 shorter events, 5.7 us)
Async XLA Ops:
  10.1 72.8 %copy-start.7 = (bf16[1536]{0:T(1024)(128)(2,1)S(1)}, bf16[1536]{0:T(1024)(128)(2,1)}, u32[]{:S(2)}) copy-start(bf16[1536]{0:T(1024)(128)(2,1)} %param.34) | copy-start | bytes 9220
  10.2 72.8 %copy-start.9 = (bf16[384]{0:T(512)(128)(2,1)S(1)}, bf16[384]{0:T(512)(128)(2,1)}, u32[]{:S(2)}) copy-start(bf16[384]{0:T(512)(128)(2,1)} %param.25) | copy-start | bytes 2308
  10.2 72.8 %copy-start.10 = (bf16[384]{0:T(512)(128)(2,1)S(1)}, bf16[384]{0:T(512)(128)(2,1)}, u32[]{:S(2)}) copy-start(bf16[384]{0:T(512)(128)(2,1)} %param.28) | copy-start | bytes 2308
  84.5 0.6 copy-start.11
  186.8 136.4 %copy-start.5 = (bf16[512,768]{1,0:T(8,128)(2,1)S(1)}, bf16[512,768]{1,0:T(8,128)(2,1)}, u32[]{:S(2)}) copy-start(bf16[512,768]{1,0:T(8,128)(2,1)} %get-tuple-element.83) | copy-start | bytes 2359300
  323.2 4.1 %copy-start.1 = (bf16[768,1024]{1,0:T(8,128)(2,1)S(1)}, bf16[768,1024]{1,0:T(8,128)(2,1)}, u32[]{:S(2)}) copy-start(bf16[768,1024]{1,0:T(8,128)(2,1)} %get-tuple-element.82) | copy-start | bytes 4718596
  323.2 4.1 %copy-start.4 = (bf16[768,512]{1,0:T(8,128)(2,1)S(1)}, bf16[768,512]{1,0:T(8,128)(2,1)}, u32[]{:S(2)}) copy-start(bf16[768,512]{1,0:T(8,128)(2,1)} %get-tuple-element.81) | copy-start | bytes 2359300
  327.3 2.8 copy-start.3
  330.4 5.1 %copy-start = (bf16[768,1152]{1,0:T(8,128)(2,1)S(1)}, bf16[768,1152]{1,0:T(8,128)(2,1)}, u32[]{:S(2)}) copy-start(bf16[768,1152]{1,0:T(8,128)(2,1)} %get-tuple-element.79) | copy-start | bytes 5308420
  337.3 1.9 copy-start.2
  339.2 2.1 copy-start.6
  341.3 1.5 copy-start.8

commit v6 on v5

--- a/solution.py
+++ b/solution.py
@@ -461,10 +461,10 @@
     sems = [scratch[2 * i : 2 * i + 2] for i in range(6)]
     mine = [wq_hbm, wk_hbm, wv_hbm]
     projections = [
-        Fetch(place, own, cat_ref.at[1, :, pl.ds(i * half, half)], sems[i], False)
+        Fetch(place, own, cat_ref.at[1, :, pl.ds(i * half, half)], sems[i], True)
         for i, own in enumerate(mine)
     ]
-    fetch_out = Fetch(place, wout_hbm, wout_ref.at[pl.ds(half, half)], sems[3], False)
+    fetch_out = Fetch(place, wout_hbm, wout_ref.at[pl.ds(half, half)], sems[3], True)
     fetch_up = Fetch(place, wup_hbm, up2_ref, sems[4], True)
     fetch_down = Fetch(place, wdown_hbm, down2_ref, sems[5], True)
     bias_copy = send_to(
@@ -521,20 +521,29 @@
     def at_step(when):
         return pl.when(step == when)
 
-    @at_step(base[1] - 1)
+    @at_step(base[1] - 2)
     def _():
         fetch_up.begin()
         fetch_down.begin()
 
-    @at_step(base[1] + 1)
+    @at_step(base[1])
     def _():
         for one in (*projections, fetch_out):
             one.share()
 
+    @at_step(base[1] + 1)
+    def _():
+        for one in (*projections, fetch_out):
+            one.more_x()
+
     @at_step(base[2] - 1)
     def _():
         for one in (*projections, fetch_out):
             one.to_core()
+        kept_copy.start()
+        fetch_up.share()
+        fetch_down.share()
+        cot_copy.start()
 
     @at_step(base[2])
     def _():
@@ -544,20 +553,25 @@
         out_load.wait()
         for copy in stores:
             copy.start()
-        kept_copy.start()
-        fetch_up.share()
-        fetch_down.share()
-        cot_copy.start()
-
-    @at_step(base[3] + 2)
+
+    @at_step(base[3] + 1)
     def _():
         fetch_up.more_x()
         fetch_down.more_x()
 
-    @at_step(base[4] + 2)
+    @at_step(base[4] + 1)
     def _():
         fetch_up.to_core()
         fetch_down.to_core()
+
+    @at_step(base[4] + blocks - 1)
+    def _():
+        for one in (fetch_up, fetch_down):
+            one.end()
+        kept_copy.wait()
+        cot_copy.wait()
+        for copy in last_stores:
+            copy.start()
 
     def project(which, i, bias):
         at = pl.ds(pl.multiple_of(i * FRONT_BLOCK, FRONT_BLOCK), FRONT_BLOCK)
@@ -600,13 +614,6 @@
 
     @pl.when(step == base[4] + blocks - 1)
     def _():
-        for one in (fetch_up, fetch_down):
-            one.end()
-        for copy in last_stores[1:]:
-            copy.start()
-        cot_copy.wait()
-        kept_copy.wait()
-        last_stores[0].start()
         for copy in (*stores, *last_stores):
             copy.wait()
 
@@ -1021,14 +1028,13 @@
     (0, 4, 6, 10, 13, 15),
     (0, 5, 8, 12, 14, 16),
     (0, 8, 10, 13, 15, 17),
+    (None, 17, 18, 20),
     (None, 17, 19),
     (None, 17, 20),
-    (None, 17),
 )
 LAST_ACTIONS = (
-    (7, "along_z"), 0, (5, "back_along_z"), 1, (6, "back_along_z"), 2,
-    (7, "back_along_z"), (5, "back_along_x"), (6, "back_along_x"), (7, "back_along_x"),
-    (5, "back_to_core"), (6, "back_to_core"), (7, "back_to_core"),
+    0, (6, "back_along_z"), (5, "back_along_x"), 1, (7, "back_along_z"), (6, "back_along_x"),
+    (5, "back_to_core"), 2, (7, "back_along_x"), (6, "back_to_core"), (7, "back_to_core"),
 )
 
 

time: 351 us -> 342 us (0.974)
  the two profiles are of different devices: /device:TPU:9 before, /device:TPU:0 now
where the time goes in v6:
time: 342 us; the launch traced here: 336 us
  Pallas kernels  300 us (88%)
  other arithmetic  17.7 us (5%)
  local copies, waits for them, and re-layouts  17.3 us (5%)
    pallas_call x1, Pallas kernels, tail(): pl.pallas_call(functools.partial(tail_kernel, heads=heads, block=block),...  131 us
    pallas_call x1, Pallas kernels, mid_part(): pl.pallas_call(functools.partial(mid_kernel, blocks=blocks), grid=(first...  98.6 us
    pallas_call x1, Pallas kernels, front(): pl.pallas_call(functools.partial(front_kernel, heads=heads, block=block),...  69.7 us
    select_n x2, other arithmetic, joined(): jnp.where(second, jnp.concatenate([theirs, mine], 0), jnp.concatenate([mi...  7.19 us

profile of v6, /device:TPU:0, one launch (start us, length us, event | category | flops | bytes accessed | tf_op | source)
XLA Modules:
  0.0 335.8 jit_solution(16852994220480750179)
XLA Ops:
  0.7 0.7 dynamic_slice.10
  1.5 1.2 dynamic_slice.9
  2.7 0.6 iota_compare_fusion.1
  4.0 0.7 stack.26
  4.7 0.7 stack.27
  5.4 0.7 stack.28
  6.1 0.7 stack.29
  6.7 0.7 stack.30
  7.4 0.7 stack.31
  8.8 0.7 fusion.5
  10.2 69.7 %front.1 = (bf16[2048,768]{1,0:T(8,128)(2,1)}, bf16[2,1152,2048]{2,1,0:T(8,128)(2,1)}, bf16[2,8,48,2048]{3,2,1,0:T(8,128)(2,1)}, f32[2,8,1,2048]{3,2,1,0:T(1,128...) custom-call(f32[1,2048]{1,0:T(1,128)} %add_select_fusion.mask_ref, ...), custom_call_target="tpu_custom_call" | custom-call | flops 29930553344 | bytes 62914560 | tf_op jit(solution)/shard_map/front/pallas_call | solution.py:691
  79.9 0.7 constant_dynamic-update-slice_fusion.5
  80.7 0.7 constant_dynamic-update-slice_fusion.3
  81.4 0.7 constant_dynamic-update-slice_fusion.2
  82.8 98.6 %mid.1 = (bf16[2048,768]{1,0:T(8,128)(2,1)}, f32[2048,768]{1,0:T(8,128)}, bf16[768,2048]{1,0:T(8,128)(2,1)}, bf16[768,384]{1,0:T(8,128)(2,1)}, bf16[768,384]{1,0...) custom-call(bf16[2048,768]{1,0:T(8,128)(2,1)} %get-tuple-element.54., ...), custom_call_target="tpu_custom_call" | custom-call | flops 62813896704 | bytes 94371840 | tf_op jit(solution)/shard_map/mid/pallas_call | solution.py:984
  181.4 0.7 slice_bitcast_fusion.5
  182.7 131.4 %tail.1 = (f32[1024,768]{1,0:T(8,128)}, f32[16,768]{1,0:T(8,128)}, bf16[1024,768]{1,0:T(8,128)(2,1)}, bf16[768,1024]{1,0:T(8,128)(2,1)}, bf16[1024,768]{1,0:T(8,...) custom-call(f32[1,2048]{1,0:T(1,128)} %add_select_fusion.mask_ref, ...), custom_call_target="tpu_custom_call" | custom-call | flops 53687091200 | bytes 25165824 | tf_op jit(solution)/shard_map/tail/pallas_call | solution.py:1355
  314.1 4.1 %maximum_convert_fusion.1 = f32[1536,768]{1,0:T(8,128)} fusion(bf16[1024,768]{1,0:T(8,128)(2,1)} %get-tuple-element.84, bf16[512,768]{1,0:T(8,128)(2,1)S(1)} %copy-done.5), kind=kLoop, calls=%fused_computation.3 | loop fusion | flops 4718592 | bytes 7077888 | tf_op jit(solution)/shard_map/convert_element_type | solution.py:1472
  318.2 2.8 maximum_convert_fusion
  321.3 5.1 %maximum_select_fusion = f32[2048,768]{1,0:T(8,128)} fusion(f32[1024,768]{1,0:T(8,128)} %get-tuple-element.77, f32[1024,768]{1,0:T(8,128)S(1)} %convert_element_type.37, pred[]{:T(512)S(6)} %eq.3), kind=kLoop, calls=%fused_computation | loop fusion | flops 4718592 | bytes 12582913 | tf_op jit(solution)/shard_map/jit(_where)/select_n | solution.py:1393
  326.4 1.9 fusion.4
  328.2 1.6 constant_dynamic-slice_fusion
  330.1 2.1 maximum_select_fusion.1
  332.3 1.4 copy.36
  (46 shorter events, 5.7 us)
Async XLA Ops:
  10.1 70.5 %copy-start.7 = (bf16[1536]{0:T(1024)(128)(2,1)S(1)}, bf16[1536]{0:T(1024)(128)(2,1)}, u32[]{:S(2)}) copy-start(bf16[1536]{0:T(1024)(128)(2,1)} %param.34) | copy-start | bytes 9220
  10.2 70.5 %copy-start.9 = (bf16[384]{0:T(512)(128)(2,1)S(1)}, bf16[384]{0:T(512)(128)(2,1)}, u32[]{:S(2)}) copy-start(bf16[384]{0:T(512)(128)(2,1)} %param.25) | copy-start | bytes 2308
  10.2 70.5 %copy-start.10 = (bf16[384]{0:T(512)(128)(2,1)S(1)}, bf16[384]{0:T(512)(128)(2,1)}, u32[]{:S(2)}) copy-start(bf16[384]{0:T(512)(128)(2,1)} %param.28) | copy-start | bytes 2308
  82.2 0.6 copy-start.11
  182.7 131.4 %copy-start.5 = (bf16[512,768]{1,0:T(8,128)(2,1)S(1)}, bf16[512,768]{1,0:T(8,128)(2,1)}, u32[]{:S(2)}) copy-start(bf16[512,768]{1,0:T(8,128)(2,1)} %get-tuple-element.83) | copy-start | bytes 2359300
  314.1 4.1 %copy-start.1 = (bf16[768,1024]{1,0:T(8,128)(2,1)S(1)}, bf16[768,1024]{1,0:T(8,128)(2,1)}, u32[]{:S(2)}) copy-start(bf16[768,1024]{1,0:T(8,128)(2,1)} %get-tuple-element.82) | copy-start | bytes 4718596
  314.1 4.1 %copy-start.4 = (bf16[768,512]{1,0:T(8,128)(2,1)S(1)}, bf16[768,512]{1,0:T(8,128)(2,1)}, u32[]{:S(2)}) copy-start(bf16[768,512]{1,0:T(8,128)(2,1)} %get-tuple-element.81) | copy-start | bytes 2359300
  318.2 2.8 copy-start.3
  321.3 5.1 %copy-start = (bf16[768,1152]{1,0:T(8,128)(2,1)S(1)}, bf16[768,1152]{1,0:T(8,128)(2,1)}, u32[]{:S(2)}) copy-start(bf16[768,1152]{1,0:T(8,128)(2,1)} %get-tuple-element.79) | copy-start | bytes 5308420
  328.2 1.9 copy-start.2
  330.1 2.1 copy-start.6
  332.2 1.5 copy-start.8

commit v7 on v6

--- a/solution.py
+++ b/solution.py
@@ -33,6 +33,10 @@
     return pl.CostEstimate(
         flops=int(flops), bytes_accessed=int(bytes_accessed), transcendentals=int(transcendentals)
     )
+
+
+def row(ref):
+    return ref[...].astype(F32).reshape(1, ref.shape[0])
 
 
 def whole(shape):
@@ -441,7 +445,7 @@
 
 
 def front_kernel(
-    mask_ref, vec_ref, bias_ref, tok_hbm, wq_hbm, wk_hbm, wv_hbm, wout_hbm, wup_hbm, wdown_hbm, cot_hbm,
+    mask_ref, gain_ref, shift_ref, bout_ref, gain2_ref, shift2_ref, bias_ref, tok_hbm, wq_hbm, wk_hbm, wv_hbm, wout_hbm, wup_hbm, wdown_hbm, cot_hbm,
     x_out, qkv_out, att_out, log_out, resid_out, mid_out,
     cat_hbm, wout_all_hbm, up2_hbm, down2_hbm, grads_hbm, bias2_hbm, tok_out,
     tok_ref, x_ref, qkv_ref, att_ref, cat_ref, wout_ref, bias2_ref, up2_ref, down2_ref, grads_ref,
@@ -449,9 +453,6 @@
 ):
     step = pl.program_id(0)
     place = Place()
-    gain_ref, shift_ref, bout_ref, gain2_ref, shift2_ref = (
-        vec_ref.at[pl.ds(i, 1)] for i in range(5)
-    )
     half = heads * HEAD_DIM
     rows = tok_ref.shape[0]
     blocks = rows // FRONT_BLOCK
@@ -584,7 +585,7 @@
     def _():
         at = pl.ds(pl.multiple_of(step * FRONT_BLOCK, FRONT_BLOCK), FRONT_BLOCK)
         hat, _ = norm_parts(tok_ref[at, :].astype(F32))
-        normed = (hat * gain_ref[...] + shift_ref[...]).astype(BF16)
+        normed = (hat * row(gain_ref) + row(shift_ref)).astype(BF16)
         x_ref[at, :] = normed
         x_out[...] = normed
         project(0, step, bias_ref[...])
@@ -607,10 +608,10 @@
         i = step - base[4]
         at = pl.ds(pl.multiple_of(i * FRONT_BLOCK, FRONT_BLOCK), FRONT_BLOCK)
         product = contract(att_ref[:, at], wout_ref[...], 0, 0)
-        resid = tok_ref[at, :].astype(F32) + product + bout_ref[...]
+        resid = tok_ref[at, :].astype(F32) + product + row(bout_ref)
         resid_out[...] = resid
         hat, _ = norm_parts(resid)
-        mid_out[...] = (hat * gain2_ref[...] + shift2_ref[...]).astype(BF16)
+        mid_out[...] = (hat * row(gain2_ref) + row(shift2_ref)).astype(BF16)
 
     @pl.when(step == base[4] + blocks - 1)
     def _():
@@ -693,7 +694,7 @@
         grid=(base[4] + blocks,),
         in_specs=[
             whole((1, rows)),
-            whole((8, width)),
+            *(whole((width,)) for _ in range(5)),
             whole(bias.shape),
         ]
         + [anywhere] * 8,
@@ -746,7 +747,7 @@
         ),
         name="front",
     )(
-        mask, vectors, bias, tokens, w_query, w_key, w_value, w_out, w_up, w_down, cotangent,
+        mask, *vectors, bias, tokens, w_query, w_key, w_value, w_out, w_up, w_down, cotangent,
     )
 
 
@@ -774,7 +775,7 @@
 
 
 def mid_kernel(
-    mid_ref, grad_ref, bias_ref, resid_ref, vec_ref, w_ref, att_ref,
+    mid_ref, grad_ref, bias_ref, resid_ref, gain_ref, bdown_ref, w_ref, att_ref,
     up2_hbm, up_hbm, down2_hbm, down_hbm,
     out_ref, gresid_ref, gatt_ref, dw_own_ref, dw_other_ref, small_ref, db_ref,
     dup_hbm, ddown_hbm, seen_up, seen_down, gup_hbm, gdown_hbm,
@@ -920,10 +921,10 @@
         here = pl.ds(pl.multiple_of(start, MID_BLOCK), MID_BLOCK)
         resid = resid_ref[...]
         grads = grad_ref[here, :].astype(F32)
-        out_ref[...] = (resid + sum_ref[here, :] + vec_ref[5:6]).astype(BF16)
+        out_ref[...] = (resid + sum_ref[here, :] + row(bdown_ref)).astype(BF16)
         gmid = gmid_ref[here, :]
         hat, inv = norm_parts(resid)
-        gresid = grads + norm_back(hat, inv, gmid * vec_ref[3:4])
+        gresid = grads + norm_back(hat, inv, gmid * row(gain_ref))
         gresid_ref[...] = gresid
         branch = gresid.astype(BF16)
         gatt_ref[...] = contract(w_ref[...], branch, 1, 1).astype(BF16)
@@ -949,7 +950,7 @@
             one.end()
 
 
-def mid_part(mid, grads, biases, resid, vectors, w_out, attended, up2, up, down2, down):
+def mid_part(mid, grads, biases, resid, gain, b_down, w_out, attended, up2, up, down2, down):
     rows, width = mid.shape
     hidden = up.shape[1]
     blocks = hidden // HIDDEN_BLOCK
@@ -985,8 +986,8 @@
         functools.partial(mid_kernel, blocks=blocks),
         grid=(first + rows // MID_BLOCK,),
         in_specs=[
-            once((rows, width)), once((rows, width)), by_hidden, by_row, whole((8, width)),
-            once((heads_width, width)), columns,
+            once((rows, width)), once((rows, width)), by_hidden, by_row, whole((width,)),
+            whole((width,)), once((heads_width, width)), columns,
         ]
         + [anywhere] * 4,
         out_specs=[
@@ -1017,7 +1018,7 @@
             4 * rows * hidden,
         ),
         name="mid",
-    )(mid, grads, biases, resid, vectors, w_out, attended, up2, up, down2, down)
+    )(mid, grads, biases, resid, gain, b_down, w_out, attended, up2, up, down2, down)
 
 
 TAIL_BLOCK = 512
@@ -1039,7 +1040,7 @@
 
 
 def tail_kernel(
-    mask_ref, qkv_ref, att_ref, log_ref, gatt_ref, vec_ref, small2_ref, dbup1_ref, dbup2_ref,
+    mask_ref, qkv_ref, att_ref, log_ref, gatt_ref, gain_ref, small2_ref, dbup1_ref, dbup2_ref,
     wout2_ref, x_hbm, w_hbm, tok_hbm, gresid_hbm, up_hbm, down_hbm, wout_hbm, seen_up,
     seen_down, out_hbm,
     gtok_ref, small_ref, got_hbm, gup_hbm, gdown_hbm, gout_hbm, gcat_hbm, got_out,
@@ -1213,7 +1214,7 @@
             gin = contract(d_ref[0, :, here], w_ref[0], 0, 1)
             gin += contract(d_ref[1, :, here], w_ref[1], 0, 1)
             hat, inv = norm_parts(tok_ref[i % 2].astype(F32))
-            gtok = gresid_ref[i % 2] + norm_back(hat, inv, gin * vec_ref[0:1])
+            gtok = gresid_ref[i % 2] + norm_back(hat, inv, gin * row(gain_ref))
             own_small[0:1] += jnp.sum(gin * hat, axis=0, keepdims=True)
             own_small[1:2] += jnp.sum(gin, axis=0, keepdims=True)
             if i < 2:
@@ -1312,7 +1313,7 @@
 
 
 def tail(
-    mask, qkv, att, log_total, gatt, vectors, small2, dbup1, dbup2, dwout2, normed, w_cat,
+    mask, qkv, att, log_total, gatt, gain, small2, dbup1, dbup2, dwout2, normed, w_cat,
     tokens, gresid, dup, ddown, dwout, seen_up, seen_down, out_rows, block=256,
 ):
     _, _, heads, _, rows = qkv.shape
@@ -1328,7 +1329,7 @@
         (1, 3, 1, HEAD_DIM, rows), lambda h: (head(h)[0], 0, head(h)[1], 0, 0)
     )
     one = pl.BlockSpec((1, 1, HEAD_DIM, rows), lambda h: (*head(h), 0, 0))
-    row = pl.BlockSpec((1, 1, 1, rows), lambda h: (*head(h), 0, 0))
+    per_head = pl.BlockSpec((1, 1, 1, rows), lambda h: (*head(h), 0, 0))
     sum_shapes = [dwout.shape] + [(width, HIDDEN_BLOCK)] * 2 + [(HIDDEN_BLOCK, width)] * 2 + [(width, out // 3)] * 3
     scratch = [
         pltpu.VMEM((2, out, rows), BF16),
@@ -1356,7 +1357,7 @@
         functools.partial(tail_kernel, heads=heads, block=block),
         grid=(first_rows + 4,),
         in_specs=[
-            whole((1, rows)), all_three, one, row, one, whole((8, width)), whole((8, width)),
+            whole((1, rows)), all_three, one, per_head, one, whole((width,)), whole((8, width)),
             whole((1, 2 * width)), whole((1, 2 * width)), whole(dwout.shape),
         ]
         + [anywhere] * 10,
@@ -1384,7 +1385,7 @@
         cost_estimate=cost(pairs * 5 * 512, 32 * heads * HEAD_DIM * rows, pairs),
         name="tail",
     )(
-        mask, qkv, att, log_total, gatt, vectors, small2, dbup1, dbup2, dwout2, normed, w_cat,
+        mask, qkv, att, log_total, gatt, gain, small2, dbup1, dbup2, dwout2, normed, w_cat,
         tokens, gresid, dup, ddown, dwout, seen_up, seen_down, out_rows,
     )
 
@@ -1419,15 +1420,13 @@
         ]
     )
     mask = jnp.where(valid, 0.0, -1e30).astype(F32).reshape(1, -1)
-    vectors = jnp.stack(
-        [ln1_gain, ln1_bias, b_out, ln2_gain, ln2_bias, b_down, b_down, b_down]
-    ).astype(F32)
     biases = jnp.concatenate([b_query, jnp.zeros_like(b_query), b_value, b_up]).astype(F32)
     bias = jnp.broadcast_to(biases.reshape(1, -1), (8, biases.shape[0]))
 
     (normed, qkv, att, log_total, resid, mid, w_cat, w_out_all, w_up2, w_down2, grads, bias2,
      own_tokens) = front(
-        mask, vectors, bias, tokens, w_query, w_key, w_value, w_out, w_up, w_down, cotangent, heads,
+        mask, (ln1_gain, ln1_bias, b_out, ln2_gain, ln2_bias), bias,
+        tokens, w_query, w_key, w_value, w_out, w_up, w_down, cotangent, heads,
     )
     qkv = qkv.reshape(2, 3, heads, HEAD_DIM, rows)
     attended = att.reshape(2 * half, rows)
@@ -1438,7 +1437,7 @@
     up_bias = jnp.stack([up_bias[side][i] for side, i in HIDDEN_ORDER])
     (out, gresid, gatt, dwout1, dwout2, small2, db_up, dup1, ddown1, seen_up, seen_down,
      first_up, first_down) = mid_part(
-        mid, grads, up_bias, resid, vectors, w_out_all,
+        mid, grads, up_bias, resid, ln2_gain, b_down, w_out_all,
         attended, w_up2, w_up, w_down2, w_down,
     )
     dbup1, dbup2 = (
@@ -1446,7 +1445,7 @@
         for side in (0, 1)
     )
     gtok, small, got_tok, grad_up, grad_down, grad_out_t, grad_cat, got_out = tail(
-        mask, qkv, att, log_total, gatt.reshape(2, heads, HEAD_DIM, rows), vectors, small2,
+        mask, qkv, att, log_total, gatt.reshape(2, heads, HEAD_DIM, rows), ln1_gain, small2,
         dbup1, dbup2, dwout2, normed, w_cat, own_tokens, gresid, dup1, ddown1, dwout1,
         seen_up, seen_down, out,
     )

time: 342 us -> 338 us (0.988)
  local copies, waits for them, and re-layouts: 17.3 us -> 13.2 us
    another operation x7 -> x0, local copies, waits for them, and re-layouts: 4.16 us -> none  [by_images(): jnp.stack([ln1_gain, ln1_bias, b_out, ln2_gain, ln2_bias, b_down, b_down,...]
where the time goes in v7:
time: 338 us; the launch traced here: 331 us
  Pallas kernels  300 us (89%)
  other arithmetic  17.1 us (5%)
  local copies, waits for them, and re-layouts  13.2 us (4%)
    pallas_call x1, Pallas kernels, tail(): pl.pallas_call(functools.partial(tail_kernel, heads=heads, block=block),...  132 us
    pallas_call x1, Pallas kernels, mid_part(): pl.pallas_call(functools.partial(mid_kernel, blocks=blocks), grid=(first...  98.3 us
    pallas_call x1, Pallas kernels, front(): pl.pallas_call(functools.partial(front_kernel, heads=heads, block=block),...  69.9 us
    select_n x2, other arithmetic, joined(): jnp.where(second, jnp.concatenate([theirs, mine], 0), jnp.concatenate([mi...  7.19 us

profile of v7, /device:TPU:0, one launch (start us, length us, event | category | flops | bytes accessed | tf_op | source)
XLA Modules:
  0.0 331.1 jit_solution(10940973628688622054)
XLA Ops:
  0.7 0.7 dynamic_slice.10
  1.5 1.2 dynamic_slice.9
  2.7 0.6 iota_compare_fusion.1
  3.4 0.6 add_select_fusion.mask_ref
  4.0 0.7 fusion.5
  4.7 0.6 broadcast_in_dim.23.bias_ref
  5.4 69.9 %front.1 = (bf16[2048,768]{1,0:T(8,128)(2,1)}, bf16[2,1152,2048]{2,1,0:T(8,128)(2,1)}, bf16[2,8,48,2048]{3,2,1,0:T(8,128)(2,1)}, f32[2,8,1,2048]{3,2,1,0:T(1,128...) custom-call(f32[1,2048]{1,0:T(1,128)} %add_select_fusion.mask_ref, ...), custom_call_target="tpu_custom_call" | custom-call | flops 29930553344 | bytes 62914560 | tf_op jit(solution)/shard_map/front/pallas_call | solution.py:692
  75.3 0.7 constant_dynamic-update-slice_fusion.5
  76.1 0.7 constant_dynamic-update-slice_fusion.3
  76.8 0.7 constant_dynamic-update-slice_fusion.2
  78.1 98.3 %mid.1 = (bf16[2048,768]{1,0:T(8,128)(2,1)}, f32[2048,768]{1,0:T(8,128)}, bf16[768,2048]{1,0:T(8,128)(2,1)}, bf16[768,384]{1,0:T(8,128)(2,1)}, bf16[768,384]{1,0...) custom-call(bf16[2048,768]{1,0:T(8,128)(2,1)} %get-tuple-element.54., ...), custom_call_target="tpu_custom_call" | custom-call | flops 62813896704 | bytes 94371840 | tf_op jit(solution)/shard_map/mid/pallas_call | solution.py:985
  176.5 0.7 slice_bitcast_fusion.5
  177.2 0.6 pad_maximum_fusion
  177.8 131.6 %tail.1 = (f32[1024,768]{1,0:T(8,128)}, f32[16,768]{1,0:T(8,128)}, bf16[1024,768]{1,0:T(8,128)(2,1)}, bf16[768,1024]{1,0:T(8,128)(2,1)}, bf16[1024,768]{1,0:T(8,...) custom-call(f32[1,2048]{1,0:T(1,128)} %add_select_fusion.mask_ref, ...), custom_call_target="tpu_custom_call" | custom-call | flops 53687091200 | bytes 25165824 | tf_op jit(solution)/shard_map/tail/pallas_call | solution.py:1356
  309.4 4.1 %maximum_convert_fusion.1 = f32[1536,768]{1,0:T(8,128)} fusion(bf16[1024,768]{1,0:T(8,128)(2,1)} %get-tuple-element.84, bf16[512,768]{1,0:T(8,128)(2,1)S(1)} %copy-done.5), kind=kLoop, calls=%fused_computation.3 | loop fusion | flops 4718592 | bytes 7077888 | tf_op jit(solution)/shard_map/convert_element_type | solution.py:1471
  313.6 2.8 maximum_convert_fusion
  316.6 5.1 %maximum_select_fusion = f32[2048,768]{1,0:T(8,128)} fusion(f32[1024,768]{1,0:T(8,128)} %get-tuple-element.77, f32[1024,768]{1,0:T(8,128)S(1)} %convert_element_type.33, pred[]{:T(512)S(6)} %eq.3), kind=kLoop, calls=%fused_computation | loop fusion | flops 4718592 | bytes 12582913 | tf_op jit(solution)/shard_map/jit(_where)/select_n | solution.py:1394
  321.7 1.9 fusion.4
  323.6 1.6 constant_dynamic-slice_fusion
  325.5 2.1 maximum_select_fusion.1
  327.7 1.4 copy.36
  329.1 0.6 slice_reduce_fusion
  329.7 0.6 reshape.154
  330.3 0.6 slice_reduce_fusion.6
  (38 shorter events, 1.3 us)
Async XLA Ops:
  5.4 70.6 %copy-start.7 = (bf16[1536]{0:T(1024)(128)(2,1)S(1)}, bf16[1536]{0:T(1024)(128)(2,1)}, u32[]{:S(2)}) copy-start(bf16[1536]{0:T(1024)(128)(2,1)} %param.34) | copy-start | bytes 9220
  5.4 70.6 %copy-start.9 = (bf16[384]{0:T(512)(128)(2,1)S(1)}, bf16[384]{0:T(512)(128)(2,1)}, u32[]{:S(2)}) copy-start(bf16[384]{0:T(512)(128)(2,1)} %param.25) | copy-start | bytes 2308
  5.4 70.6 %copy-start.10 = (bf16[384]{0:T(512)(128)(2,1)S(1)}, bf16[384]{0:T(512)(128)(2,1)}, u32[]{:S(2)}) copy-start(bf16[384]{0:T(512)(128)(2,1)} %param.28) | copy-start | bytes 2308
  77.5 0.6 copy-start.11
  177.8 131.6 %copy-start.5 = (bf16[512,768]{1,0:T(8,128)(2,1)S(1)}, bf16[512,768]{1,0:T(8,128)(2,1)}, u32[]{:S(2)}) copy-start(bf16[512,768]{1,0:T(8,128)(2,1)} %get-tuple-element.83) | copy-start | bytes 2359300
  309.4 4.1 %copy-start.1 = (bf16[768,1024]{1,0:T(8,128)(2,1)S(1)}, bf16[768,1024]{1,0:T(8,128)(2,1)}, u32[]{:S(2)}) copy-start(bf16[768,1024]{1,0:T(8,128)(2,1)} %get-tuple-element.82) | copy-start | bytes 4718596
  309.4 4.1 %copy-start.4 = (bf16[768,512]{1,0:T(8,128)(2,1)S(1)}, bf16[768,512]{1,0:T(8,128)(2,1)}, u32[]{:S(2)}) copy-start(bf16[768,512]{1,0:T(8,128)(2,1)} %get-tuple-element.81) | copy-start | bytes 2359300
  313.6 2.8 copy-start.3
  316.6 5.1 %copy-start = (bf16[768,1152]{1,0:T(8,128)(2,1)S(1)}, bf16[768,1152]{1,0:T(8,128)(2,1)}, u32[]{:S(2)}) copy-start(bf16[768,1152]{1,0:T(8,128)(2,1)} %get-tuple-element.79) | copy-start | bytes 5308420
  323.6 1.9 copy-start.2
  325.5 2.1 copy-start.6
  327.6 1.5 copy-start.8
